TPU v7x, 32 devices: a whole 2x2x4 slice. The times are simulated.
32 devices in a mesh: section: 2 (over core), dp: 4 (over y, x), seq: 4 (over z).
Axes of the slice: x: 2, y: 2, z: 4, core: 2. Of those that a mesh axis runs over, the one named last changes fastest.
Arguments:
- inputs: bfloat16 [16, 2048, 768], P('dp', 'seq'), may hold values from -80 to 80
- shifts: int32 [16], P('dp'), may hold values from -3 to 3, as said below
- flips: int32 [16], P('dp'), may hold values from 0 to 1, as said below
- norm1_gain: float32 [768], replicated, may hold values from 0.25 to 1.75
- norm1_bias: float32 [768], replicated, may hold values from -2.5 to 2.5
- conv1_weight: bfloat16 [5, 768, 768], replicated, may hold values from -0.09375 to 0.09375
- norm2_gain: float32 [768], replicated, may hold values from 0.25 to 1.75
- norm2_bias: float32 [768], replicated, may hold values from -2.5 to 2.5
- dilated_conv2_weight: bfloat16 [3, 768, 384], replicated, may hold values from -0.125 to 0.125
- norm3_gain: float32 [384], replicated, may hold values from 0.25 to 1.75
- norm3_bias: float32 [384], replicated, may hold values from -2.5 to 2.5
- conv3_weight: bfloat16 [384, 768], replicated, may hold values from -0.3125 to 0.3125
- out_grad: bfloat16 [16, 1024, 768], P('dp', 'seq'), may hold values from -6 to 6
Outputs:
- result: bfloat16 [16, 1024, 768], P('dp', 'seq', 'section')
- input_grad: bfloat16 [16, 2048, 768], P('dp', 'seq', 'section')
- conv1_grad: float32 [5, 768, 768], replicated
- norm1_gain_grad: float32 [768], replicated
- norm1_bias_grad: float32 [768], replicated
- conv2_grad: float32 [3, 768, 384], replicated
- norm2_gain_grad: float32 [768], replicated
- norm2_bias_grad: float32 [768], replicated
- conv3_grad: float32 [384, 768], replicated
- norm3_gain_grad: float32 [384], replicated
- norm3_bias_grad: float32 [384], replicated
Inputs may be any that keep to these rules, and one draw needn't show every extreme that they name: `shifts`: 3 and -3 both occur. `flips`: both values occur.
All inputs are finite; a program needn't handle non-finite values.
Results may differ from a plain program's by a relative error of at most 0.012.
The roundings to bfloat16 on the way count: a program that leaves them out, or rounds other values in their place, can miss the bound.
Values may be sent and summed in bfloat16 or wider, within the bound.
A program may use at most 192 MiB of HBM per device.

v0:
```python
import jax
import jax.numpy as jnp
from jax import lax
from jax.sharding import PartitionSpec as P

DILATION_SIZE = 11
SHIFT_MAX = 3
MB = 4


EPSILON = 0.001


def for_sending(x):
    return jax.tree.map(lambda a: a.astype(jnp.bfloat16) if a.dtype == jnp.float32 else a, x)


def from_partner(block, axis, bit):
    count = lax.axis_size(axis)
    route = []
    for low in range(count):
        high = low | 1 << bit
        if high != low and high < count:
            route += [(low, high), (high, low)]
    return lax.ppermute(block, axis, route)


def extended(x, sides, width, wrap):
    for axis, dim in sides:
        size, length = (lax.axis_size(axis), x.shape[dim])
        up = [(i, (i + 1) % size) for i in range(size if wrap else size - 1)]
        down = [(j, i) for i, j in up]
        last = lax.slice_in_dim(x, length - width, length, axis=dim)
        first = lax.slice_in_dim(x, 0, width, axis=dim)
        before = lax.ppermute(last, axis, up)
        after = lax.ppermute(first, axis, down)
        x = jnp.concatenate([before, x, after], axis=dim)
    return x


def passed_along(x, axis, by):
    size = lax.axis_size(axis)
    pairs = [(i, i + by) for i in range(size) if 0 <= i + by < size]
    return lax.ppermute(x, axis, pairs)


def gelu_apply(values):
    return jax.nn.gelu(values, approximate=True)


def gelu_back(values, gradient):
    _, pullback = jax.vjp(gelu_apply, values)
    return pullback(gradient)[0]


def mirror(block_data):
    arrived = block_data
    levels = lax.axis_size("seq").bit_length() - 1
    for bit_level in range(levels):
        arrived = jax.tree.map(
            lambda part, own: part.astype(own.dtype),
            from_partner(for_sending(arrived), "seq", bit_level),
            arrived,
        )
    return jnp.flip(arrived, axis=1)


def rotate(block_data, offsets):
    padded = extended(block_data, (("seq", 1),), SHIFT_MAX, True)
    extent = block_data.shape[1]

    def one_row(seq_row, offset):
        return lax.dynamic_slice_in_dim(seq_row, (SHIFT_MAX - offset).astype(jnp.int32), extent, 0)

    return jax.vmap(one_row)(padded, offsets)


def rim_wide(block_data, border_width):
    return extended(block_data, (("seq", 1),), border_width, False)


def dilated_border(block_data, border_width):
    return extended(block_data, (("seq", 1),), border_width, False)


def moments(values):
    tally = values.shape[0] * values.shape[1] * lax.axis_size("dp") * lax.axis_size("seq")
    average = lax.psum(jnp.sum(values, axis=(0, 1)), ("dp", "seq")) / tally
    centred = values - average
    spread = lax.psum(jnp.sum(centred * centred, axis=(0, 1)), ("dp", "seq")) / tally
    return (average, lax.rsqrt(spread + EPSILON))


def norm_back(grad_pre, normed, gain, inv_spread):
    tally = grad_pre.shape[0] * grad_pre.shape[1] * lax.axis_size("dp") * lax.axis_size("seq")
    bias_part = jnp.sum(grad_pre, axis=(0, 1))
    gain_part = jnp.sum(grad_pre * normed, axis=(0, 1))
    bias_total, gain_total = lax.psum((bias_part, gain_part), ("dp", "seq"))
    grad_values = (
        gain * inv_spread * (grad_pre - bias_total / tally - normed * (gain_total / tally))
    )
    return (grad_values, (bias_part, gain_part))


def kernel_taps_forward(padded, weight, stride):
    tap_count = weight.shape[0]
    extent = padded.shape[1] - (tap_count - 1) * stride
    running = jnp.einsum(
        "slc,co->slo", padded[:, 0:extent], weight[0], preferred_element_type=jnp.float32
    )
    for tap_index in range(1, tap_count):
        start_bin = tap_index * stride
        running = running + jnp.einsum(
            "slc,co->slo",
            padded[:, start_bin : start_bin + extent],
            weight[tap_index],
            preferred_element_type=jnp.float32,
        )
    return running


def kernel_taps_input_gradient(grad_padded, weight, stride):
    tap_count = weight.shape[0]
    extent = grad_padded.shape[1] - (tap_count - 1) * stride
    running = None
    for tap_index in range(tap_count):
        start_bin = (tap_count - 1 - tap_index) * stride
        partial_sum = jnp.einsum(
            "slo,co->slc",
            grad_padded[:, start_bin : start_bin + extent],
            weight[tap_index],
            preferred_element_type=jnp.float32,
        )
        running = partial_sum if tap_index == 0 else running + partial_sum
    return running


def kernel_taps_weight_gradient(padded, gradient, stride, tap_count):
    extent = gradient.shape[1]
    return jnp.stack(
        [
            jnp.einsum(
                "slc,slo->co",
                padded[:, tap_index * stride : tap_index * stride + extent],
                gradient,
                preferred_element_type=jnp.float32,
            )
            for tap_index in range(tap_count)
        ]
    )


def first_forward(inputs_block, shift_block, flip_block, norm1_gain, norm1_bias, conv1_weight):
    turned = jnp.where(flip_block[:, None, None] == 1, mirror(inputs_block), inputs_block)
    offsets = jnp.where(flip_block == 1, -shift_block, shift_block)
    shifted = rotate(turned, offsets)
    values = shifted.astype(jnp.float32)
    average, inv_spread = moments(values)
    normed = (values - average) * inv_spread
    first_act = gelu_apply(norm1_gain * normed + norm1_bias).astype(jnp.bfloat16)
    first_pad = rim_wide(first_act, conv1_weight.shape[0] // 2)
    wide_out = kernel_taps_forward(first_pad, conv1_weight, 1)
    pair_view = wide_out.reshape(wide_out.shape[0], wide_out.shape[1] // 2, 2, wide_out.shape[2])
    pooled = jnp.logaddexp(pair_view[:, :, 0], pair_view[:, :, 1]).astype(jnp.bfloat16)
    even_share = jax.nn.sigmoid(pair_view[:, :, 0] - pair_view[:, :, 1])
    return (pooled, (shifted, average, inv_spread, first_pad, even_share, offsets, flip_block))


def first_backward(grad_in, kept_data, norm1_gain, norm1_bias, conv1_weight):
    shifted, average, inv_spread, first_pad, even_share, offsets, flip_block = kept_data
    pooled_grad = grad_in.astype(jnp.float32)
    grad_wide = jnp.stack([pooled_grad * even_share, pooled_grad * (1.0 - even_share)], axis=2)
    grad_wide = grad_wide.reshape(shifted.shape[0], shifted.shape[1], grad_wide.shape[3]).astype(
        jnp.bfloat16
    )
    weight_grad = kernel_taps_weight_gradient(first_pad, grad_wide, 1, conv1_weight.shape[0])
    grad_pad = rim_wide(grad_wide, conv1_weight.shape[0] // 2)
    grad_act = kernel_taps_input_gradient(grad_pad, conv1_weight, 1)
    values = shifted.astype(jnp.float32)
    normed = (values - average) * inv_spread
    grad_pre = gelu_back(norm1_gain * normed + norm1_bias, grad_act)
    grad_values, partials = norm_back(grad_pre, normed, norm1_gain, inv_spread)
    back_moved = rotate(grad_values.astype(jnp.bfloat16), -offsets)
    returned = jnp.where(flip_block[:, None, None] == 1, mirror(back_moved), back_moved)
    return (returned, weight_grad, partials)


def second_pass(
    pooled_in,
    cotangent,
    norm2_gain,
    norm2_bias,
    dilated_conv2_weight,
    norm3_gain,
    norm3_bias,
    conv3_weight,
):
    border_width = (dilated_conv2_weight.shape[0] - 1) // 2 * DILATION_SIZE
    pooled_values = pooled_in.astype(jnp.float32)
    average_two, scale_two = moments(pooled_values)
    normed_two = (pooled_values - average_two) * scale_two
    pre_two = norm2_gain * normed_two + norm2_bias
    second_activation = gelu_apply(pre_two).astype(jnp.bfloat16)
    second_padding = dilated_border(second_activation, border_width)
    narrow_output = kernel_taps_forward(second_padding, dilated_conv2_weight, DILATION_SIZE)
    average_three, scale_three = moments(narrow_output)
    normed_three = (narrow_output - average_three) * scale_three
    pre_three = norm3_gain * normed_three + norm3_bias
    third_act = gelu_apply(pre_three).astype(jnp.bfloat16)
    branch_out = jnp.einsum(
        "slh,hc->slc", third_act, conv3_weight, preferred_element_type=jnp.float32
    )
    result_block = (pooled_values + branch_out).astype(jnp.bfloat16)
    last_grad = jnp.einsum("slh,slc->hc", third_act, cotangent, preferred_element_type=jnp.float32)
    grad_third = jnp.einsum(
        "slc,hc->slh", cotangent, conv3_weight, preferred_element_type=jnp.float32
    )
    gradient_narrow_part, third_parts = norm_back(
        gelu_back(pre_three, grad_third), normed_three, norm3_gain, scale_three
    )
    gradient_narrow_part = gradient_narrow_part.astype(jnp.bfloat16)
    narrow_gradient = kernel_taps_weight_gradient(
        second_padding, gradient_narrow_part, DILATION_SIZE, dilated_conv2_weight.shape[0]
    )
    gradient_second_part = kernel_taps_input_gradient(
        dilated_border(gradient_narrow_part, border_width), dilated_conv2_weight, DILATION_SIZE
    )
    grad_pooled, second_parts = norm_back(
        gelu_back(pre_two, gradient_second_part), normed_two, norm2_gain, scale_two
    )
    grad_pooled = (cotangent.astype(jnp.float32) + grad_pooled).astype(jnp.bfloat16)
    return (result_block, grad_pooled, narrow_gradient, last_grad, second_parts, third_parts)


def on_device(
    inputs,
    shifts,
    flips,
    norm1_gain,
    norm1_bias,
    conv1_weight,
    norm2_gain,
    norm2_bias,
    dilated_conv2_weight,
    norm3_gain,
    norm3_bias,
    conv3_weight,
    out_grad,
):
    seq_rows = inputs.shape[0] // MB
    bin_count = inputs.shape[1]
    pooled_bins = bin_count // 2
    channels = inputs.shape[2]
    hidden = conv3_weight.shape[0]
    taps_first = conv1_weight.shape[0]
    taps_second = dilated_conv2_weight.shape[0]
    section_index = lax.axis_index("section")
    is_first = section_index == 0
    kept_empty = (
        jnp.zeros((seq_rows, bin_count, channels), jnp.bfloat16),
        jnp.zeros((channels,), jnp.float32),
        jnp.zeros((channels,), jnp.float32),
        jnp.zeros((seq_rows, bin_count + taps_first - 1, channels), jnp.bfloat16),
        jnp.zeros((seq_rows, pooled_bins, channels), jnp.float32),
        jnp.zeros((seq_rows,), jnp.int32),
        jnp.zeros((seq_rows,), jnp.int32),
    )
    ledger = {
        "inbox": jnp.zeros((seq_rows, pooled_bins, channels), jnp.bfloat16),
        "outbox": jnp.zeros((seq_rows, pooled_bins, channels), jnp.bfloat16),
        "kept": [kept_empty for batch_index in range(MB)],
        "wide_grad": jnp.zeros((taps_first, channels, channels), jnp.float32),
        "first_gain": jnp.zeros((channels,), jnp.float32),
        "first_bias": jnp.zeros((channels,), jnp.float32),
        "narrow_grad": jnp.zeros((taps_second, channels, hidden), jnp.float32),
        "second_gain": jnp.zeros((channels,), jnp.float32),
        "second_bias": jnp.zeros((channels,), jnp.float32),
        "last_grad": jnp.zeros((hidden, channels), jnp.float32),
        "third_gain": jnp.zeros((hidden,), jnp.float32),
        "third_bias": jnp.zeros((hidden,), jnp.float32),
        "results": jnp.zeros((MB * seq_rows, pooled_bins, channels), jnp.bfloat16),
        "returned": jnp.zeros((MB * seq_rows, bin_count, channels), jnp.bfloat16),
    }
    for step_index in range(MB + 2):

        def first_section(ledger, step_index=step_index):
            ledger = dict(ledger)
            kept_list = list(ledger["kept"])
            if step_index < MB:
                start_row = step_index * seq_rows
                end_row = start_row + seq_rows
                pooled, kept_data = first_forward(
                    inputs[start_row:end_row],
                    shifts[start_row:end_row],
                    flips[start_row:end_row],
                    norm1_gain,
                    norm1_bias,
                    conv1_weight,
                )
                ledger["outbox"] = pooled
                kept_list[step_index] = kept_data
            else:
                ledger["outbox"] = jnp.zeros_like(ledger["outbox"])
            if step_index >= 2:
                batch_index = step_index - 2
                start_row = batch_index * seq_rows
                returned, weight_grad, partials = first_backward(
                    ledger["inbox"], kept_list[batch_index], norm1_gain, norm1_bias, conv1_weight
                )
                ledger["returned"] = (
                    ledger["returned"].at[start_row : start_row + seq_rows].set(returned)
                )
                ledger["wide_grad"] = ledger["wide_grad"] + weight_grad
                ledger["first_bias"] = ledger["first_bias"] + partials[0]
                ledger["first_gain"] = ledger["first_gain"] + partials[1]
            ledger["kept"] = kept_list
            return ledger

        def second_section(ledger, step_index=step_index):
            ledger = dict(ledger)
            if 1 <= step_index <= MB:
                batch_index = step_index - 1
                start_row = batch_index * seq_rows
                cotangent = out_grad[start_row : start_row + seq_rows]
                result_block, grad_pooled, narrow_gradient, last_grad, second_parts, third_parts = (
                    second_pass(
                        ledger["inbox"],
                        cotangent,
                        norm2_gain,
                        norm2_bias,
                        dilated_conv2_weight,
                        norm3_gain,
                        norm3_bias,
                        conv3_weight,
                    )
                )
                ledger["results"] = (
                    ledger["results"].at[start_row : start_row + seq_rows].set(result_block)
                )
                ledger["outbox"] = grad_pooled
                ledger["narrow_grad"] = ledger["narrow_grad"] + narrow_gradient
                ledger["last_grad"] = ledger["last_grad"] + last_grad
                ledger["second_bias"] = ledger["second_bias"] + second_parts[0]
                ledger["second_gain"] = ledger["second_gain"] + second_parts[1]
                ledger["third_bias"] = ledger["third_bias"] + third_parts[0]
                ledger["third_gain"] = ledger["third_gain"] + third_parts[1]
            else:
                ledger["outbox"] = jnp.zeros_like(ledger["outbox"])
            return ledger

        first_ledger = first_section(ledger)
        second_ledger = second_section(ledger)
        ledger = jax.tree.map(
            lambda left, right: jnp.where(is_first, left, right), first_ledger, second_ledger
        )
        if step_index < MB + 1:
            ledger = dict(ledger)
            ledger["inbox"] = from_partner(for_sending(ledger["outbox"]), "section", 0)
    half_width = channels // 2
    result_low = passed_along(for_sending(ledger["results"][:, :, :half_width]), "section", -1)
    result_shard = jnp.where(is_first, result_low, ledger["results"][:, :, half_width:])
    grad_high = passed_along(for_sending(ledger["returned"][:, :, half_width:]), "section", 1)
    input_shard = jnp.where(is_first, ledger["returned"][:, :, :half_width], grad_high)
    summed = tuple(
        lax.psum(
            (
                ledger["wide_grad"],
                ledger["first_gain"],
                ledger["first_bias"],
                ledger["narrow_grad"],
                ledger["second_gain"],
                ledger["second_bias"],
                ledger["last_grad"],
                ledger["third_gain"],
                ledger["third_bias"],
            ),
            ("section", "dp", "seq"),
        )
    )
    return (
        result_shard,
        input_shard,
        summed[0],
        summed[1],
        summed[2],
        summed[3],
        summed[4],
        summed[5],
        summed[6],
        summed[7],
        summed[8],
    )


def solution(mesh):
    return jax.shard_map(
        on_device,
        mesh=mesh,
        in_specs=(
            P("dp", "seq", None),
            P("dp"),
            P("dp"),
            P(),
            P(),
            P(),
            P(),
            P(),
            P(),
            P(),
            P(),
            P(),
            P("dp", "seq", None),
        ),
        out_specs=(
            P("dp", "seq", "section"),
            P("dp", "seq", "section"),
            P(),
            P(),
            P(),
            P(),
            P(),
            P(),
            P(),
            P(),
            P(),
        ),
        check_vma=False,
    )
```

profile of v0, /device:TPU:9, one launch (start us, length us, event | category | flops | bytes accessed | tf_op | source)
XLA Modules:
  0.0 2301.0 jit_solution(10617302730172117243)
XLA Ops:
  198.7 33.3 %psum.399 = f32[768]{0:T(1024)S(1)} all-reduce(f32[768]{0:T(1024)S(1)} %get-tuple-element.272), channel_id=1, replica_groups=mesh['section'=2,'dp'=4,'seq'=4] {'dp','seq'}, use_global_device_ids=true, to_apply=%region_1.2 | all-reduce | flops 768 | bytes 6144 | tf_op jit(solution)/shard_map/psum | solution.py:88
  232.9 35.1 %psum.400 = f32[768]{0:T(1024)S(1)} all-reduce(f32[768]{0:T(1024)S(1)} %fusion.38), channel_id=1, replica_groups=mesh['section'=2,'dp'=4,'seq'=4] {'dp','seq'}, use_global_device_ids=true, to_apply=%region_3.4 | all-reduce | flops 768 | bytes 6144 | tf_op jit(solution)/shard_map/psum | solution.py:90
  353.6 33.6 %psum.402 = f32[768]{0:T(1024)} all-reduce(f32[768]{0:T(1024)} %fusion.395), channel_id=1, replica_groups=mesh['section'=2,'dp'=4,'seq'=4] {'dp','seq'}, use_global_device_ids=true, to_apply=%region_7.8 | all-reduce | flops 768 | bytes 6144 | tf_op jit(solution)/shard_map/psum | solution.py:90
  431.7 32.2 %psum.404 = f32[384]{0:T(512)} all-reduce(f32[384]{0:T(512)} %multiply_reduce_fusion.7), channel_id=1, replica_groups=mesh['section'=2,'dp'=4,'seq'=4] {'dp','seq'}, use_global_device_ids=true, to_apply=%region_11.12 | all-reduce | flops 384 | bytes 3072 | tf_op jit(solution)/shard_map/psum | solution.py:90
  515.3 54.3 %all-reduce.11 = (f32[768]{0:T(1024)}, f32[768]{0:T(1024)}, f32[768]{0:T(1024)}) all-reduce(f32[768]{0:T(1024)} %get-tuple-element.210, f32[768]{0:T(1024)} %get-tuple-element.209, f32[768]{0:T(1024)} %fusion.28), channel_id=1, replica_groups=mesh['section'=2,'dp'=4,'seq'=4] {'dp','seq'}, use_global_device_ids=true, to_apply=%region_23.24 | all-reduce | flops 2304 | bytes 18432 | tf_op jit(solution)/shard_map/psum | solution.py:98
  601.4 52.2 %collective-permute-start.17 = (bf16[1,256,768]{2,1,0:T(8,128)(2,1)S(1)}, bf16[1,256,768]{2,1,0:T(8,128)(2,1)S(1)}, u32[]{:S(2)}, u32[]{:S(2)}) collective-permute-start(bf16[1,256,768]{2,1,0:T(8,128)(2,1)S(1)} %fusion.530), channel_id=1, source_target_pairs={{0,16},{16,0},{1,17},{17,1},{2,18},{18,2},{3,19},{19,3},{4,20},{20... | collective-permute-start | bytes 1179656 | tf_op jit(solution)/shard_map/ppermute | solution.py:25
  688.0 32.4 %psum.412 = f32[768]{0:T(1024)S(1)} all-reduce(f32[768]{0:T(1024)S(1)} %fusion.380), channel_id=1, replica_groups=mesh['section'=2,'dp'=4,'seq'=4] {'dp','seq'}, use_global_device_ids=true, to_apply=%region_27.28 | all-reduce | flops 768 | bytes 6144 | tf_op jit(solution)/shard_map/psum | solution.py:90
  764.2 32.1 %psum.414 = f32[384]{0:T(512)} all-reduce(f32[384]{0:T(512)} %multiply_reduce_fusion.5), channel_id=1, replica_groups=mesh['section'=2,'dp'=4,'seq'=4] {'dp','seq'}, use_global_device_ids=true, to_apply=%region_31.32 | all-reduce | flops 384 | bytes 3072 | tf_op jit(solution)/shard_map/psum | solution.py:90
  851.3 54.6 %all-reduce.9 = (f32[768]{0:T(1024)S(1)}, f32[768]{0:T(1024)S(1)}, f32[768]{0:T(1024)S(1)}) all-reduce(f32[768]{0:T(1024)S(1)} %get-tuple-element.208, f32[768]{0:T(1024)S(1)} %get-tuple-element.207, f32[768]{0:T(1024)S(1)} %copy-done.200), channel_id=1, replica_groups=mesh['section'=2,'dp'=4,'seq'=4] {'dp','seq'}, use_global_device_ids=true, to_apply=%region_43.44 | all-reduce | flops 2304 | bytes 18432 | tf_op jit(solution)/shard_map/psum | solution.py:98
  945.3 51.8 %collective-permute-start.28 = (bf16[1,256,768]{2,1,0:T(8,128)(2,1)}, bf16[1,256,768]{2,1,0:T(8,128)(2,1)S(1)}, u32[]{:S(2)}, u32[]{:S(2)}) collective-permute-start(bf16[1,256,768]{2,1,0:T(8,128)(2,1)} %get-tuple-element.340), channel_id=1, source_target_pairs={{0,16},{16,0},{1,17},{17,1},{2,18},{18,2},{3,19},{19,3},{4,20},{20... | collective-permute-start | bytes 1179656 | tf_op jit(solution)/shard_map/ppermute | solution.py:25
  1018.2 32.2 %psum.421 = f32[768]{0:T(1024)} all-reduce(f32[768]{0:T(1024)} %convert_reduce_fusion.5), channel_id=1, replica_groups=mesh['section'=2,'dp'=4,'seq'=4] {'dp','seq'}, use_global_device_ids=true, to_apply=%region_45.46 | all-reduce | flops 768 | bytes 6144 | tf_op jit(solution)/shard_map/psum | solution.py:88
  1128.9 32.4 %psum.424 = f32[384]{0:T(512)} all-reduce(f32[384]{0:T(512)} %multiply_reduce_fusion.3), channel_id=1, replica_groups=mesh['section'=2,'dp'=4,'seq'=4] {'dp','seq'}, use_global_device_ids=true, to_apply=%region_51.52 | all-reduce | flops 384 | bytes 3072 | tf_op jit(solution)/shard_map/psum | solution.py:90
  1216.0 54.6 %all-reduce.7 = (f32[768]{0:T(1024)S(1)}, f32[768]{0:T(1024)S(1)}, f32[768]{0:T(1024)S(1)}) all-reduce(f32[768]{0:T(1024)S(1)} %get-tuple-element.206, f32[768]{0:T(1024)S(1)} %get-tuple-element.205, f32[768]{0:T(1024)S(1)} %copy-done.201), channel_id=1, replica_groups=mesh['section'=2,'dp'=4,'seq'=4] {'dp','seq'}, use_global_device_ids=true, to_apply=%region_63.64 | all-reduce | flops 2304 | bytes 18432 | tf_op jit(solution)/shard_map/psum | solution.py:98
  1311.9 52.4 %collective-permute-start.39 = (bf16[1,256,768]{2,1,0:T(8,128)(2,1)}, bf16[1,256,768]{2,1,0:T(8,128)(2,1)S(1)}, u32[]{:S(2)}, u32[]{:S(2)}) collective-permute-start(bf16[1,256,768]{2,1,0:T(8,128)(2,1)} %get-tuple-element.339), channel_id=1, source_target_pairs={{0,16},{16,0},{1,17},{17,1},{2,18},{18,2},{3,19},{19,3},{4,20},{20... | collective-permute-start | bytes 1179656 | tf_op jit(solution)/shard_map/ppermute | solution.py:25
  1386.2 31.9 %psum.431 = f32[768]{0:T(1024)} all-reduce(f32[768]{0:T(1024)} %convert_reduce_fusion.4), channel_id=1, replica_groups=mesh['section'=2,'dp'=4,'seq'=4] {'dp','seq'}, use_global_device_ids=true, to_apply=%region_65.66 | all-reduce | flops 768 | bytes 6144 | tf_op jit(solution)/shard_map/psum | solution.py:88
  1496.8 32.1 %psum.434 = f32[384]{0:T(512)} all-reduce(f32[384]{0:T(512)} %multiply_reduce_fusion.1), channel_id=1, replica_groups=mesh['section'=2,'dp'=4,'seq'=4] {'dp','seq'}, use_global_device_ids=true, to_apply=%region_71.72 | all-reduce | flops 384 | bytes 3072 | tf_op jit(solution)/shard_map/psum | solution.py:90
  1627.6 46.5 %collective-permute-start.63 = (bf16[1,256,768]{2,1,0:T(8,128)(2,1)S(1)}, bf16[1,256,768]{2,1,0:T(8,128)(2,1)S(1)}, u32[]{:S(2)}, u32[]{:S(2)}) collective-permute-start(bf16[1,256,768]{2,1,0:T(8,128)(2,1)S(1)} %copy-done.92), channel_id=1, source_target_pairs={{0,16},{16,0},{1,17},{17,1},{2,18},{18,2},{3,19},{19,3},{4,20},{20... | collective-permute-start | bytes 1179656 | tf_op jit(solution)/shard_map/ppermute | solution.py:25
  1709.9 56.2 %all-reduce.4 = (f32[768]{0:T(1024)S(1)}, f32[768]{0:T(1024)S(1)}, f32[768]{0:T(1024)S(1)}, f32[768]{0:T(1024)S(1)}, f32[768]{0:T(1024)S(1)}, /*index=5*/f32[768]{0:T(1024)S(1)}, f32[768]{0:T(1024)S(1)}, f32[768]{0:T(1024)S(1)}) all-reduce(f32[768]{0:T(1024)S(1)} %copy-done.221, ...), channel_id=1, replica_groups=mesh['section'=2,'dp'=4,'seq'=4] {'dp','seq'}, use_global_device_ids=true, to_apply=%region_75.76 | all-reduce | flops 6144 | bytes 49152 | tf_op jit(solution)/shard_map/psum | solution.py:98
  1870.1 36.7 %collective-permute-done.53 = bf16[1,512,768]{2,1,0:T(8,128)(2,1)} collective-permute-done((bf16[1,512,768]{2,1,0:T(8,128)(2,1)S(1)}, bf16[1,512,768]{2,1,0:T(8,128)(2,1)}, u32[]{:S(2)}, u32[]{:S(2)}) %collective-permute-start.53) | collective-permute-done | bytes 786464 | tf_op jit(solution)/shard_map/ppermute | solution.py:25
  1906.8 50.6 %collective-permute-done.59 = bf16[1,512,768]{2,1,0:T(8,128)(2,1)} collective-permute-done((bf16[1,512,768]{2,1,0:T(8,128)(2,1)S(1)}, bf16[1,512,768]{2,1,0:T(8,128)(2,1)}, u32[]{:S(2)}, u32[]{:S(2)}) %collective-permute-start.59) | collective-permute-done | bytes 786464 | tf_op jit(solution)/shard_map/ppermute | solution.py:25
  1957.3 44.3 %collective-permute-done.68 = bf16[1,512,768]{2,1,0:T(8,128)(2,1)} collective-permute-done((bf16[1,512,768]{2,1,0:T(8,128)(2,1)S(1)}, bf16[1,512,768]{2,1,0:T(8,128)(2,1)}, u32[]{:S(2)}, u32[]{:S(2)}) %collective-permute-start.68) | collective-permute-done | bytes 786464 | tf_op jit(solution)/shard_map/ppermute | solution.py:25
  2041.5 40.9 %collective-permute-done.69 = bf16[1,512,768]{2,1,0:T(8,128)(2,1)} collective-permute-done((bf16[1,512,768]{2,1,0:T(8,128)(2,1)}, bf16[1,512,768]{2,1,0:T(8,128)(2,1)}, u32[]{:S(2)}, u32[]{:S(2)}) %collective-permute-start.69) | collective-permute-done | bytes 786464 | tf_op jit(solution)/shard_map/ppermute | solution.py:25
  2136.1 42.1 %all-reduce.2 = (f32[768]{0:T(1024)}, f32[768]{0:T(1024)}, f32[768]{0:T(1024)}, f32[768]{0:T(1024)}, f32[384]{0:T(512)}, /*index=5*/f32[384]{0:T(512)}) all-reduce(f32[768]{0:T(1024)S(1)} %get-tuple-element.419, f32[768]{0:T(1024)S(1)} %get-tuple-element.418, ...), channel_id=1, replica_groups=mesh['section'=2,'dp'=4,'seq'=4] {'section','dp','seq'}, use_global_device_ids=true, to_apply=%region_97.98 | all-reduce | flops 3840 | bytes 30720 | tf_op jit(solution)/shard_map/psum | solution.py:365
  2182.3 98.1 %all-reduce.15.cloned.1.call-done = (f32[5,768,768]{2,1,0:T(8,128)}, f32[3,768,384]{2,1,0:T(8,128)}, f32[384,768]{1,0:T(8,128)}) async-done(((f32[5,768,768]{2,1,0:T(8,128)}, f32[3,768,384]{2,1,0:T(8,128)}, f32[384,768]{1,0:T(8,128)}), (f32[5,768,768]{2,1,0:T(8,128)}, f32[3,768,384]{2,1,0:T(8,128)}, f32[384,768]{1,0:T(8,128)})) %all-reduce.15.cloned.1.call-update) | async-done | bytes 16515088 | tf_op jit(solution)/shard_map/psum | solution.py:365
  (972 shorter events, 1210.2 us)
Async XLA Ops:
  7.2 2273.3 %all-reduce.15.cloned.1.call-start = ((), (), s32[]{:S(2)}) async-start(), calls=%async_computation | async-start | bytes 33030144 | tf_op jit(solution)/shard_map/psum | solution.py:365
  10.9 81.6 %collective-permute-start.9 = (bf16[1,512,768]{2,1,0:T(8,128)(2,1)S(1)}, bf16[1,512,768]{2,1,0:T(8,128)(2,1)}, u32[]{:S(2)}, u32[]{:S(2)}) collective-permute-start(bf16[1,512,768]{2,1,0:T(8,128)(2,1)S(1)} %get-tuple-element.279), channel_id=1, source_target_pairs={{0,1},{1,0},{2,3},{3,2},{4,5},{5,4},{6,7},{7,6},{8,9},{9,8},{10,11... | collective-permute-start | bytes 2359304 | tf_op jit(solution)/shard_map/ppermute | solution.py:25
  11.0 98.4 %collective-permute-start.20 = (bf16[1,512,768]{2,1,0:T(8,128)(2,1)S(1)}, bf16[1,512,768]{2,1,0:T(8,128)(2,1)}, u32[]{:S(2)}, u32[]{:S(2)}) collective-permute-start(bf16[1,512,768]{2,1,0:T(8,128)(2,1)S(1)} %get-tuple-element.281), channel_id=1, source_target_pairs={{0,1},{1,0},{2,3},{3,2},{4,5},{5,4},{6,7},{7,6},{8,9},{9,8},{10,11... | collective-permute-start | bytes 2359304 | tf_op jit(solution)/shard_map/ppermute | solution.py:25
  27.9 92.5 %collective-permute-start.32 = (bf16[1,512,768]{2,1,0:T(8,128)(2,1)}, bf16[1,512,768]{2,1,0:T(8,128)(2,1)}, u32[]{:S(2)}, u32[]{:S(2)}) collective-permute-start(bf16[1,512,768]{2,1,0:T(8,128)(2,1)} %collective-permute-done.31), channel_id=1, source_target_pairs={{0,2},{2,0},{1,3},{3,1},{4,6},{6,4},{5,7},{7,5},{8,10},{10,8},{9,1... | collective-permute-start | bytes 2359304 | tf_op jit(solution)/shard_map/ppermute | solution.py:25
  59.7 72.7 %collective-permute-start.1 = (bf16[1,512,768]{2,1,0:T(8,128)(2,1)}, bf16[1,512,768]{2,1,0:T(8,128)(2,1)S(1)}, u32[]{:S(2)}, u32[]{:S(2)}) collective-permute-start(bf16[1,512,768]{2,1,0:T(8,128)(2,1)} %collective-permute-done), channel_id=1, source_target_pairs={{0,2},{2,0},{1,3},{3,1},{4,6},{6,4},{5,7},{7,5},{8,10},{10,8},{9,1... | collective-permute-start | bytes 2359304 | tf_op jit(solution)/shard_map/ppermute | solution.py:25
  92.5 70.5 %collective-permute-start.10 = (bf16[1,512,768]{2,1,0:T(8,128)(2,1)}, bf16[1,512,768]{2,1,0:T(8,128)(2,1)S(1)}, u32[]{:S(2)}, u32[]{:S(2)}) collective-permute-start(bf16[1,512,768]{2,1,0:T(8,128)(2,1)} %collective-permute-done.9), channel_id=1, source_target_pairs={{0,2},{2,0},{1,3},{3,1},{4,6},{6,4},{5,7},{7,5},{8,10},{10,8},{9,1... | collective-permute-start | bytes 2359304 | tf_op jit(solution)/shard_map/ppermute | solution.py:25
  109.4 70.5 %collective-permute-start.21 = (bf16[1,512,768]{2,1,0:T(8,128)(2,1)}, bf16[1,512,768]{2,1,0:T(8,128)(2,1)S(1)}, u32[]{:S(2)}, u32[]{:S(2)}) collective-permute-start(bf16[1,512,768]{2,1,0:T(8,128)(2,1)} %collective-permute-done.20), channel_id=1, source_target_pairs={{0,2},{2,0},{1,3},{3,1},{4,6},{6,4},{5,7},{7,5},{8,10},{10,8},{9,1... | collective-permute-start | bytes 2359304 | tf_op jit(solution)/shard_map/ppermute | solution.py:25
  193.4 97.1 %collective-permute-start.12 = (bf16[1,3,768]{2,1,0:T(4,128)(2,1)S(1)}, bf16[1,3,768]{2,1,0:T(4,128)(2,1)S(1)}, u32[]{:S(2)}, u32[]{:S(2)}) collective-permute-start(bf16[1,3,768]{2,1,0:T(4,128)(2,1)S(1)} %get-tuple-element.333), channel_id=1, source_target_pairs={{1,0},{2,1},{3,2},{0,3},{5,4},{6,5},{7,6},{4,7},{9,8},{10,9},{11,1... | collective-permute-start | bytes 13832 | tf_op jit(solution)/shard_map/ppermute | solution.py:36
  195.0 97.3 %collective-permute-start.11 = (bf16[1,3,768]{2,1,0:T(4,128)(2,1)S(1)}, bf16[1,3,768]{2,1,0:T(4,128)(2,1)S(1)}, u32[]{:S(2)}, u32[]{:S(2)}) collective-permute-start(bf16[1,3,768]{2,1,0:T(4,128)(2,1)S(1)} %get-tuple-element.332), channel_id=1, source_target_pairs={{0,1},{1,2},{2,3},{3,0},{4,5},{5,6},{6,7},{7,4},{8,9},{9,10},{10,1... | collective-permute-start | bytes 13832 | tf_op jit(solution)/shard_map/ppermute | solution.py:35
  195.0 119.5 %collective-permute-start.23 = (bf16[1,3,768]{2,1,0:T(4,128)(2,1)S(1)}, bf16[1,3,768]{2,1,0:T(4,128)(2,1)S(1)}, u32[]{:S(2)}, u32[]{:S(2)}) collective-permute-start(bf16[1,3,768]{2,1,0:T(4,128)(2,1)S(1)} %get-tuple-element.329), channel_id=1, source_target_pairs={{1,0},{2,1},{3,2},{0,3},{5,4},{6,5},{7,6},{4,7},{9,8},{10,9},{11,1... | collective-permute-start | bytes 13832 | tf_op jit(solution)/shard_map/ppermute | solution.py:36
  197.9 116.6 %collective-permute-start.22 = (bf16[1,3,768]{2,1,0:T(4,128)(2,1)S(1)}, bf16[1,3,768]{2,1,0:T(4,128)(2,1)S(1)}, u32[]{:S(2)}, u32[]{:S(2)}) collective-permute-start(bf16[1,3,768]{2,1,0:T(4,128)(2,1)S(1)} %get-tuple-element.328), channel_id=1, source_target_pairs={{0,1},{1,2},{2,3},{3,0},{4,5},{5,6},{6,7},{7,4},{8,9},{9,10},{10,1... | collective-permute-start | bytes 13832 | tf_op jit(solution)/shard_map/ppermute | solution.py:35
  601.4 55.2 %collective-permute-start.17 = (bf16[1,256,768]{2,1,0:T(8,128)(2,1)S(1)}, bf16[1,256,768]{2,1,0:T(8,128)(2,1)S(1)}, u32[]{:S(2)}, u32[]{:S(2)}) collective-permute-start(bf16[1,256,768]{2,1,0:T(8,128)(2,1)S(1)} %fusion.530), channel_id=1, source_target_pairs={{0,16},{16,0},{1,17},{17,1},{2,18},{18,2},{3,19},{19,3},{4,20},{20... | collective-permute-start | bytes 1179656 | tf_op jit(solution)/shard_map/ppermute | solution.py:25
  945.3 72.1 %collective-permute-start.28 = (bf16[1,256,768]{2,1,0:T(8,128)(2,1)}, bf16[1,256,768]{2,1,0:T(8,128)(2,1)S(1)}, u32[]{:S(2)}, u32[]{:S(2)}) collective-permute-start(bf16[1,256,768]{2,1,0:T(8,128)(2,1)} %get-tuple-element.340), channel_id=1, source_target_pairs={{0,16},{16,0},{1,17},{17,1},{2,18},{18,2},{3,19},{19,3},{4,20},{20... | collective-permute-start | bytes 1179656 | tf_op jit(solution)/shard_map/ppermute | solution.py:25
  1311.9 73.5 %collective-permute-start.39 = (bf16[1,256,768]{2,1,0:T(8,128)(2,1)}, bf16[1,256,768]{2,1,0:T(8,128)(2,1)S(1)}, u32[]{:S(2)}, u32[]{:S(2)}) collective-permute-start(bf16[1,256,768]{2,1,0:T(8,128)(2,1)} %get-tuple-element.339), channel_id=1, source_target_pairs={{0,16},{16,0},{1,17},{17,1},{2,18},{18,2},{3,19},{19,3},{4,20},{20... | collective-permute-start | bytes 1179656 | tf_op jit(solution)/shard_map/ppermute | solution.py:25
  1619.8 58.5 %collective-permute-start.56 = (bf16[1,2,768]{2,1,0:T(2,128)(2,1)S(1)}, bf16[1,2,768]{2,1,0:T(2,128)(2,1)S(1)}, u32[]{:S(2)}, u32[]{:S(2)}) collective-permute-start(bf16[1,2,768]{2,1,0:T(2,128)(2,1)S(1)} %get-tuple-element.317), channel_id=1, source_target_pairs={{0,1},{1,2},{2,3},{4,5},{5,6},{6,7},{8,9},{9,10},{10,11},{12,13},{... | collective-permute-start | bytes 9224 | tf_op jit(solution)/shard_map/ppermute | solution.py:35
  1627.6 57.9 %collective-permute-start.63 = (bf16[1,256,768]{2,1,0:T(8,128)(2,1)S(1)}, bf16[1,256,768]{2,1,0:T(8,128)(2,1)S(1)}, u32[]{:S(2)}, u32[]{:S(2)}) collective-permute-start(bf16[1,256,768]{2,1,0:T(8,128)(2,1)S(1)} %copy-done.92), channel_id=1, source_target_pairs={{0,16},{16,0},{1,17},{17,1},{2,18},{18,2},{3,19},{19,3},{4,20},{20... | collective-permute-start | bytes 1179656 | tf_op jit(solution)/shard_map/ppermute | solution.py:25
  1853.7 103.6 %collective-permute-start.59 = (bf16[1,512,768]{2,1,0:T(8,128)(2,1)S(1)}, bf16[1,512,768]{2,1,0:T(8,128)(2,1)}, u32[]{:S(2)}, u32[]{:S(2)}) collective-permute-start(bf16[1,512,768]{2,1,0:T(8,128)(2,1)S(1)} %fusion.290), channel_id=1, source_target_pairs={{0,1},{1,0},{2,3},{3,2},{4,5},{5,4},{6,7},{7,6},{8,9},{9,8},{10,11... | collective-permute-start | bytes 2359304 | tf_op jit(solution)/shard_map/ppermute | solution.py:25
  1855.9 145.7 %collective-permute-start.68 = (bf16[1,512,768]{2,1,0:T(8,128)(2,1)S(1)}, bf16[1,512,768]{2,1,0:T(8,128)(2,1)}, u32[]{:S(2)}, u32[]{:S(2)}) collective-permute-start(bf16[1,512,768]{2,1,0:T(8,128)(2,1)S(1)} %fusion.285), channel_id=1, source_target_pairs={{0,1},{1,0},{2,3},{3,2},{4,5},{5,4},{6,7},{7,6},{8,9},{9,8},{10,11... | collective-permute-start | bytes 2359304 | tf_op jit(solution)/shard_map/ppermute | solution.py:25
  1867.6 136.1 %collective-permute-start.48 = (bf16[1,512,768]{2,1,0:T(8,128)(2,1)S(1)}, bf16[1,512,768]{2,1,0:T(8,128)(2,1)}, u32[]{:S(2)}, u32[]{:S(2)}) collective-permute-start(bf16[1,512,768]{2,1,0:T(8,128)(2,1)S(1)} %collective-permute-done.47), channel_id=1, source_target_pairs={{0,2},{2,0},{1,3},{3,1},{4,6},{6,4},{5,7},{7,5},{8,10},{10,8},{9,1... | collective-permute-start | bytes 2359304 | tf_op jit(solution)/shard_map/ppermute | solution.py:25
  1906.8 110.9 %collective-permute-start.54 = (bf16[1,512,768]{2,1,0:T(8,128)(2,1)}, bf16[1,512,768]{2,1,0:T(8,128)(2,1)}, u32[]{:S(2)}, u32[]{:S(2)}) collective-permute-start(bf16[1,512,768]{2,1,0:T(8,128)(2,1)} %collective-permute-done.53), channel_id=1, source_target_pairs={{0,2},{2,0},{1,3},{3,1},{4,6},{6,4},{5,7},{7,5},{8,10},{10,8},{9,1... | collective-permute-start | bytes 2359304 | tf_op jit(solution)/shard_map/ppermute | solution.py:25
  1957.3 72.3 %collective-permute-start.60 = (bf16[1,512,768]{2,1,0:T(8,128)(2,1)}, bf16[1,512,768]{2,1,0:T(8,128)(2,1)}, u32[]{:S(2)}, u32[]{:S(2)}) collective-permute-start(bf16[1,512,768]{2,1,0:T(8,128)(2,1)} %collective-permute-done.59), channel_id=1, source_target_pairs={{0,2},{2,0},{1,3},{3,1},{4,6},{6,4},{5,7},{7,5},{8,10},{10,8},{9,1... | collective-permute-start | bytes 2359304 | tf_op jit(solution)/shard_map/ppermute | solution.py:25
  2001.6 80.9 %collective-permute-start.69 = (bf16[1,512,768]{2,1,0:T(8,128)(2,1)}, bf16[1,512,768]{2,1,0:T(8,128)(2,1)}, u32[]{:S(2)}, u32[]{:S(2)}) collective-permute-start(bf16[1,512,768]{2,1,0:T(8,128)(2,1)} %collective-permute-done.68), channel_id=1, source_target_pairs={{0,2},{2,0},{1,3},{3,1},{4,6},{6,4},{5,7},{7,5},{8,10},{10,8},{9,1... | collective-permute-start | bytes 2359304 | tf_op jit(solution)/shard_map/ppermute | solution.py:25
  2103.9 75.2 %collective-permute-start.70 = (bf16[4,512,384]{2,1,0:T(8,128)(2,1)}, bf16[4,512,384]{2,1,0:T(8,128)(2,1)}, u32[]{:S(2)}, u32[]{:S(2)}) collective-permute-start(bf16[4,512,384]{2,1,0:T(8,128)(2,1)} %slice.1129), channel_id=1, source_target_pairs={{0,16},{1,17},{2,18},{3,19},{4,20},{5,21},{6,22},{7,23},{8,24},{9,... | collective-permute-start | bytes 4718600 | tf_op jit(solution)/shard_map/ppermute | solution.py:44
  2107.5 70.6 %collective-permute-start.42 = (bf16[4,256,384]{2,1,0:T(8,128)(2,1)}, bf16[4,256,384]{2,1,0:T(8,128)(2,1)S(1)}, u32[]{:S(2)}, u32[]{:S(2)}) collective-permute-start(bf16[4,256,384]{2,1,0:T(8,128)(2,1)} %slice.1090), channel_id=1, source_target_pairs={{16,0},{17,1},{18,2},{19,3},{20,4},{21,5},{22,6},{23,7},{24,8},{25... | collective-permute-start | bytes 2359304 | tf_op jit(solution)/shard_map/ppermute | solution.py:44
  (315 other events, 5641.0 us)
Sparse Core Ops, SparseCore 0:
  1831.9 448.5 all-reduce.14
where the time goes:
time: 2320 us; the launch traced here: 2300 us
  blocking collectives  985 us (42%)
  waiting for transfers between devices  409 us (18%)
  starting transfers between devices  392 us (17%)
  matrix products  197 us (8%)
  local copies, waits for them, and re-layouts  171 us (7%)
  other arithmetic  119 us (5%)
  between operations  28.4 us (1%)
    psum x9, blocking collectives, norm_back(): bias_total, gain_total = lax.psum((bias_part, gain_part), ('dp', 'seq'))  374 us
    ppermute x21, waiting for transfers between devices, from_partner(): return lax.ppermute(block, axis, route)  305 us
    psum x9, blocking collectives, moments(): lax.psum(jnp.sum(centred * centred, axis=(0, 1)), ('dp', 'seq')) / tally  291 us
    psum x9, blocking collectives, moments(): average = lax.psum(jnp.sum(values, axis=(0, 1)), ('dp', 'seq')) / tally  278 us
    ppermute x21, starting transfers between devices, from_partner(): return lax.ppermute(block, axis, route)  242 us
    psum x1, waiting for transfers between devices, on_device(): lax.psum((ledger['wide_grad'], ledger['first_gain'], ledger['first_bias']...  98.1 us
    rev x8, local copies, waits for them, and re-layouts, mirror(): return jnp.flip(arrived, axis=1)  82.6 us
    ppermute x24, starting transfers between devices, extended(): after = lax.ppermute(first, axis, down)  78.4 us
  transfers between devices with their start and end apart: 72, of which 20 were waited for; matrix products, arithmetic and copies ran while one was open for 10% of the time, Pallas kernels for 0%

commit v1 on v0

v1 whole, which is shorter than its diff:
```python
import functools

import jax
import jax.numpy as jnp
from jax import lax
from jax.experimental import pallas as pl
from jax.experimental.pallas import tpu as pltpu
from jax.sharding import PartitionSpec as P

DILATION_SIZE = 11
EPSILON = 0.001
EDGE = 16
MESH = pl.DeviceIdType.MESH
F32 = jnp.float32
BF16 = jnp.bfloat16
SCALE = 0.7978845608028654
CUBIC = 0.044715
TN = (((0,), (0,)), ((), ()))
NT = (((1,), (1,)), ((), ()))


def gelu(u):
    return 0.5 * u * (1.0 + jnp.tanh(SCALE * u * (1.0 + CUBIC * (u * u))))


def gelu_slope(u):
    square = u * u
    t = jnp.tanh(SCALE * u * (1.0 + CUBIC * square))
    return 0.5 * (1.0 + t) + (0.5 * SCALE) * u * (1.0 - t * t) * (1.0 + (3.0 * CUBIC) * square)


def chunks(count, body, carry=0, unroll=1):
    def step(i, carry):
        return body(pl.multiple_of(i * EDGE, EDGE), carry)

    return lax.fori_loop(0, count // EDGE, step, carry, unroll=unroll)


def eight(row):
    return jnp.broadcast_to(row, (8, row.shape[-1]))


def halves(block):
    return block.reshape(block.shape[0] // 8, 8, block.shape[1])


def flat(block):
    return block.reshape(block.shape[0] * 8, block.shape[2])


def row_sum(block):
    return jnp.sum(block, axis=0, keepdims=True)


class Place:
    def __init__(self, nd, nq):
        self.nd, self.nq = nd, nq
        self.s, self.d, self.q = (lax.axis_index(a) for a in ("section", "dp", "seq"))
        self.mirror = nq - 1 - self.q
        self.next = lax.rem(self.q + 1, nq)
        self.prev = lax.rem(self.q + nq - 1, nq)
        self.partner = (1 - self.s, self.d, self.q)

    def plane(self):
        return [(self.s, lax.rem(self.d + i, self.nd), self.q) for i in range(1, self.nd)]

    def line(self):
        return [(self.s, self.d, lax.rem(self.q + i, self.nq)) for i in range(1, self.nq)]

    def greet(self, devices):
        barrier = pltpu.get_barrier_semaphore()
        for device in devices:
            pl.semaphore_signal(barrier, inc=1, device_id=device, device_id_type=MESH)
        pl.semaphore_wait(barrier, len(devices))


def remote(src, dst, send_sem, recv_sem, device):
    return pltpu.make_async_remote_copy(
        src_ref=src,
        dst_ref=dst,
        send_sem=send_sem,
        recv_sem=recv_sem,
        device_id=device,
        device_id_type=MESH,
    )


class Exchange:
    def __init__(self, place, number, plane_buf, line_buf, send_sem, recv_sem):
        self.place, self.number = place, number
        self.plane_buf, self.line_buf = plane_buf.at[number], line_buf.at[number]
        self.send_sem, self.recv_sem = send_sem.at[number], recv_sem.at[number]

    def _start(self, buf, slot, rows, devices, base):
        for at, row in enumerate(rows):
            buf[slot, at : at + 1, 0 : row.shape[1]] = row
        self.copies = [
            remote(
                buf.at[slot],
                buf.at[slot],
                self.send_sem.at[base + i],
                self.recv_sem.at[base + i],
                device,
            )
            for i, device in enumerate(devices)
        ]
        for copy in self.copies:
            copy.start()

    def _finish(self, buf, count, n_rows, width):
        for copy in self.copies:
            copy.wait()
        return [[buf[j, at : at + 1, 0:width] for at in range(n_rows)] for j in range(count)]

    def start(self, rows):
        self.n_rows, self.width = len(rows), rows[0].shape[1]
        self._start(self.plane_buf, self.place.d, rows, self.place.plane(), 0)

    def relay(self, join):
        parts = self._finish(self.plane_buf, self.place.nd, self.n_rows, self.width)
        self._start(
            self.line_buf, self.place.q, join(parts), self.place.line(), self.place.nd - 1
        )

    def finish(self, join):
        return join(self._finish(self.line_buf, self.place.nq, self.n_rows, self.width))


def join_sums(parts):
    totals = parts[0]
    for part in parts[1:]:
        totals = [total + row for total, row in zip(totals, part)]
    return totals


def join_moments(count):
    def join(parts):
        n = len(parts[0]) // 2
        totals = join_sums(parts)
        means = [total * (1.0 / len(parts)) for total in totals[:n]]
        squares = totals[n:]
        for part in parts:
            squares = [
                square + count * (row - mean) * (row - mean)
                for square, row, mean in zip(squares, part[:n], means)
            ]
        return means + squares

    return join


class Norm:
    def __init__(self, mean, inv, gain, bias):
        self.mean, self.inv, self.gain, self.bias = eight(mean), eight(inv), eight(gain), eight(bias)

    def normed(self, block):
        return (block - self.mean[None]) * self.inv[None]

    def pre(self, normed):
        return normed * self.gain[None] + self.bias[None]


def first_kernel(
    dims,
    inputs,
    out_grad,
    shifts,
    flips,
    gain1,
    bias1,
    weight1,
    gain2,
    bias2,
    weight2,
    gain3,
    bias3,
    weight3,
    taps_out,
    placed_out,
    grad_out,
    halo_out,
    stats_out,
    sums_out,
    result_out,
    conv2_out,
    conv3_out,
    window,
    placed,
    act,
    taps,
    w1,
    w2,
    w3,
    even,
    odd,
    share,
    pooled,
    edges,
    edges_in,
    second,
    narrow,
    own_grad,
    far_grad,
    third_in,
    third,
    narrow_grad,
    narrow_taps,
    second_grad,
    conv2_grad,
    conv3_grad,
    wide_grad,
    halo,
    ours,
    near,
    far,
    stats,
    sums,
    plane_buf,
    line_buf,
    local_sem,
    exchange_send,
    exchange_recv,
    halo_send,
    halo_recv,
    far_send,
    far_recv,
    result_send,
    result_recv,
):
    C, H, L, B, nd, nq = dims
    half = L // 2
    rows = B * half
    place = Place(nd, nq)
    s, q = place.s, place.q
    cross = (1 - s, place.d, place.mirror)
    place.greet(place.plane() + place.line() + [place.partner, cross])

    flip = [flips[s * B + b] for b in range(B)]
    shift = [shifts[s * B + b] for b in range(B)]
    block_at = [flip[b] * (nq - 1 - q) + (1 - flip[b]) * q for b in range(B)]
    mine = pl.ds(s * B, B)

    def exchange(number):
        return Exchange(place, number, plane_buf, line_buf, exchange_send, exchange_recv)

    def pair(number, to_next, to_prev, from_prev, from_next):
        return [
            remote(
                to_next,
                from_prev,
                halo_send.at[number, 0],
                halo_recv.at[number, 0],
                (s, place.d, place.next),
            ),
            remote(
                to_prev,
                from_next,
                halo_send.at[number, 1],
                halo_recv.at[number, 1],
                (s, place.d, place.prev),
            ),
        ]

    load = [
        pltpu.make_async_copy(inputs.at[mine], window.at[:, EDGE : EDGE + L], local_sem.at[0]),
        pltpu.make_async_copy(weight1, w1, local_sem.at[1]),
        pltpu.make_async_copy(weight2, w2, local_sem.at[2]),
        pltpu.make_async_copy(weight3, w3, local_sem.at[3]),
        pltpu.make_async_copy(out_grad.at[mine], own_grad, local_sem.at[4]),
    ]
    for copy in load:
        copy.start()
    ring = pair(
        0,
        inputs.at[mine, L - EDGE : L],
        inputs.at[mine, 0:EDGE],
        window.at[:, 0:EDGE],
        window.at[:, EDGE + L : 2 * EDGE + L],
    )
    for copy in ring:
        copy.start()

    load[0].wait()
    zero = jnp.zeros((8, C), F32)

    def moments(read, count, width):
        none = jnp.zeros((8, width), F32)
        means, squares = [], []
        for b in range(B):
            total = chunks(count, lambda r, t: t + jnp.sum(halves(read(b, r)), axis=0), none, 2)
            mean = row_sum(total) * (1.0 / count)
            mean8 = eight(mean)

            def deviations(r, t):
                away = halves(read(b, r)) - mean8[None]
                return t + jnp.sum(away * away, axis=0)

            means.append(mean)
            squares.append(row_sum(chunks(count, deviations, none, 2)))
        return means + squares

    def norms(exchange, count, gain, bias):
        exchange.relay(join_moments(float(count)))
        joined = exchange.finish(join_moments(float(count * nd)))
        scale = 1.0 / (count * nd * nq)
        inverse = [lax.rsqrt(square * scale + EPSILON) for square in joined[B:]]
        return [Norm(joined[b], inverse[b], gain[...], bias[...]) for b in range(B)]

    step = exchange(0)
    step.start(
        moments(lambda b, r: window[b, pl.ds(EDGE + r, EDGE)].astype(F32), L, C)
    )

    for copy in ring:
        copy.wait()
    tall = half + EDGE
    for b in range(B):
        for parity in range(2):
            shape = (tall, L + 2 * EDGE)
            at = 2 * (lax.broadcasted_iota(jnp.int32, shape, 0) - 8) + parity
            source = flip[b] * (L - 1) + (1 - 2 * flip[b]) * at - shift[b] + EDGE
            pick = jnp.where(lax.broadcasted_iota(jnp.int32, shape, 1) == source, 1.0, 0.0)
            placed[b, parity] = jnp.dot(
                pick.astype(BF16), window[b], preferred_element_type=F32
            ).astype(BF16)
    first_norm = norms(step, L, gain1, bias1)
    mirrored = remote(
        out_grad.at[mine],
        far_grad,
        far_send.at[0],
        far_recv.at[0],
        (s, place.d, place.mirror),
    )
    mirrored.start()
    save = [pltpu.make_async_copy(placed, placed_out, local_sem.at[5])]
    save[0].start()

    for b in range(B):
        stats[b : b + 1, :] = first_norm[b].mean[0:1]
        stats[B + b : B + b + 1, :] = first_norm[b].inv[0:1]
        for parity in range(2):

            def activate(r, c):
                norm = first_norm[b]
                value = gelu(norm.pre(norm.normed(halves(placed[b, parity, pl.ds(r, EDGE)].astype(F32)))))
                value = flat(value)
                at = lax.broadcasted_iota(jnp.int32, value.shape, 0) + (r - 8)
                at = 2 * at + (parity + block_at[b] * L)
                act[pl.ds(r, EDGE)] = jnp.where((at >= 0) & (at < nq * L), value, 0.0)
                return c

            chunks(tall, activate)

            def spread(r, c):
                values = act[pl.ds(r, 2 * EDGE)]
                for off in range(3):
                    at = (2 * off + parity) * C
                    taps[pl.ds(b * half + r, EDGE), at : at + C] = values[
                        7 + off : 7 + off + EDGE
                    ].astype(BF16)
                return c

            chunks(half, spread)
    save.append(pltpu.make_async_copy(taps, taps_out, local_sem.at[6]))
    save[1].start()

    load[1].wait()
    wide = even.shape[1]
    for j in range(C // wide):
        cols = slice(j * wide, (j + 1) * wide)
        even[...] = jnp.dot(taps[:, 0 : 5 * C], w1[:, cols], preferred_element_type=F32)
        odd[...] = jnp.dot(taps[:, C : 6 * C], w1[:, cols], preferred_element_type=F32)
        for b in range(B):

            def pool(r, c):
                at = pl.ds(b * half + r, EDGE)
                left, right = even[at, :], odd[at, :]
                away = left - right
                small = jnp.exp(-jnp.abs(away))
                pooled[b, pl.ds(EDGE + r, EDGE), cols] = (
                    jnp.maximum(left, right) + jnp.log(1.0 + small)
                ).astype(BF16)
                part = 1.0 / (1.0 + small)
                share[at, cols] = jnp.where(away >= 0, part, small * part)
                return c

            chunks(half, pool)

    def send_edges(number, first, last, width):
        for b in range(B):
            for at, (head, tail) in enumerate(zip(first(b), last(b))):
                head, tail = head.astype(F32), tail.astype(F32)
                turned = flip[b] == 1
                place_at = at * B + b
                edges[number, 0, place_at, :, 0:width] = jnp.where(turned, head, tail).astype(BF16)
                edges[number, 1, place_at, :, 0:width] = jnp.where(turned, tail, head).astype(BF16)
        copies = pair(
            number + 1,
            edges.at[number, 0],
            edges.at[number, 1],
            edges_in.at[number, 0],
            edges_in.at[number, 1],
        )
        for copy in copies:
            copy.start()
        return copies

    def take_edges(number, at, b, width):
        from_prev = edges_in[number, 0, at * B + b, :, 0:width].astype(F32)
        from_next = edges_in[number, 1, at * B + b, :, 0:width].astype(F32)
        turned = flip[b] == 1
        before = jnp.where(turned, from_next, from_prev)
        after = jnp.where(turned, from_prev, from_next)
        before = jnp.where(block_at[b] > 0, before, 0.0)
        after = jnp.where(block_at[b] < nq - 1, after, 0.0)
        return before, after

    step = exchange(1)
    step.start(moments(lambda b, r: pooled[b, pl.ds(EDGE + r, EDGE)].astype(F32), half, C))
    ring = send_edges(
        0,
        lambda b: [pooled[b, EDGE : 2 * EDGE]],
        lambda b: [pooled[b, half : half + EDGE]],
        C,
    )
    second_norm = norms(step, half, gain2, bias2)
    for copy in ring:
        copy.wait()
    for b in range(B):
        before, after = take_edges(0, 0, b, C)
        pooled[b, 0:EDGE] = before.astype(BF16)
        pooled[b, EDGE + half : 2 * EDGE + half] = after.astype(BF16)
        norm = second_norm[b]

        def activate(r, c):
            value = flat(gelu(norm.pre(norm.normed(halves(pooled[b, pl.ds(r, EDGE)].astype(F32))))))
            at = lax.broadcasted_iota(jnp.int32, value.shape, 0) + (r - EDGE + block_at[b] * half)
            act[pl.ds(r, EDGE)] = jnp.where((at >= 0) & (at < nq * half), value, 0.0)
            return c

        chunks(half + 2 * EDGE, activate)

        def spread(r, c):
            values = act[pl.ds(r, 3 * EDGE)]
            for k in range(3):
                at = EDGE + (k - 1) * DILATION_SIZE
                second[pl.ds(b * half + r, EDGE), k * C : (k + 1) * C] = values[
                    at : at + EDGE
                ].astype(BF16)
            return c

        chunks(half, spread)

    load[2].wait()
    narrow[...] = jnp.dot(second[...], w2[...], preferred_element_type=F32)
    step = exchange(2)
    step.start(moments(lambda b, r: narrow[pl.ds(b * half + r, EDGE)], half, H))
    load[3].wait()
    load[4].wait()
    mirrored.wait()
    for b in range(B):

        def choose(r, c):
            at = pl.ds(r, EDGE)
            own_grad[b, at] = jnp.where(
                flip[b] == 1, far_grad[b, at].astype(F32), own_grad[b, at].astype(F32)
            ).astype(BF16)
            return c

        chunks(half, choose)
        third_in[b * half : (b + 1) * half] = lax.dot_general(
            own_grad[b], w3[...], NT, preferred_element_type=F32
        )
    third_norm = norms(step, half, gain3, bias3)

    none = jnp.zeros((8, H), F32)
    totals = []
    for b in range(B):
        norm = third_norm[b]

        def activate(r, carry):
            at = pl.ds(b * half + r, EDGE)
            normed = norm.normed(halves(narrow[at]))
            pre = norm.pre(normed)
            third[at] = flat(gelu(pre)).astype(BF16)
            grad = halves(third_in[at]) * gelu_slope(pre)
            third_in[at] = flat(grad)
            return carry[0] + jnp.sum(grad, axis=0), carry[1] + jnp.sum(grad * normed, axis=0)

        totals.append(chunks(half, activate, (none, none)))
    step = exchange(3)
    step.start([row_sum(t[0]) for t in totals] + [row_sum(t[1]) for t in totals])

    for b in range(B):
        at = slice(b * half, (b + 1) * half)
        for side in range(2):
            cols = slice(side * (C // 2), (side + 1) * (C // 2))
            ours[side, b] = (
                pooled[b, EDGE : EDGE + half, cols].astype(F32)
                + jnp.dot(third[at], w3[:, cols], preferred_element_type=F32)
            ).astype(BF16)
    step.relay(join_sums)
    away = [
        remote(
            ours.at[side],
            far.at[mine],
            result_send.at[i],
            result_recv.at[i],
            (side, place.d, place.mirror),
        )
        for i, side in enumerate((s, 1 - s))
    ]
    across = remote(
        ours.at[1 - s], near.at[mine], result_send.at[2], result_recv.at[2], place.partner
    )
    conv3_grad[...] = sum(
        lax.dot_general(
            third[b * half : (b + 1) * half], own_grad[b], TN, preferred_element_type=F32
        )
        for b in range(B)
    ).astype(BF16)
    back = step.finish(join_sums)
    for copy in away + [across]:
        copy.start()
    save.append(pltpu.make_async_copy(conv3_grad, conv3_out, local_sem.at[7]))
    save[2].start()
    sums[4:5, 0:H] = sum(back[B:])
    sums[5:6, 0:H] = sum(back[:B])
    scale = 1.0 / (half * nd * nq)
    for b in range(B):
        norm = third_norm[b]
        mean_bias, mean_gain = eight(back[b] * scale), eight(back[B + b] * scale)
        factor = norm.gain * norm.inv

        def input_grad(r, c):
            at = pl.ds(b * half + r, EDGE)
            normed = norm.normed(halves(narrow[at]))
            value = factor[None] * (halves(third_in[at]) - mean_bias[None] - normed * mean_gain[None])
            narrow_grad[b, pl.ds(EDGE + r, EDGE)] = flat(value).astype(BF16)
            return c

        chunks(half, input_grad)
    ring = send_edges(
        1,
        lambda b: [narrow_grad[b, EDGE : 2 * EDGE]],
        lambda b: [narrow_grad[b, half : half + EDGE]],
        H,
    )
    for k in range(3):
        conv2_grad[k * C : (k + 1) * C] = sum(
            lax.dot_general(
                second[b * half : (b + 1) * half, k * C : (k + 1) * C],
                narrow_grad[b, EDGE : EDGE + half],
                TN,
                preferred_element_type=F32,
            )
            for b in range(B)
        ).astype(BF16)
    save.append(pltpu.make_async_copy(conv2_grad, conv2_out, local_sem.at[8]))
    save[3].start()
    for copy in ring:
        copy.wait()
    for b in range(B):
        before, after = take_edges(1, 0, b, H)
        narrow_grad[b, 0:EDGE] = before.astype(BF16)
        narrow_grad[b, EDGE + half : 2 * EDGE + half] = after.astype(BF16)

        def spread(r, c):
            values = narrow_grad[b, pl.ds(r, 3 * EDGE)].astype(F32)
            for k in range(3):
                at = EDGE - (k - 1) * DILATION_SIZE
                narrow_taps[pl.ds(b * half + r, EDGE), k * H : (k + 1) * H] = values[
                    at : at + EDGE
                ].astype(BF16)
            return c

        chunks(half, spread)
    second_grad[...] = sum(
        lax.dot_general(
            narrow_taps[:, k * H : (k + 1) * H],
            w2[k * C : (k + 1) * C],
            NT,
            preferred_element_type=F32,
        )
        for k in range(3)
    )
    totals = []
    for b in range(B):
        norm = second_norm[b]

        def slope(r, carry):
            at = pl.ds(b * half + r, EDGE)
            normed = norm.normed(halves(pooled[b, pl.ds(EDGE + r, EDGE)].astype(F32)))
            grad = halves(second_grad[at]) * gelu_slope(norm.pre(normed))
            second_grad[at] = flat(grad)
            return carry[0] + jnp.sum(grad, axis=0), carry[1] + jnp.sum(grad * normed, axis=0)

        totals.append(chunks(half, slope, (zero, zero)))
    step = exchange(4)
    step.start([row_sum(t[0]) for t in totals] + [row_sum(t[1]) for t in totals])
    step.relay(join_sums)
    back = step.finish(join_sums)
    sums[2:3, :] = sum(back[B:])
    sums[3:4, :] = sum(back[:B])
    for b in range(B):
        norm = second_norm[b]
        mean_bias, mean_gain = eight(back[b] * scale), eight(back[B + b] * scale)
        factor = norm.gain * norm.inv

        def unpool(r, c):
            at = pl.ds(b * half + r, EDGE)
            normed = norm.normed(halves(pooled[b, pl.ds(EDGE + r, EDGE)].astype(F32)))
            value = factor[None] * (
                halves(second_grad[at]) - mean_bias[None] - normed * mean_gain[None]
            )
            value = flat(value) + own_grad[b, pl.ds(r, EDGE)].astype(F32)
            value = value.astype(BF16).astype(F32)
            part = share[at]
            wide_grad[0, at] = (value * part).astype(BF16)
            wide_grad[1, at] = (value * (1.0 - part)).astype(BF16)
            return c

        chunks(half, unpool)
    ring = send_edges(
        2,
        lambda b: [wide_grad[p, b * half : b * half + EDGE] for p in range(2)],
        lambda b: [wide_grad[p, (b + 1) * half - EDGE : (b + 1) * half] for p in range(2)],
        C,
    )
    save.append(pltpu.make_async_copy(wide_grad, grad_out, local_sem.at[9]))
    save[4].start()
    for copy in away + [across]:
        copy.wait()
    for b in range(B):
        near[s * B + b] = ours[s, b]
    for b in range(2 * B):
        turned = flips[b]

        def deliver(r, c):
            at = pl.ds(r, EDGE)
            near[b, at] = jnp.where(
                turned == 1, far[b, at].astype(F32), near[b, at].astype(F32)
            ).astype(BF16)
            return c

        chunks(half, deliver)
    save.append(pltpu.make_async_copy(near, result_out, local_sem.at[10]))
    save[5].start()
    for copy in ring:
        copy.wait()
    for b in range(B):
        for parity in range(2):
            before, after = take_edges(2, parity, b, C)
            halo[0, parity, b] = before.astype(BF16)
            halo[1, parity, b] = after.astype(BF16)
    save += [
        pltpu.make_async_copy(halo, halo_out, local_sem.at[11]),
        pltpu.make_async_copy(stats, stats_out, local_sem.at[12]),
        pltpu.make_async_copy(sums, sums_out, local_sem.at[13]),
    ]
    for copy in save[6:]:
        copy.start()
    for copy in save:
        copy.wait()


def weight_kernel(even, odd, even_grad, odd_grad, out):
    out[...] = (
        lax.dot_general(even[...], even_grad[0], TN, preferred_element_type=F32)
        + lax.dot_general(odd[...], odd_grad[0], TN, preferred_element_type=F32)
    ).astype(BF16)


def last_kernel(
    dims,
    placed_in,
    grad_in,
    halo_in,
    stats,
    sums_in,
    shifts,
    flips,
    gain1,
    bias1,
    weight1,
    out,
    sums_out,
    placed,
    grads,
    halo,
    w1,
    taps,
    act_grad,
    edges,
    edges_in,
    window,
    ours,
    final,
    sums,
    plane_buf,
    line_buf,
    local_sem,
    exchange_send,
    exchange_recv,
    halo_send,
    halo_recv,
    core_send,
    core_recv,
):
    C, H, L, B, nd, nq = dims
    half = L // 2
    place = Place(nd, nq)
    s, q = place.s, place.q
    place.greet(place.plane() + place.line() + [place.partner])
    flip = [flips[s * B + b] for b in range(B)]
    shift = [shifts[s * B + b] for b in range(B)]
    load = [
        pltpu.make_async_copy(grad_in, grads, local_sem.at[0]),
        pltpu.make_async_copy(halo_in, halo, local_sem.at[1]),
        pltpu.make_async_copy(weight1, w1, local_sem.at[2]),
        pltpu.make_async_copy(placed_in, placed, local_sem.at[3]),
    ]
    for copy in load:
        copy.start()
    load[0].wait()
    load[1].wait()
    for b in range(B):
        for parity in range(2):
            base = (1 - parity) * C

            def put(r, values):
                for at in range(3):
                    lanes = base + 2 * at * C
                    taps[pl.ds(b * half + r, EDGE), lanes : lanes + C] = values[
                        EDGE + 1 - at : 2 * EDGE + 1 - at
                    ].astype(BF16)

            def spread(r, c):
                put(r, grads[parity, pl.ds(b * half + r - EDGE, 3 * EDGE)].astype(F32))
                return c

            lax.fori_loop(
                1, half // EDGE - 1, lambda i, c: spread(pl.multiple_of(i * EDGE, EDGE), c), 0
            )
            low, high = b * half, (b + 1) * half
            put(
                0,
                jnp.concatenate(
                    [halo[0, parity, b], grads[parity, low : low + 2 * EDGE]], axis=0
                ).astype(F32),
            )
            put(
                half - EDGE,
                jnp.concatenate(
                    [grads[parity, high - 2 * EDGE : high], halo[1, parity, b]], axis=0
                ).astype(F32),
            )
    load[2].wait()
    load[3].wait()
    for parity in range(2):

        def convolve(j, c):
            cols = pl.multiple_of(j * 256, 256)
            total = None
            for k in range(5):
                lanes = (k + 1 - parity) * C
                part = lax.dot_general(
                    taps[:, lanes : lanes + C],
                    w1[k, pl.ds(cols, 256), :],
                    NT,
                    preferred_element_type=F32,
                )
                total = part if total is None else total + part
            act_grad[parity, :, pl.ds(cols, 256)] = total
            return c

        lax.fori_loop(0, C // 256, convolve, 0)
    norms = [
        Norm(stats[b : b + 1, :], stats[B + b : B + b + 1, :], gain1[...], bias1[...])
        for b in range(B)
    ]
    zero = jnp.zeros((8, C), F32)
    totals = []
    for b in range(B):
        norm = norms[b]
        carry = (zero, zero)
        for parity in range(2):

            def slope(r, carry):
                at = pl.ds(b * half + r, EDGE)
                values = placed[b, parity, pl.ds(r, 2 * EDGE)].astype(F32)[8 : 8 + EDGE]
                normed = norm.normed(halves(values))
                grad = halves(act_grad[parity, at]) * gelu_slope(norm.pre(normed))
                act_grad[parity, at] = flat(grad)
                return carry[0] + jnp.sum(grad, axis=0), carry[1] + jnp.sum(grad * normed, axis=0)

            carry = chunks(half, slope, carry)
        totals.append(carry)
    step = Exchange(place, 0, plane_buf, line_buf, exchange_send, exchange_recv)
    step.start([row_sum(t[0]) for t in totals] + [row_sum(t[1]) for t in totals])
    step.relay(join_sums)
    back = step.finish(join_sums)
    sums[0] = sums_in[...]
    sums[0, 0:1, :] = sum(back[B:])
    sums[0, 1:2, :] = sum(back[:B])
    swap = remote(sums.at[0], sums.at[1], core_send.at[0], core_recv.at[0], place.partner)
    swap.start()
    scale = 1.0 / (L * nd * nq)
    for b in range(B):
        norm = norms[b]
        mean_bias, mean_gain = eight(back[b] * scale), eight(back[B + b] * scale)
        factor = norm.gain * norm.inv
        for parity in range(2):

            def input_grad(r, c):
                values = placed[b, parity, pl.ds(r, 2 * EDGE)].astype(F32)[8 : 8 + EDGE]
                normed = norm.normed(halves(values))
                value = factor[None] * (
                    halves(act_grad[parity, pl.ds(b * half + r, EDGE)])
                    - mean_bias[None]
                    - normed * mean_gain[None]
                )
                window[b, pl.ds(parity * (half + 2 * EDGE) + EDGE + r, EDGE)] = flat(value).astype(
                    BF16
                )
                return c

            chunks(half, input_grad)
    for b in range(B):
        turned = flip[b] == 1
        for parity in range(2):
            low = parity * (half + 2 * EDGE)
            head = window[b, low + EDGE : low + 2 * EDGE].astype(F32)
            tail = window[b, low + half : low + half + EDGE].astype(F32)
            edges[0, parity, b] = jnp.where(turned, head, tail).astype(BF16)
            edges[1, parity, b] = jnp.where(turned, tail, head).astype(BF16)
    ring = [
        remote(
            edges.at[i],
            edges_in.at[i],
            halo_send.at[i],
            halo_recv.at[i],
            (s, place.d, at),
        )
        for i, at in enumerate((place.next, place.prev))
    ]
    for copy in ring:
        copy.start()
    for copy in ring:
        copy.wait()
    for b in range(B):
        turned = flip[b] == 1
        for parity in range(2):
            low = parity * (half + 2 * EDGE)
            from_prev = edges_in[0, parity, b].astype(F32)
            from_next = edges_in[1, parity, b].astype(F32)
            window[b, low : low + EDGE] = jnp.where(turned, from_next, from_prev).astype(BF16)
            window[b, low + EDGE + half : low + 2 * EDGE + half] = jnp.where(
                turned, from_prev, from_next
            ).astype(BF16)
        shape = (L, 2 * (half + 2 * EDGE))
        at = lax.broadcasted_iota(jnp.int32, shape, 0) + shift[b]
        at = flip[b] * (L - 1) + (1 - 2 * flip[b]) * at
        source = (at & 1) * (half + 2 * EDGE) + (at >> 1) + EDGE
        pick = jnp.where(lax.broadcasted_iota(jnp.int32, shape, 1) == source, 1.0, 0.0).astype(BF16)
        for side in range(2):
            cols = slice(side * (C // 2), (side + 1) * (C // 2))
            ours[side, b] = jnp.dot(pick, window[b, :, cols], preferred_element_type=F32).astype(
                BF16
            )
    across = remote(
        ours.at[1 - s],
        final.at[pl.ds(s * B, B)],
        core_send.at[1],
        core_recv.at[1],
        place.partner,
    )
    across.start()
    keep = pltpu.make_async_copy(ours.at[s], out.at[pl.ds(s * B, B)], local_sem.at[4])
    keep.start()
    swap.wait()
    sums_out[...] = sums[0] + sums[1]
    across.wait()
    other = pl.ds((1 - s) * B, B)
    give = pltpu.make_async_copy(final.at[other], out.at[other], local_sem.at[5])
    give.start()
    keep.wait()
    give.wait()


def on_device(
    nd,
    nq,
    inputs,
    shifts,
    flips,
    gain1,
    bias1,
    weight1,
    gain2,
    bias2,
    weight2,
    gain3,
    bias3,
    weight3,
    out_grad,
):
    sequences, L, C = inputs.shape
    H = weight3.shape[0]
    B, half = sequences // 2, L // 2
    rows = B * half
    dims = (C, H, L, B, nd, nq)
    anywhere = pl.BlockSpec(memory_space=pl.ANY)
    vmem = pl.BlockSpec(memory_space=pltpu.VMEM)
    smem = pl.BlockSpec(memory_space=pltpu.SMEM)
    peers = nd - 1 + nq - 1
    shape = jax.ShapeDtypeStruct
    dma = pltpu.SemaphoreType.DMA
    gain1, bias1, gain2, bias2, gain3, bias3 = (
        v.reshape(1, -1) for v in (gain1, bias1, gain2, bias2, gain3, bias3)
    )
    taps, placed, grads, halo, stats, sums, result, conv2, conv3 = pl.pallas_call(
        functools.partial(first_kernel, dims),
        name="forward_and_back",
        out_shape=(
            shape((rows, 6 * C), BF16),
            shape((B, 2, half + EDGE, C), BF16),
            shape((2, rows, C), BF16),
            shape((2, 2, B, EDGE, C), BF16),
            shape((8, C), F32),
            shape((8, C), F32),
            shape((2 * B, half, C // 2), BF16),
            shape((3 * C, H), BF16),
            shape((H, C), BF16),
        ),
        in_specs=[
            anywhere,
            anywhere,
            smem,
            smem,
            vmem,
            vmem,
            anywhere,
            vmem,
            vmem,
            anywhere,
            vmem,
            vmem,
            anywhere,
        ],
        out_specs=[anywhere] * 9,
        scratch_shapes=[
            pltpu.VMEM((B, L + 2 * EDGE, C), BF16),
            pltpu.VMEM((B, 2, half + EDGE, C), BF16),
            pltpu.VMEM((half + 2 * EDGE, C), F32),
            pltpu.VMEM((rows, 6 * C), BF16),
            pltpu.VMEM((5 * C, C), BF16),
            pltpu.VMEM((3 * C, H), BF16),
            pltpu.VMEM((H, C), BF16),
            pltpu.VMEM((rows, C // 3), F32),
            pltpu.VMEM((rows, C // 3), F32),
            pltpu.VMEM((rows, C), F32),
            pltpu.VMEM((B, half + 2 * EDGE, C), BF16),
            pltpu.VMEM((3, 2, 2 * B, EDGE, C), BF16),
            pltpu.VMEM((3, 2, 2 * B, EDGE, C), BF16),
            pltpu.VMEM((rows, 3 * C), BF16),
            pltpu.VMEM((rows, H), F32),
            pltpu.VMEM((B, half, C), BF16),
            pltpu.VMEM((B, half, C), BF16),
            pltpu.VMEM((rows, H), F32),
            pltpu.VMEM((rows, H), BF16),
            pltpu.VMEM((B, half + 2 * EDGE, H), BF16),
            pltpu.VMEM((rows, 3 * H), BF16),
            pltpu.VMEM((rows, C), F32),
            pltpu.VMEM((3 * C, H), BF16),
            pltpu.VMEM((H, C), BF16),
            pltpu.VMEM((2, rows, C), BF16),
            pltpu.VMEM((2, 2, B, EDGE, C), BF16),
            pltpu.VMEM((2, B, half, C // 2), BF16),
            pltpu.VMEM((2 * B, half, C // 2), BF16),
            pltpu.VMEM((2 * B, half, C // 2), BF16),
            pltpu.VMEM((8, C), F32),
            pltpu.VMEM((8, C), F32),
            pltpu.VMEM((5, nd, 8, C), F32),
            pltpu.VMEM((5, nq, 8, C), F32),
            dma((14,)),
            dma((5, peers)),
            dma((5, peers)),
            dma((4, 2)),
            dma((4, 2)),
            dma((1,)),
            dma((1,)),
            dma((3,)),
            dma((3,)),
        ],
        compiler_params=pltpu.CompilerParams(
            collective_id=0, has_side_effects=True, vmem_limit_bytes=58 * 2**20
        ),
    )(
        inputs,
        out_grad,
        shifts,
        flips,
        gain1,
        bias1,
        weight1.reshape(5 * C, C),
        gain2,
        bias2,
        weight2.reshape(3 * C, H),
        gain3,
        bias3,
        weight3,
    )
    axes = ("section", "dp", "seq")
    conv2, conv3 = lax.psum((conv2, conv3), axes)
    conv1 = pl.pallas_call(
        weight_kernel,
        name="first_weight_gradient",
        grid=(5,),
        out_shape=shape((5 * C, C), BF16),
        in_specs=[
            pl.BlockSpec((rows, C), lambda k: (0, k)),
            pl.BlockSpec((rows, C), lambda k: (0, k + 1)),
            pl.BlockSpec((1, rows, C), lambda k: (0, 0, 0)),
            pl.BlockSpec((1, rows, C), lambda k: (1, 0, 0)),
        ],
        out_specs=pl.BlockSpec((C, C), lambda k: (k, 0)),
        compiler_params=pltpu.CompilerParams(vmem_limit_bytes=32 * 2**20),
        cost_estimate=pl.CostEstimate(
            flops=20 * rows * C * C, bytes_accessed=30 * C * C, transcendentals=0
        ),
    )(taps, taps, grads, grads)
    conv1 = lax.psum(conv1, axes)
    back, sums = pl.pallas_call(
        functools.partial(last_kernel, dims),
        name="first_input_gradient",
        out_shape=(shape((2 * B, L, C // 2), BF16), shape((8, C), F32)),
        in_specs=[
            anywhere,
            anywhere,
            anywhere,
            vmem,
            vmem,
            smem,
            smem,
            vmem,
            vmem,
            anywhere,
        ],
        out_specs=[anywhere, vmem],
        scratch_shapes=[
            pltpu.VMEM((B, 2, half + EDGE, C), BF16),
            pltpu.VMEM((2, rows, C), BF16),
            pltpu.VMEM((2, 2, B, EDGE, C), BF16),
            pltpu.VMEM((5, C, C), BF16),
            pltpu.VMEM((rows, 6 * C), BF16),
            pltpu.VMEM((2, rows, C), F32),
            pltpu.VMEM((2, 2, B, EDGE, C), BF16),
            pltpu.VMEM((2, 2, B, EDGE, C), BF16),
            pltpu.VMEM((B, 2 * (half + 2 * EDGE), C), BF16),
            pltpu.VMEM((2, B, L, C // 2), BF16),
            pltpu.VMEM((2 * B, L, C // 2), BF16),
            pltpu.VMEM((2, 8, C), F32),
            pltpu.VMEM((1, nd, 8, C), F32),
            pltpu.VMEM((1, nq, 8, C), F32),
            dma((6,)),
            dma((1, peers)),
            dma((1, peers)),
            dma((2,)),
            dma((2,)),
            dma((2,)),
            dma((2,)),
        ],
        compiler_params=pltpu.CompilerParams(
            collective_id=1, has_side_effects=True, vmem_limit_bytes=48 * 2**20
        ),
        cost_estimate=pl.CostEstimate(
            flops=20 * rows * C * C, bytes_accessed=30 * C * C, transcendentals=0
        ),
    )(placed, grads, halo, stats, sums, shifts, flips, gain1, bias1, weight1)
    return (
        result,
        back,
        conv1.reshape(5, C, C).astype(F32),
        sums[0],
        sums[1],
        conv2.reshape(3, C, H).astype(F32),
        sums[2],
        sums[3],
        conv3.astype(F32),
        sums[4, :H],
        sums[5, :H],
    )


def solution(mesh):
    whole = P()
    split = P("dp", "seq", None)
    return jax.shard_map(
        functools.partial(on_device, mesh.shape["dp"], mesh.shape["seq"]),
        mesh=mesh,
        in_specs=(split, P("dp"), P("dp")) + (whole,) * 9 + (split,),
        out_specs=(P("dp", "seq", "section"),) * 2 + (whole,) * 9,
        check_vma=False,
    )
```

time: 2320 us -> 368 us (0.16)
  blocking collectives: 985 us -> 0 us
  starting transfers between devices: 392 us -> 0.04 us
  waiting for transfers between devices: 409 us -> 140 us
  matrix products: 197 us -> 0 us
  Pallas kernels: 0 us -> 180 us
  local copies, waits for them, and re-layouts: 171 us -> 20.3 us
  other arithmetic: 119 us -> 11.5 us
    psum x28 -> x0, blocking collectives: 985 us -> none  [the longest x9 374 us: norm_back(): bias_total, gain_total = lax.psum((bias_part, gain_part), ('dp', 'seq'))]
    ppermute x71 -> x0, starting transfers between devices: 391 us -> none  [the longest x21 242 us: from_partner(): return lax.ppermute(block, axis, route)]
    ppermute x71 -> x0, waiting for transfers between devices: 311 us -> none  [the longest x21 305 us: from_partner(): return lax.ppermute(block, axis, route)]
    dot_general x108 -> x0, matrix products: 197 us -> none  [the longest x32 71.2 us: kernel_taps_input_gradient(): jnp.einsum('slo,co->slc', grad_padded[:, start_bin:start_bin + extent], w...]
    pallas_call x0 -> x3, Pallas kernels: none -> 180 us  [the longest x1 125 us: on_device(): pl.pallas_call(functools.partial(first_kernel, dims), name='forward_and_b...]
    rev x8 -> x0, local copies, waits for them, and re-layouts: 82.6 us -> none  [mirror(): return jnp.flip(arrived, axis=1)]
    psum x1, waiting for transfers between devices: 98.1 us -> 140 us  [on_device(): conv1 = lax.psum(conv1, axes)]
    select_n x22 -> x0, other arithmetic: 34.9 us -> none  [the longest x19 28.1 us: on_device(): jnp.where(is_first, left, right)]
  transfers between devices with their start and end apart: 72 -> 1, of which waited for: 20 -> 1; matrix products, arithmetic and copies ran while one was open for 10% -> 0% of each run, Pallas kernels for 0% -> 13%
where the time goes in v1:
time: 368 us; the launch traced here: 366 us
  Pallas kernels  180 us (49%)
  waiting for transfers between devices  140 us (38%)
  local copies, waits for them, and re-layouts  20.3 us (6%)
  between operations  14.1 us (4%)
  other arithmetic  11.5 us (3%)
    psum x1, waiting for transfers between devices, on_device(): conv1 = lax.psum(conv1, axes)  140 us
    pallas_call x1, Pallas kernels, on_device(): pl.pallas_call(functools.partial(first_kernel, dims), name='forward_and_b...  125 us
    pallas_call x1, Pallas kernels, on_device(): pl.pallas_call(functools.partial(last_kernel, dims), name='first_input_gr...  46.9 us
    unnamed x32, local copies, waits for them, and re-layouts  11.6 us
    convert_element_type x1, other arithmetic, on_device(): conv1.reshape(5, C, C).astype(F32)  8.42 us
    pallas_call x1, Pallas kernels, on_device(): pl.pallas_call(weight_kernel, name='first_weight_gradient', grid=(5,), ou...  7.67 us
    reshape x6, local copies, waits for them, and re-layouts, on_device(): v.reshape(1, -1)  7.56 us
  transfers between devices with their start and end apart: 1, of which 1 were waited for; matrix products, arithmetic and copies ran while one was open for 0% of the time, Pallas kernels for 13%

profile of v1, /device:TPU:9, one launch (start us, length us, event | category | flops | bytes accessed | tf_op | source)
XLA Modules:
  0.0 365.9 jit_solution(16559862817071089550)
XLA Ops:
  7.2 1.3 reshape.52.gain1
  8.5 1.3 reshape.53.bias1
  9.8 1.3 reshape.55.gain2
  11.0 1.3 reshape.56.bias2
  12.3 1.2 reshape.58.gain3
  13.5 1.2 reshape.59.bias3
  14.8 125.3 %forward_and_back.1 = (bf16[512,4608]{1,0:T(8,128)(2,1)}, bf16[2,2,272,768]{3,2,1,0:T(8,128)(2,1)}, bf16[2,512,768]{2,1,0:T(8,128)(2,1)}, bf16[2,2,2,16,768]{4,3...) custom-call(bf16[4,512,768]{2,1,0:T(8,128)(2,1)} %inputs.1, ...), custom_call_target="tpu_custom_call" | custom-call | tf_op jit(solution)/shard_map/forward_and_back/pallas_call | solution.py:922
  140.1 2.3 copy-done.5
  142.5 1.4 copy-done.7
  143.9 7.7 %first_weight_gradient.1 = bf16[3840,768]{1,0:T(8,128)(2,1)S(1)} custom-call(bf16[512,4608]{1,0:T(8,128)(2,1)S(1)} %copy-done.5, bf16[512,4608]{1,0:T(8,128)(2,1)S(1)} %copy-done.5, bf16[2,512,768]{2,1,0:T(8,128)(2,1)S(1)} %copy-done.7, bf16[2,512,768]{2,1,0:T(8,128)(2,1)S(1)} %copy-done.7), custom_call_target="tpu_custom_call" | custom-call | flops 6039797760 | bytes 17694720 | tf_op jit(solution)/shard_map/first_weight_gradient/pallas_call | solution.py:1016
  151.6 2.6 copy-done
  154.2 0.6 copy-done.1
  154.8 0.8 copy-done.6
  155.6 1.4 copy-done.8
  157.0 46.9 %first_input_gradient.1 = (bf16[4,512,384]{2,1,0:T(8,128)(2,1)S(1)}, f32[8,768]{1,0:T(8,128)S(1)}) custom-call(bf16[2,2,272,768]{3,2,1,0:T(8,128)(2,1)S(1)} %copy-done.6, bf16[2,512,768]{2,1,0:T(8,128)(2,1)S(1)} %copy-done.8, bf16[2,2,2,16,768]{4,3,2,1,0:T(8,128)(2,1)S(1)} %copy-done.9, f32[8,768]{1,0:T(8,128)S(1)} %copy-done.10, f32[8,768]{1,0:T(8,128)S(1)} %copy-done.11, ...), custom_call_target="tpu_custom_call" | custom-call | flops 6039797760 | bytes 17694720 | tf_op jit(solution)/shard_map/first_input_gradient/pallas_call | solution.py:1034
  203.9 0.6 slice_reduce_fusion.4
  204.5 0.6 slice_reduce_fusion
  205.2 140.0 %all-reduce.3.cloned.1.call-done = (bf16[5,768,768]{2,1,0:T(8,128)(2,1)}, bf16[3,768,384]{2,1,0:T(8,128)(2,1)}, bf16[384,768]{1,0:T(8,128)(2,1)}) async-done(((bf16[5,768,768]{2,1,0:T(8,128)(2,1)}, bf16[3,768,384]{2,1,0:T(8,128)(2,1)}, bf16[384,768]{1,0:T(8,128)(2,1)}), (bf16[5,768,768]{2,1,0:T(8,128)(2,1)}, bf16[3,768,384]{2,1,0:T(8,128)(2,1)}, bf16[384,768]{1,0:T(8,128)(2,1)})) %all-reduce.3.cloned.1.call-update) | async-done | bytes 8257552 | tf_op jit(solution)/shard_map/psum | solution.py:1033
  345.1 8.4 %convert_element_type.16 = f32[5,768,768]{2,1,0:T(8,128)} convert(bf16[5,768,768]{2,1,0:T(8,128)(2,1)} %get-tuple-element.39) | non-fusion elementwise | flops 2949120 | bytes 17694720 | tf_op jit(solution)/shard_map/convert_element_type | solution.py:1084
  353.6 2.0 convert_element_type.18
  355.6 1.1 convert_element_type.19
  356.7 0.4 copy-done.13
  357.1 0.9 copy.29
  357.9 1.1 copy.30
  (25 shorter events, 0.1 us)
Async XLA Ops:
  7.2 338.0 %all-reduce.3.cloned.1.call-start = ((), (), s32[]{:S(2)}) async-start(), calls=%async_computation | async-start | bytes 16515072 | tf_op jit(solution)/shard_map/psum | solution.py:1033
  140.1 2.3 copy-start.5
  142.5 1.4 copy-start.7
  151.5 2.6 copy-start
  154.1 0.7 copy-start.1
  154.1 0.7 copy-start.2
  154.1 0.7 copy-start.3
  154.1 0.7 copy-start.4
  154.1 1.5 copy-start.6
  154.1 1.5 copy-start.9
  154.1 1.5 copy-start.10
  154.2 1.5 copy-start.11
  155.6 1.4 copy-start.8
  345.1 8.4 %copy-start.12 = (bf16[3,768,384]{2,1,0:T(8,128)(2,1)S(1)}, bf16[3,768,384]{2,1,0:T(8,128)(2,1)}, u32[]{:S(2)}) copy-start(bf16[3,768,384]{2,1,0:T(8,128)(2,1)} %get-tuple-element.40) | copy-start | bytes 5308420
  353.6 2.0 copy-start.14
  355.6 1.5 copy-start.13
Sparse Core Ops, SparseCore 0:
  154.3 190.7 all-reduce.2

commit v2 on v1

--- a/solution.py
+++ b/solution.py
@@ -182,8 +182,8 @@
     stats_out,
     sums_out,
     result_out,
-    conv2_out,
-    conv3_out,
+    own_out,
+    other_out,
     window,
     placed,
     act,
@@ -206,13 +206,11 @@
     narrow_grad,
     narrow_taps,
     second_grad,
-    conv2_grad,
-    conv3_grad,
+    block_grad,
+    block_send,
     wide_grad,
     halo,
     ours,
-    near,
-    far,
     stats,
     sums,
     plane_buf,
@@ -224,16 +222,12 @@
     halo_recv,
     far_send,
     far_recv,
-    result_send,
-    result_recv,
 ):
     C, H, L, B, nd, nq = dims
     half = L // 2
-    rows = B * half
     place = Place(nd, nq)
     s, q = place.s, place.q
-    cross = (1 - s, place.d, place.mirror)
-    place.greet(place.plane() + place.line() + [place.partner, cross])
+    place.greet(place.plane() + place.line())
 
     flip = [flips[s * B + b] for b in range(B)]
     shift = [shifts[s * B + b] for b in range(B)]
@@ -499,31 +493,24 @@
                 pooled[b, EDGE : EDGE + half, cols].astype(F32)
                 + jnp.dot(third[at], w3[:, cols], preferred_element_type=F32)
             ).astype(BF16)
+    save.append(pltpu.make_async_copy(ours, result_out, local_sem.at[7]))
+    save[2].start()
     step.relay(join_sums)
-    away = [
-        remote(
-            ours.at[side],
-            far.at[mine],
-            result_send.at[i],
-            result_recv.at[i],
-            (side, place.d, place.mirror),
-        )
-        for i, side in enumerate((s, 1 - s))
-    ]
-    across = remote(
-        ours.at[1 - s], near.at[mine], result_send.at[2], result_recv.at[2], place.partner
-    )
-    conv3_grad[...] = sum(
+    width = C // 2
+
+    def keep(first, value):
+        block_grad[first : first + value.shape[0]] = value
+        block_send[first : first + value.shape[0]] = value.astype(BF16)
+
+    value = sum(
         lax.dot_general(
             third[b * half : (b + 1) * half], own_grad[b], TN, preferred_element_type=F32
         )
         for b in range(B)
-    ).astype(BF16)
+    )
+    keep(3 * C, value[:, 0:width])
+    keep(3 * C + H, value[:, width:])
     back = step.finish(join_sums)
-    for copy in away + [across]:
-        copy.start()
-    save.append(pltpu.make_async_copy(conv3_grad, conv3_out, local_sem.at[7]))
-    save[2].start()
     sums[4:5, 0:H] = sum(back[B:])
     sums[5:6, 0:H] = sum(back[:B])
     scale = 1.0 / (half * nd * nq)
@@ -547,17 +534,27 @@
         H,
     )
     for k in range(3):
-        conv2_grad[k * C : (k + 1) * C] = sum(
-            lax.dot_general(
-                second[b * half : (b + 1) * half, k * C : (k + 1) * C],
-                narrow_grad[b, EDGE : EDGE + half],
-                TN,
-                preferred_element_type=F32,
-            )
-            for b in range(B)
-        ).astype(BF16)
-    save.append(pltpu.make_async_copy(conv2_grad, conv2_out, local_sem.at[8]))
+        keep(
+            k * C,
+            sum(
+                lax.dot_general(
+                    second[b * half : (b + 1) * half, k * C : (k + 1) * C],
+                    narrow_grad[b, EDGE : EDGE + half],
+                    TN,
+                    preferred_element_type=F32,
+                )
+                for b in range(B)
+            ),
+        )
+    side = block_grad.shape[0] // 2
+    save += [
+        pltpu.make_async_copy(block_grad.at[pl.ds(s * side, side)], own_out, local_sem.at[8]),
+        pltpu.make_async_copy(
+            block_send.at[pl.ds((1 - s) * side, side)], other_out, local_sem.at[10]
+        ),
+    ]
     save[3].start()
+    save[4].start()
     for copy in ring:
         copy.wait()
     for b in range(B):
@@ -628,23 +625,6 @@
         C,
     )
     save.append(pltpu.make_async_copy(wide_grad, grad_out, local_sem.at[9]))
-    save[4].start()
-    for copy in away + [across]:
-        copy.wait()
-    for b in range(B):
-        near[s * B + b] = ours[s, b]
-    for b in range(2 * B):
-        turned = flips[b]
-
-        def deliver(r, c):
-            at = pl.ds(r, EDGE)
-            near[b, at] = jnp.where(
-                turned == 1, far[b, at].astype(F32), near[b, at].astype(F32)
-            ).astype(BF16)
-            return c
-
-        chunks(half, deliver)
-    save.append(pltpu.make_async_copy(near, result_out, local_sem.at[10]))
     save[5].start()
     for copy in ring:
         copy.wait()
@@ -664,18 +644,225 @@
         copy.wait()
 
 
-def weight_kernel(even, odd, even_grad, odd_grad, out):
-    out[...] = (
-        lax.dot_general(even[...], even_grad[0], TN, preferred_element_type=F32)
-        + lax.dot_general(odd[...], odd_grad[0], TN, preferred_element_type=F32)
-    ).astype(BF16)
-
-
-def last_kernel(
+class Cube:
+    def __init__(self, place, blocks, width, refs):
+        self.place, self.blocks, self.width = place, blocks, width
+        self.total, self.inbox, self.relayed, self.summed, self.out = refs[:5]
+        (
+            self.core_send,
+            self.core_recv,
+            self.down_send,
+            self.down_recv,
+            self.up_send,
+            self.up_recv,
+            self.share_send,
+            self.share_recv,
+            self.out_sem,
+        ) = refs[5:]
+        self.sources = [None] * blocks
+        self.axes = cube_axes(place)
+        self.flight = [None] * blocks
+        self.state = [None] * blocks
+
+    def order(self, block):
+        return [self.axes[i] for i in cube_order(block, len(self.axes))]
+
+    def events(self):
+        depth = len(self.axes)
+        return ["core"] + ["down"] * depth + ["up"] * halvings(depth) + ["share", "out"]
+
+    def _add(self, block, incoming, first, count, send):
+        total, inbox, width = self.total, self.inbox, self.width
+
+        def add(r, c):
+            at = pl.ds(pl.multiple_of(first + r, EDGE), EDGE)
+            value = total[block, at] + incoming(r).astype(F32)
+            total[block, at] = value
+            if send:
+                inbox[block, at] = value.astype(BF16)
+            return c
+
+        chunks(count, add)
+
+    def run(self, block, stage):
+        place, depth = self.place, len(self.axes)
+        s = place.s
+        last = depth + halvings(depth)
+        if self.flight[block] is not None:
+            self.flight[block].wait()
+        if stage == 0:
+            copy = remote(
+                self.sources[block],
+                self.inbox.at[block],
+                self.core_send.at[block],
+                self.core_recv.at[block],
+                place.partner,
+            )
+        elif stage <= depth:
+            k = stage - 1
+            partner, side = self.order(block)[k]
+            size, first, past = sizes(k), [0], None
+            if k > 0:
+                first, past = self.state[block]
+            offset = first[-1]
+            if k == 0:
+                incoming = lambda base: lambda r: self.inbox[
+                    block, pl.ds(pl.multiple_of(base + r, EDGE), EDGE)
+                ]
+                base_of = lambda at: at
+            else:
+                incoming = lambda base: lambda r: self.relayed[
+                    block, pl.ds(pl.multiple_of(base + r, EDGE), EDGE)
+                ]
+                base_of = lambda at: at - offset + region(k - 1)
+            if size >= 2 * EDGE:
+                small = size // 2
+                give, hold = offset + (1 - side) * small, offset + side * small
+                self._add(block, incoming(base_of(give)), give, small, True)
+            else:
+                small, give, hold = size, offset, offset
+                self._add(block, incoming(base_of(give)), give, small, True)
+                at = pl.ds(pl.multiple_of(give, EDGE), small)
+                self.total[block, at] = self.inbox[block, at].astype(F32)
+            copy = remote(
+                self.inbox.at[block, pl.ds(pl.multiple_of(give, EDGE), small)],
+                self.relayed.at[block, region(k) : region(k) + small],
+                self.down_send.at[block, k],
+                self.down_recv.at[block, k],
+                partner,
+            )
+            self.state[block] = (first + [hold], past)
+        elif stage <= last:
+            k = last - stage
+            first, _ = self.state[block]
+            partner, _ = self.order(block)[k]
+            hold, small = first[k + 1], sizes(k + 1)
+            at = pl.ds(pl.multiple_of(hold, EDGE), small)
+            if stage == depth + 1:
+                end = pl.ds(pl.multiple_of(first[-1], EDGE), sizes(depth))
+                begin = region(depth - 1)
+                self.summed[s, block, end] = (
+                    self.total[block, end]
+                    + self.relayed[block, begin : begin + sizes(depth)].astype(F32)
+                ).astype(BF16)
+            copy = remote(
+                self.summed.at[s, block, at],
+                self.summed.at[s, block, at],
+                self.up_send.at[block, k],
+                self.up_recv.at[block, k],
+                partner,
+            )
+        elif stage == last + 1:
+            copy = remote(
+                self.summed.at[s, block],
+                self.summed.at[s, block],
+                self.share_send.at[block],
+                self.share_recv.at[block],
+                place.partner,
+            )
+        else:
+            copy = pltpu.make_async_copy(
+                self.summed.at[:, block], self.out.at[:, block], self.out_sem.at[block]
+            )
+        if stage > 0 and stage <= depth:
+            copy.start()
+            if size >= 2 * EDGE:
+                self._add(block, incoming(base_of(hold)), hold, small, False)
+        else:
+            copy.start()
+        self.flight[block] = copy
+
+    def end(self):
+        for copy in self.flight:
+            copy.wait()
+
+
+BLOCK = 256
+
+
+def sizes(k):
+    return max(BLOCK >> k, EDGE)
+
+
+def region(k):
+    return sum(sizes(i + 1) for i in range(k))
+
+
+def halvings(depth):
+    return sum(sizes(k) >= 2 * EDGE for k in range(depth))
+
+
+def cube_axes(place):
+    axes = []
+    bit = 1
+    while bit < place.nd:
+        side = lax.rem(place.d // bit, 2)
+        axes.append(((place.s, place.d + bit * (1 - 2 * side), place.q), side))
+        bit *= 2
+    span = 2
+    while span <= place.nq:
+        low = lax.rem(place.q, span)
+        side = lax.rem(place.q // (span // 2) + place.q // span, 2)
+        axes.append(((place.s, place.d, place.q - low + span - 1 - low), side))
+        span *= 2
+    return axes
+
+
+def cube_order(block, depth):
+    others = [(block + i) % (depth - 1) for i in range(depth - 1)]
+    at = 1 if (block // (depth - 1)) % 2 else depth - 1
+    return others[:at] + [depth - 1] + others[at:]
+
+
+def plan(depth, blocks, pieces, events):
+    rate, wait, cost = 95e3, 1.6, 0.2
+    free = [0.0] * (depth + 1)
+    ready = {}
+    due = [(0, 0.0)] * 0
+    now, order = 0.0, []
+    pieces = list(pieces)
+    while pieces or ready:
+        able = sorted((t, b) for b, (t, _) in ready.items() if t <= now)
+        if able:
+            _, block = able[0]
+            _, stage = ready.pop(block)
+            order.append((block, stage))
+            kind = events[stage]
+            now += cost if kind == "down" else 0.05
+            if stage + 1 < len(events):
+                if kind in ("core", "share"):
+                    axis, size, speed = depth, 256, 4 * rate
+                elif kind == "down":
+                    k = stage - 1
+                    axis, size, speed = cube_order(block, depth)[k], sizes(k + 1), rate
+                elif kind == "up":
+                    k = depth + halvings(depth) - stage
+                    axis, size, speed = cube_order(block, depth)[k], sizes(k + 1), rate
+                begin = max(now, free[axis])
+                free[axis] = begin + 2 * size * 768 / speed
+                ready[block] = (free[axis] + wait, stage + 1)
+        elif pieces:
+            name, time, made, sends = pieces.pop(0)
+            order.append(name)
+            now += time
+            for block in made:
+                ready[block] = (now, 0)
+            for axis, size in sends:
+                free[axis] = max(now, free[axis]) + size / rate
+        else:
+            now = min(t for t, _ in ready.values())
+    return order
+
+
+def tail_kernel(
     dims,
+    taps_in,
     placed_in,
     grad_in,
     halo_in,
+    own_in,
+    other_in,
+    result_in,
     stats,
     sums_in,
     shifts,
@@ -683,8 +870,17 @@
     gain1,
     bias1,
     weight1,
-    out,
+    summed_out,
+    near_out,
+    far_out,
+    back_out,
     sums_out,
+    total,
+    inbox,
+    sending,
+    relayed,
+    summed,
+    product,
     placed,
     grads,
     halo,
@@ -706,85 +902,194 @@
     halo_recv,
     core_send,
     core_recv,
+    result_send,
+    result_recv,
+    *cube_sems,
 ):
     C, H, L, B, nd, nq = dims
     half = L // 2
+    width = C // 2
     place = Place(nd, nq)
     s, q = place.s, place.q
-    place.greet(place.plane() + place.line() + [place.partner])
+    cross = (1 - s, place.d, place.mirror)
+    mine = pl.ds(s * B, B)
+    first_blocks = own_in.shape[0] // BLOCK
+    per_tap = C // BLOCK
+    blocks = first_blocks + 5 * per_tap
+    cube = Cube(place, blocks, width, (total, inbox, relayed, summed, summed_out) + cube_sems)
+    depth = len(cube.axes)
+    greeted = place.plane() + place.line() + [place.partner, cross]
+    bit = 1
+    place.greet(greeted)
     flip = [flips[s * B + b] for b in range(B)]
     shift = [shifts[s * B + b] for b in range(B)]
     load = [
-        pltpu.make_async_copy(grad_in, grads, local_sem.at[0]),
-        pltpu.make_async_copy(halo_in, halo, local_sem.at[1]),
-        pltpu.make_async_copy(weight1, w1, local_sem.at[2]),
-        pltpu.make_async_copy(placed_in, placed, local_sem.at[3]),
+        pltpu.make_async_copy(
+            own_in.at[i * BLOCK : (i + 1) * BLOCK], total.at[i], local_sem.at[6 + i]
+        )
+        for i in range(first_blocks)
     ]
-    for copy in load:
+    load_taps = pltpu.make_async_copy(taps_in, taps, local_sem.at[0])
+    load_grads = pltpu.make_async_copy(grad_in, grads, local_sem.at[1])
+    load_rest = [
+        pltpu.make_async_copy(halo_in, halo, local_sem.at[2]),
+        pltpu.make_async_copy(weight1, w1, local_sem.at[3]),
+        pltpu.make_async_copy(placed_in, placed, local_sem.at[4]),
+    ]
+    for copy in [load_taps, load_grads] + load + load_rest:
         copy.start()
-    load[0].wait()
-    load[1].wait()
-    for b in range(B):
-        for parity in range(2):
-            base = (1 - parity) * C
-
-            def put(r, values):
-                for at in range(3):
-                    lanes = base + 2 * at * C
-                    taps[pl.ds(b * half + r, EDGE), lanes : lanes + C] = values[
-                        EDGE + 1 - at : 2 * EDGE + 1 - at
-                    ].astype(BF16)
-
-            def spread(r, c):
-                put(r, grads[parity, pl.ds(b * half + r - EDGE, 3 * EDGE)].astype(F32))
+    for i in range(first_blocks):
+        cube.sources[i] = other_in.at[i * BLOCK : (i + 1) * BLOCK]
+    for i in range(5 * per_tap):
+        cube.sources[first_blocks + i] = sending.at[i]
+    todo, pieces = {}, []
+
+    def piece(name, time, made=(), sends=()):
+        def keep(body):
+            todo[name] = body
+            pieces.append((name, time, made, sends))
+            return body
+
+        return keep
+
+    @piece("block gradients", 0.3, range(first_blocks))
+    def _():
+        for copy in load:
+            copy.wait()
+
+    across = remote(
+        result_in.at[1 - s], near_out.at[mine], result_send.at[0], result_recv.at[0], place.partner
+    )
+    keep_near = pltpu.make_async_copy(result_in.at[s], near_out.at[mine], local_sem.at[5])
+    away = [
+        remote(
+            result_in.at[side, b],
+            far_out.at[s * B + b],
+            result_send.at[1 + 2 * b + i],
+            result_recv.at[1 + 2 * b + i],
+            (side, place.d, place.mirror),
+        )
+        for b in range(B)
+        for i, side in enumerate((s, 1 - s))
+    ]
+    across.start()
+    keep_near.start()
+
+    def result_piece(i):
+        @piece(("result", i), 0.05, (), [(depth - 1, 2 * half * width * 2)])
+        def _():
+            away[i].start()
+
+    def weight_piece(k):
+        made = range(first_blocks + k * per_tap, first_blocks + (k + 1) * per_tap)
+
+        @piece(("weight", k), 1.9, made)
+        def _():
+            if k == 0:
+                load_taps.wait()
+                load_grads.wait()
+
+            def tile(m, c):
+                lanes = pl.multiple_of(k * C + m * BLOCK, BLOCK)
+                product[...] = lax.dot_general(
+                    taps[:, pl.ds(lanes, BLOCK)], grads[0], TN, preferred_element_type=F32
+                ) + lax.dot_general(
+                    taps[:, pl.ds(lanes + C, BLOCK)], grads[1], TN, preferred_element_type=F32
+                )
+
+                def split(r, c):
+                    at = pl.ds(r, EDGE)
+                    low = pl.ds(pl.multiple_of(s * width, width), width)
+                    high = pl.ds(pl.multiple_of((1 - s) * width, width), width)
+                    total[first_blocks + k * per_tap + m, at] = product[at, low]
+                    sending[k * per_tap + m, at] = product[at, high].astype(BF16)
+                    return c
+
+                chunks(BLOCK, split)
                 return c
 
-            lax.fori_loop(
-                1, half // EDGE - 1, lambda i, c: spread(pl.multiple_of(i * EDGE, EDGE), c), 0
-            )
+            lax.fori_loop(0, per_tap, tile, 0)
+
+    for k in range(5):
+        if k < 2 * B:
+            result_piece(k)
+        weight_piece(k)
+
+    def put(b, parity, r, values):
+        base = (1 - parity) * C
+        for at in range(3):
+            lanes = base + 2 * at * C
+            taps[pl.ds(b * half + r, EDGE), lanes : lanes + C] = values[
+                EDGE + 1 - at : 2 * EDGE + 1 - at
+            ].astype(BF16)
+
+    def spread_piece(b, parity):
+        @piece(("spread", b, parity), 0.6)
+        def _():
+            if b == 0 and parity == 0:
+                load_rest[0].wait()
+
+            def spread(i, c):
+                r = pl.multiple_of(i * EDGE, EDGE)
+                values = grads[parity, pl.ds(b * half + r - EDGE, 3 * EDGE)].astype(F32)
+                put(b, parity, r, values)
+                return c
+
+            lax.fori_loop(1, half // EDGE - 1, spread, 0)
             low, high = b * half, (b + 1) * half
             put(
+                b,
+                parity,
                 0,
                 jnp.concatenate(
                     [halo[0, parity, b], grads[parity, low : low + 2 * EDGE]], axis=0
                 ).astype(F32),
             )
             put(
+                b,
+                parity,
                 half - EDGE,
                 jnp.concatenate(
                     [grads[parity, high - 2 * EDGE : high], halo[1, parity, b]], axis=0
                 ).astype(F32),
             )
-    load[2].wait()
-    load[3].wait()
-    for parity in range(2):
-
-        def convolve(j, c):
-            cols = pl.multiple_of(j * 256, 256)
-            total = None
+
+    for b in range(B):
+        for parity in range(2):
+            spread_piece(b, parity)
+
+    def convolve_piece(parity, j):
+        @piece(("convolve", parity, j), 1.4)
+        def _():
+            if parity == 0 and j == 0:
+                load_rest[1].wait()
+                load_rest[2].wait()
+            part = None
             for k in range(5):
                 lanes = (k + 1 - parity) * C
-                part = lax.dot_general(
+                more = lax.dot_general(
                     taps[:, lanes : lanes + C],
-                    w1[k, pl.ds(cols, 256), :],
+                    w1[k, j * 256 : (j + 1) * 256, :],
                     NT,
                     preferred_element_type=F32,
                 )
-                total = part if total is None else total + part
-            act_grad[parity, :, pl.ds(cols, 256)] = total
-            return c
-
-        lax.fori_loop(0, C // 256, convolve, 0)
+                part = more if part is None else part + more
+            act_grad[parity, :, j * 256 : (j + 1) * 256] = part
+
+    for parity in range(2):
+        for j in range(C // 256):
+            convolve_piece(parity, j)
     norms = [
         Norm(stats[b : b + 1, :], stats[B + b : B + b + 1, :], gain1[...], bias1[...])
         for b in range(B)
     ]
     zero = jnp.zeros((8, C), F32)
-    totals = []
-    for b in range(B):
-        norm = norms[b]
-        carry = (zero, zero)
-        for parity in range(2):
+    carries = [(zero, zero) for _ in range(B)]
+
+    def slope_piece(b, parity):
+        @piece(("slope", b, parity), 1.2)
+        def _():
+            norm = norms[b]
 
             def slope(r, carry):
                 at = pl.ds(b * half + r, EDGE)
@@ -794,23 +1099,40 @@
                 act_grad[parity, at] = flat(grad)
                 return carry[0] + jnp.sum(grad, axis=0), carry[1] + jnp.sum(grad * normed, axis=0)
 
-            carry = chunks(half, slope, carry)
-        totals.append(carry)
+            carries[b] = chunks(half, slope, carries[b])
+
+    for b in range(B):
+        for parity in range(2):
+            slope_piece(b, parity)
     step = Exchange(place, 0, plane_buf, line_buf, exchange_send, exchange_recv)
-    step.start([row_sum(t[0]) for t in totals] + [row_sum(t[1]) for t in totals])
-    step.relay(join_sums)
-    back = step.finish(join_sums)
-    sums[0] = sums_in[...]
-    sums[0, 0:1, :] = sum(back[B:])
-    sums[0, 1:2, :] = sum(back[:B])
+    back = []
     swap = remote(sums.at[0], sums.at[1], core_send.at[0], core_recv.at[0], place.partner)
-    swap.start()
+
+    @piece("exchange", 4.0)
+    def _():
+        step.start([row_sum(t[0]) for t in carries] + [row_sum(t[1]) for t in carries])
+
+    @piece("relay", 4.0)
+    def _():
+        step.relay(join_sums)
+
+    @piece("finish", 0.1)
+    def _():
+        back.extend(step.finish(join_sums))
+        sums[0] = sums_in[...]
+        sums[0, 0:1, :] = sum(back[B:])
+        sums[0, 1:2, :] = sum(back[:B])
+        swap.start()
+
     scale = 1.0 / (L * nd * nq)
-    for b in range(B):
-        norm = norms[b]
-        mean_bias, mean_gain = eight(back[b] * scale), eight(back[B + b] * scale)
-        factor = norm.gain * norm.inv
-        for parity in range(2):
+    tall = half + 2 * EDGE
+
+    def gradient_piece(b, parity):
+        @piece(("gradient", b, parity), 0.8)
+        def _():
+            norm = norms[b]
+            mean_bias, mean_gain = eight(back[b] * scale), eight(back[B + b] * scale)
+            factor = norm.gain * norm.inv
 
             def input_grad(r, c):
                 values = placed[b, parity, pl.ds(r, 2 * EDGE)].astype(F32)[8 : 8 + EDGE]
@@ -820,20 +1142,14 @@
                     - mean_bias[None]
                     - normed * mean_gain[None]
                 )
-                window[b, pl.ds(parity * (half + 2 * EDGE) + EDGE + r, EDGE)] = flat(value).astype(
-                    BF16
-                )
+                window[b, pl.ds(parity * tall + EDGE + r, EDGE)] = flat(value).astype(BF16)
                 return c
 
             chunks(half, input_grad)
+
     for b in range(B):
-        turned = flip[b] == 1
         for parity in range(2):
-            low = parity * (half + 2 * EDGE)
-            head = window[b, low + EDGE : low + 2 * EDGE].astype(F32)
-            tail = window[b, low + half : low + half + EDGE].astype(F32)
-            edges[0, parity, b] = jnp.where(turned, head, tail).astype(BF16)
-            edges[1, parity, b] = jnp.where(turned, tail, head).astype(BF16)
+            gradient_piece(b, parity)
     ring = [
         remote(
             edges.at[i],
@@ -844,48 +1160,183 @@
         )
         for i, at in enumerate((place.next, place.prev))
     ]
-    for copy in ring:
+
+    @piece("edges", 4.0)
+    def _():
+        for b in range(B):
+            turned = flip[b] == 1
+            for parity in range(2):
+                low = parity * tall
+                head = window[b, low + EDGE : low + 2 * EDGE].astype(F32)
+                end = window[b, low + half : low + half + EDGE].astype(F32)
+                edges[0, parity, b] = jnp.where(turned, head, end).astype(BF16)
+                edges[1, parity, b] = jnp.where(turned, end, head).astype(BF16)
+        for copy in ring:
+            copy.start()
+
+    @piece("halo", 0.1)
+    def _():
+        for copy in ring:
+            copy.wait()
+
+    def place_piece(b, side):
+        @piece(("place", b, side), 1.0)
+        def _():
+            turned = flip[b] == 1
+            for parity in range(2):
+                low = parity * tall
+                from_prev = edges_in[0, parity, b].astype(F32)
+                from_next = edges_in[1, parity, b].astype(F32)
+                window[b, low : low + EDGE] = jnp.where(turned, from_next, from_prev).astype(BF16)
+                window[b, low + EDGE + half : low + tall] = jnp.where(
+                    turned, from_prev, from_next
+                ).astype(BF16)
+            shape = (L, 2 * tall)
+            at = lax.broadcasted_iota(jnp.int32, shape, 0) + shift[b]
+            at = flip[b] * (L - 1) + (1 - 2 * flip[b]) * at
+            source = (at & 1) * tall + (at >> 1) + EDGE
+            pick = jnp.where(lax.broadcasted_iota(jnp.int32, shape, 1) == source, 1.0, 0.0)
+            cols = slice(side * width, (side + 1) * width)
+            ours[side, b] = jnp.dot(
+                pick.astype(BF16), window[b, :, cols], preferred_element_type=F32
+            ).astype(BF16)
+
+    for b in range(B):
+        for side in range(2):
+            place_piece(b, side)
+    cross_back = remote(
+        ours.at[1 - s], final, core_send.at[1], core_recv.at[1], place.partner
+    )
+    keep_back = pltpu.make_async_copy(ours.at[s], back_out.at[mine], local_sem.at[0])
+    give_back = pltpu.make_async_copy(
+        final, back_out.at[pl.ds((1 - s) * B, B)], local_sem.at[1]
+    )
+
+    @piece("swap", 2.0)
+    def _():
+        cross_back.start()
+        keep_back.start()
+        swap.wait()
+        sums_out[...] = sums[0] + sums[1]
+
+    @piece("give", 0.1)
+    def _():
+        cross_back.wait()
+        give_back.start()
+
+    for item in plan(depth, blocks, pieces, cube.events()):
+        if item in todo:
+            todo[item]()
+        else:
+            cube.run(*item)
+    cube.end()
+    across.wait()
+    for copy in away:
+        copy.wait()
+    keep_near.wait()
+    keep_back.wait()
+    give_back.wait()
+
+
+def finish_kernel(
+    dims,
+    first_blocks,
+    summed,
+    near,
+    far,
+    back,
+    flips,
+    conv1,
+    conv2,
+    conv3,
+    result,
+    back_out,
+    held,
+    wide,
+    near_buf,
+    far_buf,
+    back_buf,
+    in_sem,
+    out_sem,
+    side_sem,
+):
+    C, H, L, B, nd, nq = dims
+    blocks = summed.shape[1]
+    width = C // 2
+    tasks = [(block, side) for block in range(blocks) for side in range(2)]
+    slots = wide.shape[0]
+    loads = [
+        pltpu.make_async_copy(summed.at[side, block], held.at[i], in_sem.at[i])
+        for i, (block, side) in enumerate(tasks)
+    ]
+    sides = [
+        pltpu.make_async_copy(near, near_buf, side_sem.at[0]),
+        pltpu.make_async_copy(far, far_buf, side_sem.at[1]),
+        pltpu.make_async_copy(back, back_buf, side_sem.at[2]),
+    ]
+    for copy in loads[:8] + sides + loads[8:]:
         copy.start()
-    for copy in ring:
+    bottom = 3 * C
+
+    def targets(block, side, slot):
+        if block >= first_blocks:
+            row = (block - first_blocks) * BLOCK
+            cols = slice(side * width, (side + 1) * width)
+            return [(wide.at[slot], conv1.at[row : row + BLOCK, cols])]
+        row = side * first_blocks * BLOCK + block * BLOCK
+        if row < bottom:
+            return [(wide.at[slot], conv2.at[row : row + BLOCK])]
+        parts, at = [], 0
+        while at < BLOCK:
+            place = row - bottom + at
+            which, first = place // H, place % H
+            count = min(BLOCK - at, H - first)
+            cols = slice(which * width, (which + 1) * width)
+            parts.append((wide.at[slot, at : at + count], conv3.at[first : first + count, cols]))
+            at += count
+        return parts
+
+    going = [[] for _ in range(slots)]
+    for i, (block, side) in enumerate(tasks):
+        slot = i % slots
+        for copy in going[slot]:
+            copy.wait()
+        loads[i].wait()
+
+        def widen(r, c):
+            at = pl.ds(r, EDGE)
+            wide[slot, at] = held[i, at].astype(F32)
+            return c
+
+        chunks(BLOCK, widen, 0, 2)
+        going[slot] = [
+            pltpu.make_async_copy(src, dst, out_sem.at[slot, j])
+            for j, (src, dst) in enumerate(targets(block, side, slot))
+        ]
+        for copy in going[slot]:
+            copy.start()
+    for copy in sides:
         copy.wait()
-    for b in range(B):
-        turned = flip[b] == 1
-        for parity in range(2):
-            low = parity * (half + 2 * EDGE)
-            from_prev = edges_in[0, parity, b].astype(F32)
-            from_next = edges_in[1, parity, b].astype(F32)
-            window[b, low : low + EDGE] = jnp.where(turned, from_next, from_prev).astype(BF16)
-            window[b, low + EDGE + half : low + 2 * EDGE + half] = jnp.where(
-                turned, from_prev, from_next
+    give = pltpu.make_async_copy(back_buf, back_out, side_sem.at[2])
+    give.start()
+    for b in range(near.shape[0]):
+        turned = flips[b]
+
+        def deliver(r, c):
+            at = pl.ds(r, EDGE)
+            near_buf[b, at] = jnp.where(
+                turned == 1, far_buf[b, at].astype(F32), near_buf[b, at].astype(F32)
             ).astype(BF16)
-        shape = (L, 2 * (half + 2 * EDGE))
-        at = lax.broadcasted_iota(jnp.int32, shape, 0) + shift[b]
-        at = flip[b] * (L - 1) + (1 - 2 * flip[b]) * at
-        source = (at & 1) * (half + 2 * EDGE) + (at >> 1) + EDGE
-        pick = jnp.where(lax.broadcasted_iota(jnp.int32, shape, 1) == source, 1.0, 0.0).astype(BF16)
-        for side in range(2):
-            cols = slice(side * (C // 2), (side + 1) * (C // 2))
-            ours[side, b] = jnp.dot(pick, window[b, :, cols], preferred_element_type=F32).astype(
-                BF16
-            )
-    across = remote(
-        ours.at[1 - s],
-        final.at[pl.ds(s * B, B)],
-        core_send.at[1],
-        core_recv.at[1],
-        place.partner,
-    )
-    across.start()
-    keep = pltpu.make_async_copy(ours.at[s], out.at[pl.ds(s * B, B)], local_sem.at[4])
-    keep.start()
-    swap.wait()
-    sums_out[...] = sums[0] + sums[1]
-    across.wait()
-    other = pl.ds((1 - s) * B, B)
-    give = pltpu.make_async_copy(final.at[other], out.at[other], local_sem.at[5])
-    give.start()
-    keep.wait()
+            return c
+
+        chunks(L // 2, deliver)
+    hand = pltpu.make_async_copy(near_buf, result, side_sem.at[0])
+    hand.start()
+    for copies in going:
+        for copy in copies:
+            copy.wait()
     give.wait()
+    hand.wait()
 
 
 def on_device(
@@ -919,7 +1370,9 @@
     gain1, bias1, gain2, bias2, gain3, bias3 = (
         v.reshape(1, -1) for v in (gain1, bias1, gain2, bias2, gain3, bias3)
     )
-    taps, placed, grads, halo, stats, sums, result, conv2, conv3 = pl.pallas_call(
+    width = C // 2
+    side = (3 * C * H + H * C) // width // 2
+    taps, placed, grads, halo, stats, sums, result, own, other = pl.pallas_call(
         functools.partial(first_kernel, dims),
         name="forward_and_back",
         out_shape=(
@@ -929,9 +1382,9 @@
             shape((2, 2, B, EDGE, C), BF16),
             shape((8, C), F32),
             shape((8, C), F32),
-            shape((2 * B, half, C // 2), BF16),
-            shape((3 * C, H), BF16),
-            shape((H, C), BF16),
+            shape((2, B, half, width), BF16),
+            shape((side, width), F32),
+            shape((side, width), BF16),
         ),
         in_specs=[
             anywhere,
@@ -972,13 +1425,11 @@
             pltpu.VMEM((B, half + 2 * EDGE, H), BF16),
             pltpu.VMEM((rows, 3 * H), BF16),
             pltpu.VMEM((rows, C), F32),
-            pltpu.VMEM((3 * C, H), BF16),
-            pltpu.VMEM((H, C), BF16),
+            pltpu.VMEM((2 * side, width), F32),
+            pltpu.VMEM((2 * side, width), BF16),
             pltpu.VMEM((2, rows, C), BF16),
             pltpu.VMEM((2, 2, B, EDGE, C), BF16),
-            pltpu.VMEM((2, B, half, C // 2), BF16),
-            pltpu.VMEM((2 * B, half, C // 2), BF16),
-            pltpu.VMEM((2 * B, half, C // 2), BF16),
+            pltpu.VMEM((2, B, half, width), BF16),
             pltpu.VMEM((8, C), F32),
             pltpu.VMEM((8, C), F32),
             pltpu.VMEM((5, nd, 8, C), F32),
@@ -990,8 +1441,6 @@
             dma((4, 2)),
             dma((1,)),
             dma((1,)),
-            dma((3,)),
-            dma((3,)),
         ],
         compiler_params=pltpu.CompilerParams(
             collective_id=0, has_side_effects=True, vmem_limit_bytes=58 * 2**20
@@ -1011,31 +1460,24 @@
         bias3,
         weight3,
     )
-    axes = ("section", "dp", "seq")
-    conv2, conv3 = lax.psum((conv2, conv3), axes)
-    conv1 = pl.pallas_call(
-        weight_kernel,
-        name="first_weight_gradient",
-        grid=(5,),
-        out_shape=shape((5 * C, C), BF16),
+    first_blocks = side // BLOCK
+    blocks = first_blocks + 5 * C // BLOCK
+    depth = (nd.bit_length() - 1) + (nq.bit_length() - 1)
+    summed, near, far, back, sums = pl.pallas_call(
+        functools.partial(tail_kernel, dims),
+        name="sum_and_back",
+        out_shape=(
+            shape((2, blocks, BLOCK, width), BF16),
+            shape((2 * B, half, width), BF16),
+            shape((2 * B, half, width), BF16),
+            shape((2 * B, L, width), BF16),
+            shape((8, C), F32),
+        ),
         in_specs=[
-            pl.BlockSpec((rows, C), lambda k: (0, k)),
-            pl.BlockSpec((rows, C), lambda k: (0, k + 1)),
-            pl.BlockSpec((1, rows, C), lambda k: (0, 0, 0)),
-            pl.BlockSpec((1, rows, C), lambda k: (1, 0, 0)),
-        ],
-        out_specs=pl.BlockSpec((C, C), lambda k: (k, 0)),
-        compiler_params=pltpu.CompilerParams(vmem_limit_bytes=32 * 2**20),
-        cost_estimate=pl.CostEstimate(
-            flops=20 * rows * C * C, bytes_accessed=30 * C * C, transcendentals=0
-        ),
-    )(taps, taps, grads, grads)
-    conv1 = lax.psum(conv1, axes)
-    back, sums = pl.pallas_call(
-        functools.partial(last_kernel, dims),
-        name="first_input_gradient",
-        out_shape=(shape((2 * B, L, C // 2), BF16), shape((8, C), F32)),
-        in_specs=[
+            anywhere,
+            anywhere,
+            anywhere,
+            anywhere,
             anywhere,
             anywhere,
             anywhere,
@@ -1047,8 +1489,14 @@
             vmem,
             anywhere,
         ],
-        out_specs=[anywhere, vmem],
+        out_specs=[anywhere] * 4 + [vmem],
         scratch_shapes=[
+            pltpu.VMEM((blocks, BLOCK, width), F32),
+            pltpu.VMEM((blocks, BLOCK, width), BF16),
+            pltpu.VMEM((blocks - first_blocks, BLOCK, width), BF16),
+            pltpu.VMEM((blocks, region(depth), width), BF16),
+            pltpu.VMEM((2, blocks, BLOCK, width), BF16),
+            pltpu.VMEM((BLOCK, C), F32),
             pltpu.VMEM((B, 2, half + EDGE, C), BF16),
             pltpu.VMEM((2, rows, C), BF16),
             pltpu.VMEM((2, 2, B, EDGE, C), BF16),
@@ -1058,36 +1506,84 @@
             pltpu.VMEM((2, 2, B, EDGE, C), BF16),
             pltpu.VMEM((2, 2, B, EDGE, C), BF16),
             pltpu.VMEM((B, 2 * (half + 2 * EDGE), C), BF16),
-            pltpu.VMEM((2, B, L, C // 2), BF16),
-            pltpu.VMEM((2 * B, L, C // 2), BF16),
+            pltpu.VMEM((2, B, L, width), BF16),
+            pltpu.VMEM((B, L, width), BF16),
             pltpu.VMEM((2, 8, C), F32),
             pltpu.VMEM((1, nd, 8, C), F32),
             pltpu.VMEM((1, nq, 8, C), F32),
-            dma((6,)),
+            dma((6 + first_blocks,)),
             dma((1, peers)),
             dma((1, peers)),
             dma((2,)),
             dma((2,)),
             dma((2,)),
             dma((2,)),
+            dma((1 + 2 * B,)),
+            dma((1 + 2 * B,)),
+            dma((blocks,)),
+            dma((blocks,)),
+            dma((blocks, depth)),
+            dma((blocks, depth)),
+            dma((blocks, depth)),
+            dma((blocks, depth)),
+            dma((blocks,)),
+            dma((blocks,)),
+            dma((blocks,)),
         ],
         compiler_params=pltpu.CompilerParams(
-            collective_id=1, has_side_effects=True, vmem_limit_bytes=48 * 2**20
+            collective_id=1, has_side_effects=True, vmem_limit_bytes=60 * 2**20
         ),
-        cost_estimate=pl.CostEstimate(
-            flops=20 * rows * C * C, bytes_accessed=30 * C * C, transcendentals=0
+    )(
+        taps,
+        placed,
+        grads,
+        halo,
+        own,
+        other,
+        result,
+        stats,
+        sums,
+        shifts,
+        flips,
+        gain1,
+        bias1,
+        weight1,
+    )
+    slots = 6
+    conv1, conv2, conv3, result, back = pl.pallas_call(
+        functools.partial(finish_kernel, dims, first_blocks),
+        name="widen",
+        out_shape=(
+            shape((5 * C, C), F32),
+            shape((3 * C, H), F32),
+            shape((H, C), F32),
+            shape((2 * B, half, width), BF16),
+            shape((2 * B, L, width), BF16),
         ),
-    )(placed, grads, halo, stats, sums, shifts, flips, gain1, bias1, weight1)
+        in_specs=[anywhere] * 4 + [smem],
+        out_specs=[anywhere] * 5,
+        scratch_shapes=[
+            pltpu.VMEM((2 * blocks, BLOCK, width), BF16),
+            pltpu.VMEM((slots, BLOCK, width), F32),
+            pltpu.VMEM((2 * B, half, width), BF16),
+            pltpu.VMEM((2 * B, half, width), BF16),
+            pltpu.VMEM((2 * B, L, width), BF16),
+            dma((2 * blocks,)),
+            dma((slots, 2)),
+            dma((3,)),
+        ],
+        compiler_params=pltpu.CompilerParams(vmem_limit_bytes=32 * 2**20),
+    )(summed, near, far, back, flips)
     return (
         result,
         back,
-        conv1.reshape(5, C, C).astype(F32),
+        conv1.reshape(5, C, C),
         sums[0],
         sums[1],
-        conv2.reshape(3, C, H).astype(F32),
+        conv2.reshape(3, C, H),
         sums[2],
         sums[3],
-        conv3.astype(F32),
+        conv3,
         sums[4, :H],
         sums[5, :H],
     )

time: 368 us -> 263 us (0.71)
  waiting for transfers between devices: 140 us -> 0 us
  Pallas kernels: 180 us -> 241 us
  between operations: 14.1 us -> 0.86 us
  other arithmetic: 11.5 us -> 0 us
    psum x1 -> x0, waiting for transfers between devices: 140 us -> none  [on_device(): conv1 = lax.psum(conv1, axes)]
    pallas_call x2, Pallas kernels: 54.6 us -> 149 us  [the longest x1 130 us: on_device(): pl.pallas_call(functools.partial(tail_kernel, dims), name='sum_and_back',...]
    pallas_call x1, Pallas kernels: 125 us -> 92 us  [on_device(): pl.pallas_call(functools.partial(first_kernel, dims), name='forward_and_b...]
    convert_element_type x3 -> x0, other arithmetic: 11.5 us -> none  [the longest x1 8.42 us: on_device(): conv1.reshape(5, C, C).astype(F32)]
    unnamed x32 -> x10, local copies, waits for them, and re-layouts: 11.6 us -> 7.02 us
  transfers between devices with their start and end apart: 1 -> 0, of which waited for: 1 -> 0; matrix products, arithmetic and copies ran while one was open for 0% -> 0% of each run, Pallas kernels for 13% -> 0%
where the time goes in v2:
time: 263 us; the launch traced here: 259 us
  Pallas kernels  241 us (92%)
  local copies, waits for them, and re-layouts  17.5 us (7%)
    pallas_call x1, Pallas kernels, on_device(): pl.pallas_call(functools.partial(tail_kernel, dims), name='sum_and_back',...  130 us
    pallas_call x1, Pallas kernels, on_device(): pl.pallas_call(functools.partial(first_kernel, dims), name='forward_and_b...  92 us
    pallas_call x1, Pallas kernels, on_device(): pl.pallas_call(functools.partial(finish_kernel, dims, first_blocks), name...  18.8 us
    reshape x6, local copies, waits for them, and re-layouts, on_device(): v.reshape(1, -1)  7.56 us
    unnamed x10, local copies, waits for them, and re-layouts  7.02 us

profile of v2, /device:TPU:9, one launch (start us, length us, event | category | flops | bytes accessed | tf_op | source)
XLA Modules:
  0.0 259.3 jit_solution(7084883541631425880)
XLA Ops:
  0.6 1.2 reshape.58.gain3
  1.9 1.2 reshape.59.bias3
  3.1 1.3 reshape.52.gain1
  4.4 1.3 reshape.53.bias1
  5.7 1.3 reshape.55.gain2
  6.9 1.3 reshape.56.bias2
  8.2 92.0 %forward_and_back.1 = (bf16[512,4608]{1,0:T(8,128)(2,1)}, bf16[2,2,272,768]{3,2,1,0:T(8,128)(2,1)}, bf16[2,512,768]{2,1,0:T(8,128)(2,1)}, bf16[2,2,2,16,768]{4,3...) custom-call(bf16[4,512,768]{2,1,0:T(8,128)(2,1)} %inputs.1, ...), custom_call_target="tpu_custom_call" | custom-call | tf_op jit(solution)/shard_map/forward_and_back/pallas_call | solution.py:1375
  100.2 0.0 copy-start.4
  100.2 130.1 %sum_and_back.1 = (bf16[2,21,256,384]{3,2,1,0:T(8,128)(2,1)}, bf16[4,256,384]{2,1,0:T(8,128)(2,1)}, bf16[4,256,384]{2,1,0:T(8,128)(2,1)}, bf16[4,512,384]{2,1,0:T(8,128)(2,1)}, f32[8,768]{1,0:T(8,128)}) custom-call(bf16[512,4608]{1,0:T(8,128)(2,1)} %get-tuple-element.30.taps_in, bf16[2,2,272,768]{3,2,1,0:T(8,128)(2,1)} %get-tuple-element.31.placed_in, ...), custom_call_target="tpu_custom_call" | custom-call | tf_op jit(solution)/shard_map/sum_and_back/pallas_call | solution.py:1466
  230.4 1.4 slice_reduce_fusion.4
  231.8 1.5 slice_reduce_fusion
  233.3 0.0 copy-done.4
  233.3 0.0 copy-start
  233.3 3.3 %copy-done = bf16[2,21,256,384]{3,2,1,0:T(8,128)(2,1)S(1)} copy-done((bf16[2,21,256,384]{3,2,1,0:T(8,128)(2,1)S(1)}, bf16[2,21,256,384]{3,2,1,0:T(8,128)(2,1)}, u32[]{:S(2)}) %copy-start) | copy-done | bytes 8257560
  236.6 0.0 copy-start.1
  236.6 1.4 copy-done.1
  238.0 0.0 copy-start.2
  238.0 1.1 copy-done.2
  239.2 0.0 copy-start.3
  239.2 1.1 copy-done.3
  240.3 18.8 %widen.1 = (f32[3840,768]{1,0:T(8,128)}, f32[2304,384]{1,0:T(8,128)}, f32[384,768]{1,0:T(8,128)}, bf16[4,256,384]{2,1,0:T(8,128)(2,1)}, bf16[4,512,384]{2,1,0:T(8,128)(2,1)}) custom-call(bf16[2,21,256,384]{3,2,1,0:T(8,128)(2,1)S(1)} %copy-done, bf16[4,256,384]{2,1,0:T(8,128)(2,1)S(1)} %copy-done.2, bf16[4,256,384]{2,1,0:T(8,128)(2,1)S(1)} %copy-done.3, ...), custom_call_target="tpu_custom_call" | custom-call | tf_op jit(solution)/shard_map/widen/pallas_call | solution.py:1553
Async XLA Ops:
  100.2 133.1 %copy-start.4 = (s32[4]{0:T(128)S(1)}, s32[4]{0:T(128)}, u32[]{:S(2)}) copy-start(s32[4]{0:T(128)} %flips.5) | copy-start | bytes 52
  233.3 3.3 %copy-start = (bf16[2,21,256,384]{3,2,1,0:T(8,128)(2,1)S(1)}, bf16[2,21,256,384]{3,2,1,0:T(8,128)(2,1)}, u32[]{:S(2)}) copy-start(bf16[2,21,256,384]{3,2,1,0:T(8,128)(2,1)} %get-tuple-element.39.summed) | copy-start | bytes 24772612
  236.6 1.4 copy-start.1
  238.0 1.1 copy-start.2
  239.2 1.1 copy-start.3

commit v3 on v2

--- a/solution.py
+++ b/solution.py
@@ -151,7 +151,10 @@
 
 class Norm:
     def __init__(self, mean, inv, gain, bias):
-        self.mean, self.inv, self.gain, self.bias = eight(mean), eight(inv), eight(gain), eight(bias)
+        self.mean, self.inv = eight(mean), eight(inv)
+        self.gain, self.bias = (
+            eight(vector[...].reshape(1, vector.shape[0])) for vector in (gain, bias)
+        )
 
     def normed(self, block):
         return (block - self.mean[None]) * self.inv[None]
@@ -298,7 +301,7 @@
         joined = exchange.finish(join_moments(float(count * nd)))
         scale = 1.0 / (count * nd * nq)
         inverse = [lax.rsqrt(square * scale + EPSILON) for square in joined[B:]]
-        return [Norm(joined[b], inverse[b], gain[...], bias[...]) for b in range(B)]
+        return [Norm(joined[b], inverse[b], gain, bias) for b in range(B)]
 
     step = exchange(0)
     step.start(
@@ -648,41 +651,30 @@
     def __init__(self, place, blocks, width, refs):
         self.place, self.blocks, self.width = place, blocks, width
         self.total, self.inbox, self.relayed, self.summed, self.out = refs[:5]
-        (
-            self.core_send,
-            self.core_recv,
-            self.down_send,
-            self.down_recv,
-            self.up_send,
-            self.up_recv,
-            self.share_send,
-            self.share_recv,
-            self.out_sem,
-        ) = refs[5:]
+        self.send_sem, self.core_recv, self.down_recv, self.up_recv, self.share_recv = refs[5:]
         self.sources = [None] * blocks
         self.axes = cube_axes(place)
+        self.planar = place.nd.bit_length() - 1
         self.flight = [None] * blocks
         self.state = [None] * blocks
 
     def order(self, block):
-        return [self.axes[i] for i in cube_order(block, len(self.axes))]
+        return [self.axes[i] for i in cube_order(block, self.planar, len(self.axes))]
 
     def events(self):
         depth = len(self.axes)
         return ["core"] + ["down"] * depth + ["up"] * halvings(depth) + ["share", "out"]
 
     def _add(self, block, incoming, first, count, send):
-        total, inbox, width = self.total, self.inbox, self.width
-
-        def add(r, c):
-            at = pl.ds(pl.multiple_of(first + r, EDGE), EDGE)
-            value = total[block, at] + incoming(r).astype(F32)
+        total, inbox = self.total, self.inbox
+
+        step = min(count, 4 * EDGE)
+        for r in range(0, count, step):
+            at = pl.ds(pl.multiple_of(first + r, EDGE), step)
+            value = total[block, at] + incoming(r, step).astype(F32)
             total[block, at] = value
             if send:
                 inbox[block, at] = value.astype(BF16)
-            return c
-
-        chunks(count, add)
 
     def run(self, block, stage):
         place, depth = self.place, len(self.axes)
@@ -694,7 +686,7 @@
             copy = remote(
                 self.sources[block],
                 self.inbox.at[block],
-                self.core_send.at[block],
+                self.send_sem.at[block],
                 self.core_recv.at[block],
                 place.partner,
             )
@@ -706,13 +698,13 @@
                 first, past = self.state[block]
             offset = first[-1]
             if k == 0:
-                incoming = lambda base: lambda r: self.inbox[
-                    block, pl.ds(pl.multiple_of(base + r, EDGE), EDGE)
+                incoming = lambda base: lambda r, n: self.inbox[
+                    block, pl.ds(pl.multiple_of(base + r, EDGE), n)
                 ]
                 base_of = lambda at: at
             else:
-                incoming = lambda base: lambda r: self.relayed[
-                    block, pl.ds(pl.multiple_of(base + r, EDGE), EDGE)
+                incoming = lambda base: lambda r, n: self.relayed[
+                    block, pl.ds(pl.multiple_of(base + r, EDGE), n)
                 ]
                 base_of = lambda at: at - offset + region(k - 1)
             if size >= 2 * EDGE:
@@ -727,7 +719,7 @@
             copy = remote(
                 self.inbox.at[block, pl.ds(pl.multiple_of(give, EDGE), small)],
                 self.relayed.at[block, region(k) : region(k) + small],
-                self.down_send.at[block, k],
+                self.send_sem.at[block],
                 self.down_recv.at[block, k],
                 partner,
             )
@@ -748,7 +740,7 @@
             copy = remote(
                 self.summed.at[s, block, at],
                 self.summed.at[s, block, at],
-                self.up_send.at[block, k],
+                self.send_sem.at[block],
                 self.up_recv.at[block, k],
                 partner,
             )
@@ -756,13 +748,13 @@
             copy = remote(
                 self.summed.at[s, block],
                 self.summed.at[s, block],
-                self.share_send.at[block],
+                self.send_sem.at[block],
                 self.share_recv.at[block],
                 place.partner,
             )
         else:
             copy = pltpu.make_async_copy(
-                self.summed.at[:, block], self.out.at[:, block], self.out_sem.at[block]
+                self.summed.at[:, block], self.out.at[:, block], self.send_sem.at[block]
             )
         if stage > 0 and stage <= depth:
             copy.start()
@@ -778,6 +770,7 @@
 
 
 BLOCK = 256
+HOP = 14.0
 
 
 def sizes(k):
@@ -799,28 +792,41 @@
         side = lax.rem(place.d // bit, 2)
         axes.append(((place.s, place.d + bit * (1 - 2 * side), place.q), side))
         bit *= 2
-    span = 2
-    while span <= place.nq:
-        low = lax.rem(place.q, span)
-        side = lax.rem(place.q // (span // 2) + place.q // span, 2)
-        axes.append(((place.s, place.d, place.q - low + span - 1 - low), side))
-        span *= 2
+    bit = 1
+    while bit < place.nq:
+        side = lax.rem(place.q // bit, 2)
+        axes.append(((place.s, place.d, place.q + bit * (1 - 2 * side)), side))
+        bit *= 2
     return axes
 
 
-def cube_order(block, depth):
-    others = [(block + i) % (depth - 1) for i in range(depth - 1)]
-    at = 1 if (block // (depth - 1)) % 2 else depth - 1
-    return others[:at] + [depth - 1] + others[at:]
-
-
-def plan(depth, blocks, pieces, events):
-    rate, wait, cost = 95e3, 1.6, 0.2
+def cube_order(block, planar, depth):
+    order = [(block + i) % planar for i in range(planar)] + list(range(planar, depth))
+    if block % 6 == 5:
+        order.remove(planar)
+        order = [planar] + order
+    return order
+
+
+def plan(planar, depth, blocks, pieces, events):
+    rate, cost = 95e3, 0.2
     free = [0.0] * (depth + 1)
     ready = {}
-    due = [(0, 0.0)] * 0
-    now, order = 0.0, []
+    now, order, done = 0.0, [], 0.0
     pieces = list(pieces)
+
+    def send(axis, size):
+        if axis == depth:
+            loads, speed, wait = [(depth, 1)], 6 * rate, 1.1
+        elif axis > planar:
+            loads, speed, wait = [(planar, 1), (axis, 2)], rate, 2.8
+        else:
+            loads, speed, wait = [(axis, 1)], rate, 2.2
+        begin = max([now] + [free[i] for i, _ in loads])
+        for i, times in loads:
+            free[i] = begin + times * size / speed
+        return max(free[i] for i, _ in loads) + wait
+
     while pieces or ready:
         able = sorted((t, b) for b, (t, _) in ready.items() if t <= now)
         if able:
@@ -830,27 +836,28 @@
             kind = events[stage]
             now += cost if kind == "down" else 0.05
             if stage + 1 < len(events):
+                axes = cube_order(block, planar, depth)
                 if kind in ("core", "share"):
-                    axis, size, speed = depth, 256, 4 * rate
+                    axis, size = depth, BLOCK
                 elif kind == "down":
-                    k = stage - 1
-                    axis, size, speed = cube_order(block, depth)[k], sizes(k + 1), rate
+                    axis, size = axes[stage - 1], sizes(stage)
                 elif kind == "up":
                     k = depth + halvings(depth) - stage
-                    axis, size, speed = cube_order(block, depth)[k], sizes(k + 1), rate
-                begin = max(now, free[axis])
-                free[axis] = begin + 2 * size * 768 / speed
-                ready[block] = (free[axis] + wait, stage + 1)
-        elif pieces:
-            name, time, made, sends = pieces.pop(0)
+                    axis, size = axes[k], sizes(k + 1)
+                else:
+                    axis, size = depth, 0
+                ready[block] = (send(axis, 2 * size * 768), stage + 1)
+        elif pieces and done + pieces[0][4] <= now:
+            name, time, made, sends, _ = pieces.pop(0)
             order.append(name)
             now += time
+            done = now
             for block in made:
                 ready[block] = (now, 0)
             for axis, size in sends:
-                free[axis] = max(now, free[axis]) + size / rate
+                send(axis, size)
         else:
-            now = min(t for t, _ in ready.values())
+            now = min([t for t, _ in ready.values()] + [done + p[4] for p in pieces[:1]])
     return order
 
 
@@ -874,7 +881,12 @@
     near_out,
     far_out,
     back_out,
-    sums_out,
+    gain1_out,
+    bias1_out,
+    gain2_out,
+    bias2_out,
+    gain3_out,
+    bias3_out,
     total,
     inbox,
     sending,
@@ -918,9 +930,7 @@
     blocks = first_blocks + 5 * per_tap
     cube = Cube(place, blocks, width, (total, inbox, relayed, summed, summed_out) + cube_sems)
     depth = len(cube.axes)
-    greeted = place.plane() + place.line() + [place.partner, cross]
-    bit = 1
-    place.greet(greeted)
+    place.greet(place.plane() + place.line() + [place.partner, cross])
     flip = [flips[s * B + b] for b in range(B)]
     shift = [shifts[s * B + b] for b in range(B)]
     load = [
@@ -944,10 +954,10 @@
         cube.sources[first_blocks + i] = sending.at[i]
     todo, pieces = {}, []
 
-    def piece(name, time, made=(), sends=()):
+    def piece(name, time, made=(), sends=(), after=0.0):
         def keep(body):
             todo[name] = body
-            pieces.append((name, time, made, sends))
+            pieces.append((name, time, made, sends, after))
             return body
 
         return keep
@@ -958,9 +968,8 @@
             copy.wait()
 
     across = remote(
-        result_in.at[1 - s], near_out.at[mine], result_send.at[0], result_recv.at[0], place.partner
+        result_in.at[1 - s], near_out, result_send.at[0], result_recv.at[0], place.partner
     )
-    keep_near = pltpu.make_async_copy(result_in.at[s], near_out.at[mine], local_sem.at[5])
     away = [
         remote(
             result_in.at[side, b],
@@ -973,10 +982,9 @@
         for i, side in enumerate((s, 1 - s))
     ]
     across.start()
-    keep_near.start()
 
     def result_piece(i):
-        @piece(("result", i), 0.05, (), [(depth - 1, 2 * half * width * 2)])
+        @piece(("result", i), 0.05, (), [(depth - 1, 4 * half * width)])
         def _():
             away[i].start()
 
@@ -1080,7 +1088,7 @@
         for j in range(C // 256):
             convolve_piece(parity, j)
     norms = [
-        Norm(stats[b : b + 1, :], stats[B + b : B + b + 1, :], gain1[...], bias1[...])
+        Norm(stats[b : b + 1, :], stats[B + b : B + b + 1, :], gain1, bias1)
         for b in range(B)
     ]
     zero = jnp.zeros((8, C), F32)
@@ -1108,15 +1116,15 @@
     back = []
     swap = remote(sums.at[0], sums.at[1], core_send.at[0], core_recv.at[0], place.partner)
 
-    @piece("exchange", 4.0)
+    @piece("exchange", 0.3)
     def _():
         step.start([row_sum(t[0]) for t in carries] + [row_sum(t[1]) for t in carries])
 
-    @piece("relay", 4.0)
+    @piece("relay", 0.3, after=HOP)
     def _():
         step.relay(join_sums)
 
-    @piece("finish", 0.1)
+    @piece("finish", 0.1, after=HOP)
     def _():
         back.extend(step.finish(join_sums))
         sums[0] = sums_in[...]
@@ -1161,7 +1169,7 @@
         for i, at in enumerate((place.next, place.prev))
     ]
 
-    @piece("edges", 4.0)
+    @piece("edges", 0.3)
     def _():
         for b in range(B):
             turned = flip[b] == 1
@@ -1174,7 +1182,7 @@
         for copy in ring:
             copy.start()
 
-    @piece("halo", 0.1)
+    @piece("halo", 0.1, after=HOP)
     def _():
         for copy in ring:
             copy.wait()
@@ -1212,19 +1220,23 @@
         final, back_out.at[pl.ds((1 - s) * B, B)], local_sem.at[1]
     )
 
-    @piece("swap", 2.0)
+    @piece("swap", 0.1)
     def _():
         cross_back.start()
         keep_back.start()
         swap.wait()
-        sums_out[...] = sums[0] + sums[1]
-
-    @piece("give", 0.1)
+        outs = (gain1_out, bias1_out, gain2_out, bias2_out, gain3_out, bias3_out)
+        for i, to in enumerate(outs):
+            count = to.shape[0]
+            row = sums[0, i : i + 1, 0:count] + sums[1, i : i + 1, 0:count]
+            to[...] = row.reshape(count)
+
+    @piece("give", 0.1, after=4.0)
     def _():
         cross_back.wait()
         give_back.start()
 
-    for item in plan(depth, blocks, pieces, cube.events()):
+    for item in plan(cube.planar, depth, blocks, pieces, cube.events()):
         if item in todo:
             todo[item]()
         else:
@@ -1233,7 +1245,6 @@
     across.wait()
     for copy in away:
         copy.wait()
-    keep_near.wait()
     keep_back.wait()
     give_back.wait()
 
@@ -1242,6 +1253,7 @@
     dims,
     first_blocks,
     summed,
+    mine,
     near,
     far,
     back,
@@ -1253,85 +1265,107 @@
     back_out,
     held,
     wide,
+    narrow,
     near_buf,
     far_buf,
     back_buf,
     in_sem,
-    out_sem,
+    wide_sem,
+    narrow_sem,
     side_sem,
 ):
     C, H, L, B, nd, nq = dims
+    s = lax.axis_index("section")
     blocks = summed.shape[1]
     width = C // 2
-    tasks = [(block, side) for block in range(blocks) for side in range(2)]
     slots = wide.shape[0]
-    loads = [
-        pltpu.make_async_copy(summed.at[side, block], held.at[i], in_sem.at[i])
-        for i, (block, side) in enumerate(tasks)
+    order = list(range(first_blocks, blocks)) + list(range(first_blocks))
+    loads = {
+        block: pltpu.make_async_copy(summed.at[:, block], held.at[block], in_sem.at[block])
+        for block in order
+    }
+    sides = [
+        pltpu.make_async_copy(mine.at[s], near_buf.at[pl.ds(s * B, B)], side_sem.at[0]),
+        pltpu.make_async_copy(near, near_buf.at[pl.ds((1 - s) * B, B)], side_sem.at[1]),
+        pltpu.make_async_copy(far, far_buf, side_sem.at[2]),
+        pltpu.make_async_copy(back, back_buf, side_sem.at[3]),
     ]
-    sides = [
-        pltpu.make_async_copy(near, near_buf, side_sem.at[0]),
-        pltpu.make_async_copy(far, far_buf, side_sem.at[1]),
-        pltpu.make_async_copy(back, back_buf, side_sem.at[2]),
-    ]
-    for copy in loads[:8] + sides + loads[8:]:
+    for block in order[:4]:
+        loads[block].start()
+    for copy in sides:
         copy.start()
+    for block in order[4:]:
+        loads[block].start()
     bottom = 3 * C
 
-    def targets(block, side, slot):
-        if block >= first_blocks:
-            row = (block - first_blocks) * BLOCK
-            cols = slice(side * width, (side + 1) * width)
-            return [(wide.at[slot], conv1.at[row : row + BLOCK, cols])]
+    def targets(block, side):
         row = side * first_blocks * BLOCK + block * BLOCK
         if row < bottom:
-            return [(wide.at[slot], conv2.at[row : row + BLOCK])]
+            return [(0, BLOCK, conv2.at[row : row + BLOCK])]
         parts, at = [], 0
         while at < BLOCK:
-            place = row - bottom + at
-            which, first = place // H, place % H
+            which, first = (row - bottom + at) // H, (row - bottom + at) % H
             count = min(BLOCK - at, H - first)
             cols = slice(which * width, (which + 1) * width)
-            parts.append((wide.at[slot, at : at + count], conv3.at[first : first + count, cols]))
+            parts.append((at, count, conv3.at[first : first + count, cols]))
             at += count
         return parts
 
     going = [[] for _ in range(slots)]
-    for i, (block, side) in enumerate(tasks):
+    for i, block in enumerate(order):
         slot = i % slots
         for copy in going[slot]:
             copy.wait()
-        loads[i].wait()
-
-        def widen(r, c):
-            at = pl.ds(r, EDGE)
-            wide[slot, at] = held[i, at].astype(F32)
-            return c
-
-        chunks(BLOCK, widen, 0, 2)
-        going[slot] = [
-            pltpu.make_async_copy(src, dst, out_sem.at[slot, j])
-            for j, (src, dst) in enumerate(targets(block, side, slot))
-        ]
+        loads[block].wait()
+        for side in range(2):
+
+            def widen(r, c):
+                at = pl.ds(pl.multiple_of(r * 64, 64), 64)
+                value = held[block, side, at].astype(F32)
+                if block >= first_blocks:
+                    wide[slot, at, side * width : (side + 1) * width] = value
+                else:
+                    narrow[slot, side, at] = value
+                return c
+
+            lax.fori_loop(0, BLOCK // 64, widen, 0)
+        if block >= first_blocks:
+            row = (block - first_blocks) * BLOCK
+            going[slot] = [
+                pltpu.make_async_copy(
+                    wide.at[slot], conv1.at[row : row + BLOCK], wide_sem.at[slot]
+                )
+            ]
+        else:
+            parts = [(side, *part) for side in range(2) for part in targets(block, side)]
+            going[slot] = [
+                pltpu.make_async_copy(
+                    narrow.at[slot, side, at : at + count], to, narrow_sem.at[slot, j]
+                )
+                for j, (side, at, count, to) in enumerate(parts)
+            ]
         for copy in going[slot]:
             copy.start()
-    for copy in sides:
-        copy.wait()
-    give = pltpu.make_async_copy(back_buf, back_out, side_sem.at[2])
-    give.start()
-    for b in range(near.shape[0]):
-        turned = flips[b]
-
-        def deliver(r, c):
-            at = pl.ds(r, EDGE)
-            near_buf[b, at] = jnp.where(
-                turned == 1, far_buf[b, at].astype(F32), near_buf[b, at].astype(F32)
-            ).astype(BF16)
-            return c
-
-        chunks(L // 2, deliver)
-    hand = pltpu.make_async_copy(near_buf, result, side_sem.at[0])
-    hand.start()
+        if i == 2:
+            sides[3].wait()
+            give = pltpu.make_async_copy(back_buf, back_out, side_sem.at[3])
+            give.start()
+        if i == 4:
+            for copy in sides[:3]:
+                copy.wait()
+            for b in range(2 * B):
+                turned = flips[b]
+
+                def deliver(r, c):
+                    at = pl.ds(pl.multiple_of(r * 64, 64), 64)
+                    near_buf[b, at] = jnp.where(
+                        turned == 1, far_buf[b, at].astype(F32), near_buf[b, at].astype(F32)
+                    ).astype(BF16)
+                    return c
+
+                lax.fori_loop(0, L // 128, deliver, 0)
+            hand = pltpu.make_async_copy(near_buf, result, side_sem.at[0])
+            hand.start()
     for copies in going:
         for copy in copies:
             copy.wait()
@@ -1367,9 +1401,6 @@
     peers = nd - 1 + nq - 1
     shape = jax.ShapeDtypeStruct
     dma = pltpu.SemaphoreType.DMA
-    gain1, bias1, gain2, bias2, gain3, bias3 = (
-        v.reshape(1, -1) for v in (gain1, bias1, gain2, bias2, gain3, bias3)
-    )
     width = C // 2
     side = (3 * C * H + H * C) // width // 2
     taps, placed, grads, halo, stats, sums, result, own, other = pl.pallas_call(
@@ -1463,16 +1494,17 @@
     first_blocks = side // BLOCK
     blocks = first_blocks + 5 * C // BLOCK
     depth = (nd.bit_length() - 1) + (nq.bit_length() - 1)
-    summed, near, far, back, sums = pl.pallas_call(
+    summed, near, far, back, *vectors = pl.pallas_call(
         functools.partial(tail_kernel, dims),
         name="sum_and_back",
         out_shape=(
             shape((2, blocks, BLOCK, width), BF16),
-            shape((2 * B, half, width), BF16),
+            shape((B, half, width), BF16),
             shape((2 * B, half, width), BF16),
             shape((2 * B, L, width), BF16),
-            shape((8, C), F32),
-        ),
+        )
+        + (shape((C,), F32),) * 4
+        + (shape((H,), F32),) * 2,
         in_specs=[
             anywhere,
             anywhere,
@@ -1489,7 +1521,7 @@
             vmem,
             anywhere,
         ],
-        out_specs=[anywhere] * 4 + [vmem],
+        out_specs=[anywhere] * 4 + [vmem] * 6,
         scratch_shapes=[
             pltpu.VMEM((blocks, BLOCK, width), F32),
             pltpu.VMEM((blocks, BLOCK, width), BF16),
@@ -1523,11 +1555,7 @@
             dma((blocks,)),
             dma((blocks,)),
             dma((blocks, depth)),
-            dma((blocks, depth)),
-            dma((blocks, depth)),
-            dma((blocks, depth)),
-            dma((blocks,)),
-            dma((blocks,)),
+            dma((blocks, halvings(depth))),
             dma((blocks,)),
         ],
         compiler_params=pltpu.CompilerParams(
@@ -1560,32 +1588,34 @@
             shape((2 * B, half, width), BF16),
             shape((2 * B, L, width), BF16),
         ),
-        in_specs=[anywhere] * 4 + [smem],
+        in_specs=[anywhere] * 5 + [smem],
         out_specs=[anywhere] * 5,
         scratch_shapes=[
-            pltpu.VMEM((2 * blocks, BLOCK, width), BF16),
-            pltpu.VMEM((slots, BLOCK, width), F32),
+            pltpu.VMEM((blocks, 2, BLOCK, width), BF16),
+            pltpu.VMEM((slots, BLOCK, C), F32),
+            pltpu.VMEM((slots, 2, BLOCK, width), F32),
             pltpu.VMEM((2 * B, half, width), BF16),
             pltpu.VMEM((2 * B, half, width), BF16),
             pltpu.VMEM((2 * B, L, width), BF16),
-            dma((2 * blocks,)),
-            dma((slots, 2)),
-            dma((3,)),
+            dma((blocks,)),
+            dma((slots,)),
+            dma((slots, 4)),
+            dma((4,)),
         ],
         compiler_params=pltpu.CompilerParams(vmem_limit_bytes=32 * 2**20),
-    )(summed, near, far, back, flips)
+    )(summed, result, near, far, back, flips)
     return (
         result,
         back,
         conv1.reshape(5, C, C),
-        sums[0],
-        sums[1],
+        vectors[0],
+        vectors[1],
         conv2.reshape(3, C, H),
-        sums[2],
-        sums[3],
+        vectors[2],
+        vectors[3],
         conv3,
-        sums[4, :H],
-        sums[5, :H],
+        vectors[4],
+        vectors[5],
     )
 
 

time: 263 us -> 230 us (0.87)
  Pallas kernels: 241 us -> 215 us
  local copies, waits for them, and re-layouts: 17.5 us -> 10.4 us
    pallas_call x1, Pallas kernels: 130 us -> 113 us  [on_device(): pl.pallas_call(functools.partial(tail_kernel, dims), name='sum_and_back',...]
    pallas_call x1, Pallas kernels: 18.8 us -> 10.3 us  [on_device(): pl.pallas_call(functools.partial(finish_kernel, dims, first_blocks), name...]
    reshape x6 -> x0, local copies, waits for them, and re-layouts: 7.56 us -> none  [on_device(): v.reshape(1, -1)]
    unnamed x10 -> x30, local copies, waits for them, and re-layouts: 7.02 us -> 10.4 us
    slice x2 -> x0, local copies, waits for them, and re-layouts: 2.91 us -> none  [the longest x1 1.52 us: on_device(): sums[3]]
where the time goes in v3:
time: 230 us; the launch traced here: 227 us
  Pallas kernels  215 us (93%)
  local copies, waits for them, and re-layouts  10.4 us (5%)
    pallas_call x1, Pallas kernels, on_device(): pl.pallas_call(functools.partial(tail_kernel, dims), name='sum_and_back',...  113 us
    pallas_call x1, Pallas kernels, on_device(): pl.pallas_call(functools.partial(first_kernel, dims), name='forward_and_b...  92 us
    unnamed x30, local copies, waits for them, and re-layouts  10.4 us
    pallas_call x1, Pallas kernels, on_device(): pl.pallas_call(functools.partial(finish_kernel, dims, first_blocks), name...  10.3 us

profile of v3, /device:TPU:9, one launch (start us, length us, event | category | flops | bytes accessed | tf_op | source)
XLA Modules:
  0.0 226.6 jit_solution(9665965071786018473)
XLA Ops:
  0.6 92.0 %forward_and_back.1 = (bf16[512,4608]{1,0:T(8,128)(2,1)}, bf16[2,2,272,768]{3,2,1,0:T(8,128)(2,1)}, bf16[2,512,768]{2,1,0:T(8,128)(2,1)}, bf16[2,2,2,16,768]{4,3...) custom-call(bf16[4,512,768]{2,1,0:T(8,128)(2,1)} %inputs.1, ...), custom_call_target="tpu_custom_call" | custom-call | tf_op jit(solution)/shard_map/forward_and_back/pallas_call | solution.py:1406
  92.7 0.0 copy-start.1
  92.7 0.0 copy-start.5
  92.7 113.1 %sum_and_back.1 = (bf16[2,21,256,384]{3,2,1,0:T(8,128)(2,1)}, bf16[2,256,384]{2,1,0:T(8,128)(2,1)}, bf16[4,256,384]{2,1,0:T(8,128)(2,1)}, bf16[4,512,384]{2,1,0:...) custom-call(bf16[512,4608]{1,0:T(8,128)(2,1)} %get-tuple-element.35., ...), custom_call_target="tpu_custom_call" | custom-call | tf_op jit(solution)/shard_map/sum_and_back/pallas_call | solution.py:1497
  205.8 0.0 copy-done.1
  205.8 0.0 copy-done.5
  205.8 0.0 copy-start
  205.8 3.3 %copy-done = bf16[2,21,256,384]{3,2,1,0:T(8,128)(2,1)S(1)} copy-done((bf16[2,21,256,384]{3,2,1,0:T(8,128)(2,1)S(1)}, bf16[2,21,256,384]{3,2,1,0:T(8,128)(2,1)}, u32[]{:S(2)}) %copy-start) | copy-done | bytes 8257560
  209.2 1.4 copy-done.2
  210.6 1.1 copy-done.3
  211.7 1.0 copy-done.4
  212.7 0.0 copy-start.11
  212.7 0.0 copy-start.10
  212.8 10.3 %widen.1 = (f32[3840,768]{1,0:T(8,128)}, f32[2304,384]{1,0:T(8,128)}, f32[384,768]{1,0:T(8,128)}, bf16[4,256,384]{2,1,0:T(8,128)(2,1)}, bf16[4,512,384]{2,1,0:T(8,128)(2,1)}) custom-call(bf16[2,21,256,384]{3,2,1,0:T(8,128)(2,1)S(1)} %copy-done, bf16[2,2,256,384]{3,2,1,0:T(8,128)(2,1)S(1)} %copy-done.1, bf16[2,256,384]{2,1,0:T(8,128)(2,1)S(1)} %copy-done.4, ...), custom_call_target="tpu_custom_call" | custom-call | tf_op jit(solution)/shard_map/widen/pallas_call | solution.py:1581
  223.0 0.0 copy-done.9
  223.0 0.6 copy.30
  223.6 0.0 copy-done.8
  223.6 0.6 copy.31
  224.2 0.0 copy-done.7
  224.2 0.6 copy.32
  224.8 0.0 copy-done.6
  224.8 0.6 copy.33
  225.4 0.6 copy.34
  226.0 0.6 copy.35
  (9 shorter events, 0.0 us)
Async XLA Ops:
  92.7 113.1 %copy-start.1 = (bf16[2,2,256,384]{3,2,1,0:T(8,128)(2,1)S(1)}, bf16[2,2,256,384]{3,2,1,0:T(8,128)(2,1)}, u32[]{:S(2)}) copy-start(bf16[2,2,256,384]{3,2,1,0:T(8,128)(2,1)} %get-tuple-element.41.result_in.mine) | copy-start | bytes 2359300
  92.7 113.1 %copy-start.5 = (s32[4]{0:T(128)S(1)}, s32[4]{0:T(128)}, u32[]{:S(2)}) copy-start(s32[4]{0:T(128)} %flips.5) | copy-start | bytes 52
  205.8 3.3 %copy-start = (bf16[2,21,256,384]{3,2,1,0:T(8,128)(2,1)S(1)}, bf16[2,21,256,384]{3,2,1,0:T(8,128)(2,1)}, u32[]{:S(2)}) copy-start(bf16[2,21,256,384]{3,2,1,0:T(8,128)(2,1)} %get-tuple-element.44.summed) | copy-start | bytes 24772612
  209.2 1.4 copy-start.2
  210.6 1.1 copy-start.3
  211.7 1.0 copy-start.4
  212.7 10.3 %copy-start.9 = (f32[768]{0:T(1024)S(1)}, f32[768]{0:T(1024)}, u32[]{:S(2)}) copy-start(f32[768]{0:T(1024)} %get-tuple-element.73) | copy-start | bytes 9220
  212.7 10.9 %copy-start.8 = (f32[768]{0:T(1024)S(1)}, f32[768]{0:T(1024)}, u32[]{:S(2)}) copy-start(f32[768]{0:T(1024)} %get-tuple-element.74) | copy-start | bytes 9220
  212.7 11.5 %copy-start.7 = (f32[768]{0:T(1024)S(1)}, f32[768]{0:T(1024)}, u32[]{:S(2)}) copy-start(f32[768]{0:T(1024)} %get-tuple-element.76) | copy-start | bytes 9220
  212.7 12.1 %copy-start.6 = (f32[768]{0:T(1024)S(1)}, f32[768]{0:T(1024)}, u32[]{:S(2)}) copy-start(f32[768]{0:T(1024)} %get-tuple-element.77) | copy-start | bytes 9220
  212.7 12.7 %copy-start.11 = (f32[384]{0:T(512)S(1)}, f32[384]{0:T(512)}, u32[]{:S(2)}) copy-start(f32[384]{0:T(512)} %get-tuple-element.79) | copy-start | bytes 4612
  212.7 13.3 %copy-start.10 = (f32[384]{0:T(512)S(1)}, f32[384]{0:T(512)}, u32[]{:S(2)}) copy-start(f32[384]{0:T(512)} %get-tuple-element.80) | copy-start | bytes 4612

commit v4 on v3

v4 whole, which is shorter than its diff:
```python
import functools

import jax
import jax.numpy as jnp
from jax import lax
from jax.experimental import pallas as pl
from jax.experimental.pallas import tpu as pltpu
from jax.sharding import PartitionSpec as P

DILATION_SIZE = 11
EPSILON = 0.001
EDGE = 16
MESH = pl.DeviceIdType.MESH
F32 = jnp.float32
BF16 = jnp.bfloat16
SCALE = 0.7978845608028654
CUBIC = 0.044715
TN = (((0,), (0,)), ((), ()))
NT = (((1,), (1,)), ((), ()))


def gelu(u):
    return 0.5 * u * (1.0 + jnp.tanh(SCALE * u * (1.0 + CUBIC * (u * u))))


def gelu_slope(u):
    square = u * u
    t = jnp.tanh(SCALE * u * (1.0 + CUBIC * square))
    return 0.5 * (1.0 + t) + (0.5 * SCALE) * u * (1.0 - t * t) * (1.0 + (3.0 * CUBIC) * square)


def chunks(count, body, carry=0, unroll=2):
    def step(i, carry):
        return body(pl.multiple_of(i * EDGE, EDGE), carry)

    return lax.fori_loop(0, count // EDGE, step, carry, unroll=unroll)


def eight(row):
    return jnp.broadcast_to(row, (8, row.shape[-1]))


def halves(block):
    return block.reshape(block.shape[0] // 8, 8, block.shape[1])


def flat(block):
    return block.reshape(block.shape[0] * 8, block.shape[2])


def row_sum(block):
    return jnp.sum(block, axis=0, keepdims=True)


class Place:
    def __init__(self, nd, nq):
        self.nd, self.nq = nd, nq
        self.s, self.d, self.q = (lax.axis_index(a) for a in ("section", "dp", "seq"))
        self.mirror = nq - 1 - self.q
        self.next = lax.rem(self.q + 1, nq)
        self.prev = lax.rem(self.q + nq - 1, nq)
        self.partner = (1 - self.s, self.d, self.q)

    def plane(self):
        return [(self.s, lax.rem(self.d + i, self.nd), self.q) for i in range(1, self.nd)]

    def line(self):
        return [(self.s, self.d, lax.rem(self.q + i, self.nq)) for i in range(1, self.nq)]

    def greet(self, devices):
        barrier = pltpu.get_barrier_semaphore()
        for device in devices:
            pl.semaphore_signal(barrier, inc=1, device_id=device, device_id_type=MESH)
        pl.semaphore_wait(barrier, len(devices))


def remote(src, dst, send_sem, recv_sem, device):
    return pltpu.make_async_remote_copy(
        src_ref=src,
        dst_ref=dst,
        send_sem=send_sem,
        recv_sem=recv_sem,
        device_id=device,
        device_id_type=MESH,
    )


class Exchange:
    def __init__(self, place, number, sems, plane_buf, line_buf, send_sem, recv_sem):
        self.place = place
        self.plane_buf, self.line_buf = plane_buf.at[number], line_buf.at[number]
        self.send_sem, self.recv_sem = send_sem.at[sems], recv_sem.at[sems]

    def _start(self, buf, slot, rows, devices, base):
        for at, row in enumerate(rows):
            buf[slot, at : at + 1, 0 : row.shape[1]] = row
        self.copies = [
            remote(
                buf.at[slot],
                buf.at[slot],
                self.send_sem.at[base + i],
                self.recv_sem.at[base + i],
                device,
            )
            for i, device in enumerate(devices)
        ]
        for copy in self.copies:
            copy.start()

    def _finish(self, buf, count, n_rows, width):
        for copy in self.copies:
            copy.wait()
        return [[buf[j, at : at + 1, 0:width] for at in range(n_rows)] for j in range(count)]

    def start(self, rows):
        self.n_rows, self.width = len(rows), rows[0].shape[1]
        self._start(self.plane_buf, self.place.d, rows, self.place.plane(), 0)

    def relay(self, join):
        parts = self._finish(self.plane_buf, self.place.nd, self.n_rows, self.width)
        self._start(
            self.line_buf, self.place.q, join(parts), self.place.line(), self.place.nd - 1
        )

    def finish(self, join):
        return join(self._finish(self.line_buf, self.place.nq, self.n_rows, self.width))


def join_sums(parts):
    totals = parts[0]
    for part in parts[1:]:
        totals = [total + row for total, row in zip(totals, part)]
    return totals


def join_moments(count):
    def join(parts):
        n = len(parts[0]) // 2
        totals = join_sums(parts)
        means = [total * (1.0 / len(parts)) for total in totals[:n]]
        squares = totals[n:]
        for part in parts:
            squares = [
                square + count * (row - mean) * (row - mean)
                for square, row, mean in zip(squares, part[:n], means)
            ]
        return means + squares

    return join


class Norm:
    def __init__(self, mean, inv, gain, bias):
        self.mean, self.inv = eight(mean), eight(inv)
        self.gain, self.bias = (
            eight(vector[...].reshape(1, vector.shape[0])) for vector in (gain, bias)
        )

    def normed(self, block):
        return (block - self.mean[None]) * self.inv[None]

    def pre(self, normed):
        return normed * self.gain[None] + self.bias[None]


def chain_kernel(
    dims,
    inputs,
    out_grad,
    shifts,
    flips,
    gain1,
    bias1,
    weight1,
    gain2,
    bias2,
    weight2,
    gain3,
    bias3,
    weight3,
    taps_out,
    grad_out,
    result_out,
    summed_out,
    back_out,
    gain1_out,
    bias1_out,
    gain2_out,
    bias2_out,
    gain3_out,
    bias3_out,
    window,
    placed,
    act,
    taps,
    w1,
    w2,
    w3,
    even,
    odd,
    share,
    pooled,
    edges,
    edges_in,
    second,
    narrow,
    own_grad,
    far_grad,
    third_in,
    third,
    narrow_grad,
    narrow_taps,
    second_grad,
    block_grad,
    block_send,
    inbox,
    relayed,
    summed,
    wide_grad,
    ours,
    act_grad,
    placed_back,
    final,
    sums,
    plane_buf,
    line_buf,
    local_sem,
    load_sem,
    exchange_send,
    exchange_recv,
    halo_send,
    halo_recv,
    far_send,
    far_recv,
    core_send,
    core_recv,
    *cube_sems,
):
    C, H, L, B, nd, nq = dims
    half = L // 2
    width = C // 2
    tall = half + EDGE
    long = half + 2 * EDGE
    place = Place(nd, nq)
    s, q = place.s, place.q
    blocks = inbox.shape[0]
    cube = Cube(place, blocks, s * blocks, (block_grad, inbox, relayed, summed, summed_out) + cube_sems)
    for i in range(blocks):
        cube.sources[i] = block_send.at[(1 - s) * blocks + i]
    place.greet(place.plane() + place.line() + [place.partner])
    flip = [flips[s * B + b] for b in range(B)]
    shift = [shifts[s * B + b] for b in range(B)]
    block_at = [flip[b] * (nq - 1 - q) + (1 - flip[b]) * q for b in range(B)]

    load = [
        pltpu.make_async_copy(
            inputs.at[s * B + b], window.at[b, EDGE : EDGE + L], load_sem.at[b]
        )
        for b in range(B)
    ]
    load_w1 = pltpu.make_async_copy(weight1, w1, local_sem.at[0])
    load_w2 = pltpu.make_async_copy(weight2, w2, local_sem.at[1])
    load_w3 = pltpu.make_async_copy(weight3, w3, local_sem.at[2])
    load_grad = pltpu.make_async_copy(out_grad.at[pl.ds(s * B, B)], own_grad, local_sem.at[3])

    def pair(number, b, to_next, to_prev, from_prev, from_next):
        return [
            remote(
                to_next,
                from_prev,
                halo_send.at[number, b, 0],
                halo_recv.at[number, b, 0],
                (s, place.d, place.next),
            ),
            remote(
                to_prev,
                from_next,
                halo_send.at[number, b, 1],
                halo_recv.at[number, b, 1],
                (s, place.d, place.prev),
            ),
        ]

    rings = [
        pair(
            4,
            b,
            inputs.at[s * B + b, L - EDGE : L],
            inputs.at[s * B + b, 0:EDGE],
            window.at[b, 0:EDGE],
            window.at[b, EDGE + L : 2 * EDGE + L],
        )
        for b in range(B)
    ]
    for b in range(B):
        load[b].start()
        for copy in rings[b]:
            copy.start()
    for copy in (load_w1, load_w2, load_w3, load_grad):
        copy.start()

    quarter = half // 4
    mirrored = [
        [
            remote(
                out_grad.at[s * B + b, i * quarter : (i + 1) * quarter],
                far_grad.at[b, i * quarter : (i + 1) * quarter],
                far_send.at[b, i],
                far_recv.at[b, i],
                (s, place.d, place.mirror),
            )
            for i in range(4)
        ]
        for b in range(B)
    ]
    letters = [copy for copies in mirrored for copy in copies]

    def post(count):
        for copy in letters[:count]:
            copy.start()
        del letters[:count]

    def send_edges(number, b, first, last, size, wrap=False):
        turned = flip[b] == 1
        for at, (head, tail) in enumerate(zip(first, last)):
            head, tail = head.astype(F32), tail.astype(F32)
            edges[number, 0, b, at, :, 0:size] = jnp.where(turned, head, tail).astype(BF16)
            edges[number, 1, b, at, :, 0:size] = jnp.where(turned, tail, head).astype(BF16)
        n = len(first)
        copies = pair(
            number,
            b,
            edges.at[number, 0, b, 0:n, :, 0:size],
            edges.at[number, 1, b, 0:n, :, 0:size],
            edges_in.at[number, 0, b, 0:n, :, 0:size],
            edges_in.at[number, 1, b, 0:n, :, 0:size],
        )
        for copy in copies:
            copy.start()
        return copies

    def take_edges(number, b, at, size, wrap=False):
        from_prev = edges_in[number, 0, b, at, :, 0:size].astype(F32)
        from_next = edges_in[number, 1, b, at, :, 0:size].astype(F32)
        turned = flip[b] == 1
        before = jnp.where(turned, from_next, from_prev)
        after = jnp.where(turned, from_prev, from_next)
        if not wrap:
            before = jnp.where(block_at[b] > 0, before, 0.0)
            after = jnp.where(block_at[b] < nq - 1, after, 0.0)
        return before.astype(BF16), after.astype(BF16)

    def moments(read, count, size):
        none = jnp.zeros((8, size), F32)
        total = chunks(count, lambda r, t: t + jnp.sum(halves(read(r)), axis=0), none, 2)
        mean = row_sum(total) * (1.0 / count)
        mean8 = eight(mean)

        def deviations(r, t):
            away = halves(read(r)) - mean8[None]
            return t + jnp.sum(away * away, axis=0)

        return [mean, row_sum(chunks(count, deviations, none, 2))]

    def norm_of(step, count, gain, bias):
        mean, square = step.finish(join_moments(float(count * nd)))
        return Norm(mean, lax.rsqrt(square * (1.0 / (count * nd * nq)) + EPSILON), gain, bias)

    def gradients(norm, back, count):
        scale = 1.0 / (count * nd * nq)
        bias_mean, gain_mean = eight(back[0] * scale), eight(back[1] * scale)
        factor = norm.gain * norm.inv

        def value(grad, normed):
            return factor[None] * (grad - bias_mean[None] - normed * gain_mean[None])

        return value

    def tally(row, b, back):
        for at, total in ((row, back[1]), (row + 1, back[0])):
            to = sums.at[0, at : at + 1, 0 : total.shape[1]]
            if b == 0:
                to[...] = total
            else:
                to[...] = to[...] + total

    def gather(b, first, value):
        at = slice(first // BLOCK, (first + value.shape[0]) // BLOCK)
        value = value.reshape(value.shape[0] // BLOCK, BLOCK, width)
        if b > 0:
            value = value + block_grad[at]
        block_grad[at] = value
        if b == B - 1:
            block_send[at] = value.astype(BF16)

    saved = []

    def save(src, dst, sem):
        copy = pltpu.make_async_copy(src, dst, sem)
        copy.start()
        saved.append(copy)
        return copy

    zero = jnp.zeros((8, C), F32)
    none = jnp.zeros((8, H), F32)
    tap_saves = [None] * B
    swap = remote(sums.at[0], sums.at[1], core_send.at[B], core_recv.at[B], place.partner)
    last = []

    def chain(b):
        low, high = b * half, (b + 1) * half
        turned = flip[b] == 1

        def exchange(number):
            return Exchange(
                place,
                b * 6 + number,
                b * 2 + number % 2,
                plane_buf,
                line_buf,
                exchange_send,
                exchange_recv,
            )

        load[b].wait()
        step = exchange(0)
        step.start(moments(lambda r: window[b, pl.ds(EDGE + r, EDGE)].astype(F32), L, C))
        yield
        for copy in rings[b]:
            copy.wait()
        for parity in range(2):
            shape = (tall, L + 2 * EDGE)
            at = 2 * (lax.broadcasted_iota(jnp.int32, shape, 0) - 8) + parity
            source = flip[b] * (L - 1) + (1 - 2 * flip[b]) * at - shift[b] + EDGE
            pick = jnp.where(lax.broadcasted_iota(jnp.int32, shape, 1) == source, 1.0, 0.0)
            placed[b, parity] = jnp.dot(
                pick.astype(BF16), window[b, 0 : L + 2 * EDGE], preferred_element_type=F32
            ).astype(BF16)
        step.relay(join_moments(float(L)))
        post(2)
        yield
        norm1 = norm_of(step, L, gain1, bias1)
        for parity in range(2):

            def activate(r, c):
                block = halves(placed[b, parity, pl.ds(r, EDGE)].astype(F32))
                value = flat(gelu(norm1.pre(norm1.normed(block))))
                at = lax.broadcasted_iota(jnp.int32, value.shape, 0) + (r - 8)
                at = 2 * at + (parity + block_at[b] * L)
                act[pl.ds(r, EDGE)] = jnp.where((at >= 0) & (at < nq * L), value, 0.0)
                return c

            chunks(tall, activate)

            def spread(r, c):
                values = act[pl.ds(r, 2 * EDGE)]
                for off in range(3):
                    at = (2 * off + parity) * C
                    taps[pl.ds(low + r, EDGE), at : at + C] = values[
                        7 + off : 7 + off + EDGE
                    ].astype(BF16)
                return c

            chunks(half, spread)
        tap_saves[b] = save(taps.at[low:high], taps_out.at[low:high], load_sem.at[B + b])
        yield
        if b == 0:
            load_w1.wait()
        tile = even.shape[1]

        def convolve(j, c):
            cols = pl.ds(pl.multiple_of(j * tile, tile), tile)
            even[...] = jnp.dot(
                taps[low:high, 0 : 5 * C], w1[:, cols], preferred_element_type=F32
            )
            odd[...] = jnp.dot(
                taps[low:high, C : 6 * C], w1[:, cols], preferred_element_type=F32
            )

            def pool(r, c):
                at = pl.ds(r, EDGE)
                left, right = even[at, :], odd[at, :]
                away = left - right
                small = jnp.exp(-jnp.abs(away))
                pooled[b, pl.ds(EDGE + r, EDGE), cols] = (
                    jnp.maximum(left, right) + jnp.log(1.0 + small)
                ).astype(BF16)
                part = 1.0 / (1.0 + small)
                share[pl.ds(low + r, EDGE), cols] = jnp.where(away >= 0, part, small * part)
                return c

            chunks(half, pool, 0, 2)
            return c

        lax.fori_loop(0, C // tile, convolve, 0)
        step = exchange(1)
        step.start(moments(lambda r: pooled[b, pl.ds(EDGE + r, EDGE)].astype(F32), half, C))
        ring = send_edges(
            0, b, [pooled[b, EDGE : 2 * EDGE]], [pooled[b, half : half + EDGE]], C
        )
        yield
        step.relay(join_moments(float(half)))
        post(2)
        yield
        norm2 = norm_of(step, half, gain2, bias2)
        for copy in ring:
            copy.wait()
        pooled[b, 0:EDGE], pooled[b, EDGE + half : long] = take_edges(0, b, 0, C)

        def activate(r, c):
            block = halves(pooled[b, pl.ds(r, EDGE)].astype(F32))
            value = flat(gelu(norm2.pre(norm2.normed(block))))
            at = lax.broadcasted_iota(jnp.int32, value.shape, 0) + (r - EDGE + block_at[b] * half)
            act[pl.ds(r, EDGE)] = jnp.where((at >= 0) & (at < nq * half), value, 0.0)
            return c

        chunks(long, activate)

        def spread(r, c):
            values = act[pl.ds(r, 3 * EDGE)]
            for k in range(3):
                at = EDGE + (k - 1) * DILATION_SIZE
                second[pl.ds(low + r, EDGE), k * C : (k + 1) * C] = values[
                    at : at + EDGE
                ].astype(BF16)
            return c

        chunks(half, spread)
        if b == 0:
            load_w2.wait()
        narrow[low:high] = jnp.dot(second[low:high], w2[...], preferred_element_type=F32)
        step = exchange(2)
        step.start(moments(lambda r: narrow[pl.ds(low + r, EDGE)], half, H))
        yield
        step.relay(join_moments(float(half)))
        if b == 0:
            load_w3.wait()
            load_grad.wait()
        for copy in mirrored[b]:
            copy.wait()

        def choose(r, c):
            at = pl.ds(r, EDGE)
            own_grad[b, at] = jnp.where(
                turned, far_grad[b, at].astype(F32), own_grad[b, at].astype(F32)
            ).astype(BF16)
            return c

        chunks(half, choose)
        third_in[low:high] = lax.dot_general(
            own_grad[b], w3[...], NT, preferred_element_type=F32
        )
        yield
        norm3 = norm_of(step, half, gain3, bias3)

        def activate(r, carry):
            at = pl.ds(low + r, EDGE)
            normed = norm3.normed(halves(narrow[at]))
            pre = norm3.pre(normed)
            third[at] = flat(gelu(pre)).astype(BF16)
            grad = halves(third_in[at]) * gelu_slope(pre)
            third_in[at] = flat(grad)
            return carry[0] + jnp.sum(grad, axis=0), carry[1] + jnp.sum(grad * normed, axis=0)

        step = exchange(3)
        step.start([row_sum(t) for t in chunks(half, activate, (none, none))])
        for side in range(2):
            cols = slice(side * width, (side + 1) * width)
            ours[side, b] = (
                pooled[b, EDGE : EDGE + half, cols].astype(F32)
                + jnp.dot(third[low:high], w3[:, cols], preferred_element_type=F32)
            ).astype(BF16)
        if b == B - 1:
            save(ours, result_out, local_sem.at[4])
        yield
        step.relay(join_sums)
        value = lax.dot_general(third[low:high], own_grad[b], TN, preferred_element_type=F32)
        gather(b, 3 * C, jnp.concatenate([value[:, 0:width], value[:, width:]], axis=0))
        yield
        back = step.finish(join_sums)
        tally(4, b, back)
        gradient = gradients(norm3, back, half)

        def input_grad(r, c):
            at = pl.ds(low + r, EDGE)
            value = gradient(halves(third_in[at]), norm3.normed(halves(narrow[at])))
            narrow_grad[b, pl.ds(EDGE + r, EDGE)] = flat(value).astype(BF16)
            return c

        chunks(half, input_grad)
        ring = send_edges(
            1, b, [narrow_grad[b, EDGE : 2 * EDGE]], [narrow_grad[b, half : half + EDGE]], H
        )
        for k in range(3):
            gather(
                b,
                k * C,
                lax.dot_general(
                    second[low:high, k * C : (k + 1) * C],
                    narrow_grad[b, EDGE : EDGE + half],
                    TN,
                    preferred_element_type=F32,
                ),
            )
        yield
        for copy in ring:
            copy.wait()
        narrow_grad[b, 0:EDGE], narrow_grad[b, EDGE + half : long] = take_edges(1, b, 0, H)

        def spread(r, c):
            values = narrow_grad[b, pl.ds(r, 3 * EDGE)].astype(F32)
            for k in range(3):
                at = EDGE - (k - 1) * DILATION_SIZE
                narrow_taps[pl.ds(low + r, EDGE), k * H : (k + 1) * H] = values[
                    at : at + EDGE
                ].astype(BF16)
            return c

        chunks(half, spread)
        second_grad[low:high] = sum(
            lax.dot_general(
                narrow_taps[low:high, k * H : (k + 1) * H],
                w2[k * C : (k + 1) * C],
                NT,
                preferred_element_type=F32,
            )
            for k in range(3)
        )

        def slope(r, carry):
            at = pl.ds(low + r, EDGE)
            normed = norm2.normed(halves(pooled[b, pl.ds(EDGE + r, EDGE)].astype(F32)))
            grad = halves(second_grad[at]) * gelu_slope(norm2.pre(normed))
            second_grad[at] = flat(grad)
            return carry[0] + jnp.sum(grad, axis=0), carry[1] + jnp.sum(grad * normed, axis=0)

        step = exchange(4)
        step.start([row_sum(t) for t in chunks(half, slope, (zero, zero))])
        yield
        step.relay(join_sums)
        yield
        back = step.finish(join_sums)
        tally(2, b, back)
        gradient = gradients(norm2, back, half)

        def unpool(r, c):
            at = pl.ds(low + r, EDGE)
            normed = norm2.normed(halves(pooled[b, pl.ds(EDGE + r, EDGE)].astype(F32)))
            value = flat(gradient(halves(second_grad[at]), normed))
            value = value + own_grad[b, pl.ds(r, EDGE)].astype(F32)
            value = value.astype(BF16).astype(F32)
            part = share[at]
            wide_grad[0, at] = (value * part).astype(BF16)
            wide_grad[1, at] = (value * (1.0 - part)).astype(BF16)
            return c

        chunks(half, unpool)
        ring = send_edges(
            2,
            b,
            [wide_grad[p, low : low + EDGE] for p in range(2)],
            [wide_grad[p, high - EDGE : high] for p in range(2)],
            C,
        )
        if b == B - 1:
            save(wide_grad, grad_out, local_sem.at[5])
        tap_saves[b].wait()
        saved.remove(tap_saves[b])

        def put(parity, r, values):
            for at in range(3):
                lanes = (1 - parity + 2 * at) * C
                taps[pl.ds(low + r, EDGE), lanes : lanes + C] = values[
                    EDGE + 1 - at : 2 * EDGE + 1 - at
                ].astype(BF16)

        for parity in range(2):

            def spread(i, c):
                r = pl.multiple_of(i * EDGE, EDGE)
                values = wide_grad[parity, pl.ds(low + r - EDGE, 3 * EDGE)].astype(F32)
                put(parity, r, values)
                return c

            lax.fori_loop(1, half // EDGE - 1, spread, 0)
        yield
        for copy in ring:
            copy.wait()
        for parity in range(2):
            before, after = take_edges(2, b, parity, C)
            put(
                parity,
                0,
                jnp.concatenate([before, wide_grad[parity, low : low + 2 * EDGE]], axis=0).astype(F32),
            )
            put(
                parity,
                half - EDGE,
                jnp.concatenate([wide_grad[parity, high - 2 * EDGE : high], after], axis=0).astype(F32),
            )
        carry = (zero, zero)
        for parity in range(2):
            if parity == 1:
                yield

            def convolve(j, c):
                at = pl.multiple_of(j * BLOCK, BLOCK)
                part = None
                for k in range(5):
                    lanes = (k + 1 - parity) * C
                    more = lax.dot_general(
                        taps[low:high, lanes : lanes + C],
                        w1[pl.ds(k * C + at, BLOCK), :],
                        NT,
                        preferred_element_type=F32,
                    )
                    part = more if part is None else part + more
                act_grad[parity, low:high, pl.ds(at, BLOCK)] = part
                return c

            lax.fori_loop(0, C // BLOCK, convolve, 0)

            def slope(r, carry):
                at = pl.ds(low + r, EDGE)
                values = placed[b, parity, pl.ds(r, 2 * EDGE)].astype(F32)[8 : 8 + EDGE]
                normed = norm1.normed(halves(values))
                grad = halves(act_grad[parity, at]) * gelu_slope(norm1.pre(normed))
                act_grad[parity, at] = flat(grad)
                return carry[0] + jnp.sum(grad, axis=0), carry[1] + jnp.sum(grad * normed, axis=0)

            carry = chunks(half, slope, carry)
        step = exchange(5)
        step.start([row_sum(t) for t in carry])
        yield
        step.relay(join_sums)
        yield
        back = step.finish(join_sums)
        tally(0, b, back)
        if b == B - 1:
            swap.start()
        gradient = gradients(norm1, back, L)
        for parity in range(2):

            def input_grad(r, c):
                values = placed[b, parity, pl.ds(r, 2 * EDGE)].astype(F32)[8 : 8 + EDGE]
                value = gradient(
                    halves(act_grad[parity, pl.ds(low + r, EDGE)]), norm1.normed(halves(values))
                )
                window[b, pl.ds(parity * long + EDGE + r, EDGE)] = flat(value).astype(BF16)
                return c

            chunks(half, input_grad)
        starts = [parity * long for parity in range(2)]
        ring = send_edges(
            3,
            b,
            [window[b, at + EDGE : at + 2 * EDGE] for at in starts],
            [window[b, at + half : at + half + EDGE] for at in starts],
            C,
        )
        yield
        for copy in ring:
            copy.wait()
        for parity, at in enumerate(starts):
            window[b, at : at + EDGE], window[b, at + EDGE + half : at + long] = take_edges(
                3, b, parity, C, True
            )
        shape = (L, 2 * long)
        at = lax.broadcasted_iota(jnp.int32, shape, 0) + shift[b]
        at = flip[b] * (L - 1) + (1 - 2 * flip[b]) * at
        source = (at & 1) * long + (at >> 1) + EDGE
        pick = jnp.where(lax.broadcasted_iota(jnp.int32, shape, 1) == source, 1.0, 0.0)
        pick = pick.astype(BF16)
        for side in range(2):
            cols = slice(side * width, (side + 1) * width)
            placed_back[side, b] = jnp.dot(
                pick, window[b, :, cols], preferred_element_type=F32
            ).astype(BF16)
        across = remote(
            placed_back.at[1 - s, b], final.at[b], core_send.at[b], core_recv.at[b], place.partner
        )
        across.start()
        save(placed_back.at[s, b], back_out.at[s * B + b], load_sem.at[2 * B + b])
        yield
        across.wait()
        save(final.at[b], back_out.at[(1 - s) * B + b], load_sem.at[3 * B + b])

    def adding():
        for stage in range(len(cube.events())):
            for block in range(blocks):
                cube.run(block, stage)
                if block % 3 == 2:
                    yield

    run_chains(chain, adding, B)
    cube.end()
    swap.wait()
    outs = (gain1_out, bias1_out, gain2_out, bias2_out, gain3_out, bias3_out)
    for i, to in enumerate(outs):
        count = to.shape[0]
        row = sums[0, i : i + 1, 0:count] + sums[1, i : i + 1, 0:count]
        to[...] = row.reshape(count)
    for copy in saved:
        copy.wait()


GRADS_STEP = 10


def run_chains(chain, adding, count):
    chains = [chain(b) for b in range(count)]
    taken = [0] * count
    extra = None

    def advance(b):
        taken[b] += 1
        return next(chains[b], "end") != "end"

    for b in range(count):
        advance(b)
    for b in range(count):
        advance(b)
    advance(0)
    live = list(range(count))
    while live:
        for b in list(live):
            if not advance(b):
                live.remove(b)
            if extra is None and taken[-1] >= GRADS_STEP:
                extra = adding()
            if extra is not None:
                next(extra, None)
    if extra is not None:
        for _ in extra:
            pass


class Cube:
    def __init__(self, place, blocks, base, refs):
        self.place, self.blocks, self.base = place, blocks, base
        self.total, self.inbox, self.relayed, self.summed, self.out = refs[:5]
        self.send_sem, self.core_recv, self.down_recv, self.up_recv, self.share_recv = refs[5:]
        self.sources = [None] * blocks
        self.axes = cube_axes(place)
        self.planar = place.nd.bit_length() - 1
        self.flight = [None] * blocks
        self.state = [None] * blocks

    def order(self, block):
        return [self.axes[i] for i in cube_order(block, self.planar, len(self.axes))]

    def events(self):
        depth = len(self.axes)
        return ["core"] + ["down"] * depth + ["up"] * halvings(depth) + ["share", "out"]

    def _add(self, block, incoming, first, count, send):
        total, inbox = self.total, self.inbox

        step = min(count, 4 * EDGE)
        for r in range(0, count, step):
            at = pl.ds(pl.multiple_of(first + r, EDGE), step)
            value = total[self.base + block, at] + incoming(r, step).astype(F32)
            total[self.base + block, at] = value
            if send:
                inbox[block, at] = value.astype(BF16)

    def run(self, block, stage):
        place, depth = self.place, len(self.axes)
        s = place.s
        last = depth + halvings(depth)
        if self.flight[block] is not None:
            self.flight[block].wait()
        if stage == 0:
            copy = remote(
                self.sources[block],
                self.inbox.at[block],
                self.send_sem.at[block],
                self.core_recv.at[block],
                place.partner,
            )
        elif stage <= depth:
            k = stage - 1
            partner, side = self.order(block)[k]
            size, first, past = sizes(k), [0], None
            if k > 0:
                first, past = self.state[block]
            offset = first[-1]
            if k == 0:
                incoming = lambda base: lambda r, n: self.inbox[
                    block, pl.ds(pl.multiple_of(base + r, EDGE), n)
                ]
                base_of = lambda at: at
            else:
                incoming = lambda base: lambda r, n: self.relayed[
                    block, pl.ds(pl.multiple_of(base + r, EDGE), n)
                ]
                base_of = lambda at: at - offset + region(k - 1)
            if size >= 2 * EDGE:
                small = size // 2
                give, hold = offset + (1 - side) * small, offset + side * small
                self._add(block, incoming(base_of(give)), give, small, True)
            else:
                small, give, hold = size, offset, offset
                self._add(block, incoming(base_of(give)), give, small, True)
                at = pl.ds(pl.multiple_of(give, EDGE), small)
                self.total[self.base + block, at] = self.inbox[block, at].astype(F32)
            copy = remote(
                self.inbox.at[block, pl.ds(pl.multiple_of(give, EDGE), small)],
                self.relayed.at[block, region(k) : region(k) + small],
                self.send_sem.at[block],
                self.down_recv.at[block, k],
                partner,
            )
            self.state[block] = (first + [hold], past)
        elif stage <= last:
            k = last - stage
            first, _ = self.state[block]
            partner, _ = self.order(block)[k]
            hold, small = first[k + 1], sizes(k + 1)
            at = pl.ds(pl.multiple_of(hold, EDGE), small)
            if stage == depth + 1:
                end = pl.ds(pl.multiple_of(first[-1], EDGE), sizes(depth))
                begin = region(depth - 1)
                self.summed[s, block, end] = (
                    self.total[self.base + block, end]
                    + self.relayed[block, begin : begin + sizes(depth)].astype(F32)
                ).astype(BF16)
            copy = remote(
                self.summed.at[s, block, at],
                self.summed.at[s, block, at],
                self.send_sem.at[block],
                self.up_recv.at[block, k],
                partner,
            )
        elif stage == last + 1:
            copy = remote(
                self.summed.at[s, block],
                self.summed.at[s, block],
                self.send_sem.at[block],
                self.share_recv.at[block],
                place.partner,
            )
        else:
            copy = pltpu.make_async_copy(
                self.summed.at[:, block], self.out.at[:, block], self.send_sem.at[block]
            )
        if stage > 0 and stage <= depth:
            copy.start()
            if size >= 2 * EDGE:
                self._add(block, incoming(base_of(hold)), hold, small, False)
        else:
            copy.start()
        self.flight[block] = copy

    def end(self):
        for copy in self.flight:
            copy.wait()


BLOCK = 256


def sizes(k):
    return max(BLOCK >> k, EDGE)


def region(k):
    return sum(sizes(i + 1) for i in range(k))


def halvings(depth):
    return sum(sizes(k) >= 2 * EDGE for k in range(depth))


def cube_axes(place):
    axes = []
    bit = 1
    while bit < place.nd:
        side = lax.rem(place.d // bit, 2)
        axes.append(((place.s, place.d + bit * (1 - 2 * side), place.q), side))
        bit *= 2
    bit = 1
    while bit < place.nq:
        side = lax.rem(place.q // bit, 2)
        axes.append(((place.s, place.d, place.q + bit * (1 - 2 * side)), side))
        bit *= 2
    return axes


def cube_order(block, planar, depth):
    order = [(block + i) % planar for i in range(planar)] + list(range(planar, depth))
    if block % 8 == 7:
        order.remove(planar)
        order = [planar] + order
    return order


def plan(planar, depth, blocks, pieces, events):
    rate, cost = 80e3, 0.1
    free = [0.0] * (depth + 1)
    ready = {}
    now, order, done = 0.0, [], 0.0
    pieces = list(pieces)

    def send(axis, size):
        if axis == depth:
            loads, speed, wait = [(depth, 1)], 6 * rate, 0.8
        elif axis > planar:
            loads, speed, wait = [(planar, 1), (axis, 2)], rate, 3.4
        else:
            loads, speed, wait = [(axis, 1)], rate, 2.8
        begin = max([now] + [free[i] for i, _ in loads])
        for i, times in loads:
            free[i] = begin + times * size / speed
        return max(free[i] for i, _ in loads) + wait

    while pieces or ready:
        able = sorted((t, b) for b, (t, _) in ready.items() if t <= now)
        if able:
            _, block = able[0]
            _, stage = ready.pop(block)
            order.append((block, stage))
            kind = events[stage]
            now += cost if kind == "down" else 0.05
            if stage + 1 < len(events):
                axes = cube_order(block, planar, depth)
                if kind in ("core", "share"):
                    axis, size = depth, BLOCK
                elif kind == "down":
                    axis, size = axes[stage - 1], sizes(stage)
                elif kind == "up":
                    k = depth + halvings(depth) - stage
                    axis, size = axes[k], sizes(k + 1)
                else:
                    axis, size = depth, 0
                ready[block] = (send(axis, 2 * size * 768), stage + 1)
        elif pieces and done + pieces[0][4] <= now:
            name, time, made, sends, _ = pieces.pop(0)
            order.append(name)
            now += time
            done = now
            for block in made:
                ready[block] = (now, 0)
            for axis, size in sends:
                send(axis, size)
        else:
            now = min([t for t, _ in ready.values()] + [done + p[4] for p in pieces[:1]])
    return order


def sum_kernel(
    dims,
    taps_in,
    grad_in,
    result_in,
    summed_out,
    near_out,
    far_out,
    total,
    inbox,
    sending,
    relayed,
    summed,
    product,
    taps,
    grads,
    load_sem,
    result_send,
    result_recv,
    *cube_sems,
):
    C, H, L, B, nd, nq = dims
    half = L // 2
    width = C // 2
    place = Place(nd, nq)
    s = place.s
    cross = (1 - s, place.d, place.mirror)
    mine = pl.ds(s * B, B)
    per_tap = C // BLOCK
    blocks = 5 * per_tap
    cube = Cube(place, blocks, 0, (total, inbox, relayed, summed, summed_out) + cube_sems)
    depth = len(cube.axes)
    load_grads = pltpu.make_async_copy(grad_in, grads, load_sem.at[6])
    load_taps = [
        pltpu.make_async_copy(
            taps_in.at[:, i * C : (i + 1) * C], taps.at[:, i * C : (i + 1) * C], load_sem.at[i]
        )
        for i in range(6)
    ]
    for copy in [load_grads] + load_taps:
        copy.start()
    place.greet(place.plane() + place.line() + [place.partner, cross])
    for i in range(blocks):
        cube.sources[i] = sending.at[i]
    todo, pieces = {}, []

    def piece(name, time, made=(), sends=(), after=0.0):
        def keep(body):
            todo[name] = body
            pieces.append((name, time, made, sends, after))
            return body

        return keep

    across = remote(
        result_in.at[1 - s], near_out, result_send.at[0], result_recv.at[0], place.partner
    )
    away = [
        remote(
            result_in.at[side, b],
            far_out.at[s * B + b],
            result_send.at[1 + 2 * b + i],
            result_recv.at[1 + 2 * b + i],
            (side, place.d, place.mirror),
        )
        for b in range(B)
        for i, side in enumerate((s, 1 - s))
    ]
    across.start()

    def result_piece(i, after):
        @piece(("result", i), 0.05, (), [(depth - 1, 4 * half * width)], after)
        def _():
            away[i].start()

    def weight_piece(k):
        @piece(("weight", k), WEIGHT_TIME, range(k * per_tap, (k + 1) * per_tap))
        def _():
            if k == 0:
                load_grads.wait()
                load_taps[0].wait()
            load_taps[k + 1].wait()

            def tile(m, c):
                lanes = pl.multiple_of(k * C + m * BLOCK, BLOCK)
                product[...] = lax.dot_general(
                    taps[:, pl.ds(lanes, BLOCK)], grads[0], TN, preferred_element_type=F32
                ) + lax.dot_general(
                    taps[:, pl.ds(lanes + C, BLOCK)], grads[1], TN, preferred_element_type=F32
                )

                def split(r, c):
                    at = pl.ds(r, EDGE)
                    low = pl.ds(pl.multiple_of(s * width, width), width)
                    high = pl.ds(pl.multiple_of((1 - s) * width, width), width)
                    total[k * per_tap + m, at] = product[at, low]
                    sending[k * per_tap + m, at] = product[at, high].astype(BF16)
                    return c

                chunks(BLOCK, split)
                return c

            lax.fori_loop(0, per_tap, tile, 0)

    early = len(away) // 2
    for k in range(5):
        weight_piece(k)
        if k < early:
            result_piece(k, 0.0)
    for i in range(early, len(away)):
        result_piece(i, LATE if i == early else 0.0)
    for item in plan(cube.planar, depth, blocks, pieces, cube.events()):
        if item in todo:
            todo[item]()
        else:
            cube.run(*item)
    cube.end()
    across.wait()
    for copy in away:
        copy.wait()


WEIGHT_TIME = 5.0
LATE = 45.0


def finish_kernel(
    dims,
    first,
    later,
    mine,
    near,
    far,
    back,
    flips,
    *refs,
):
    vectors, outs, rest = refs[:6], refs[6:17], refs[17:]
    for src, dst in zip(vectors, outs[5:]):
        dst[...] = src[...]
    finish(dims, first, later, mine, near, far, back, flips, *outs[:5], *rest)


def finish(
    dims,
    first,
    later,
    mine,
    near,
    far,
    back,
    flips,
    conv1,
    conv2,
    conv3,
    result,
    back_out,
    held,
    wide,
    narrow,
    near_buf,
    far_buf,
    back_buf,
    in_sem,
    wide_sem,
    narrow_sem,
    side_sem,
):
    C, H, L, B, nd, nq = dims
    s = lax.axis_index("section")
    first_blocks = first.shape[1]
    blocks = first_blocks + later.shape[1]
    width = C // 2
    slots = wide.shape[0]

    def summed(block):
        return first.at[:, block] if block < first_blocks else later.at[:, block - first_blocks]

    order = list(range(first_blocks, blocks)) + list(range(first_blocks))
    loads = {
        block: pltpu.make_async_copy(summed(block), held.at[block], in_sem.at[block])
        for block in order
    }
    sides = [
        pltpu.make_async_copy(mine.at[s], near_buf.at[pl.ds(s * B, B)], side_sem.at[0]),
        pltpu.make_async_copy(near, near_buf.at[pl.ds((1 - s) * B, B)], side_sem.at[1]),
        pltpu.make_async_copy(far, far_buf, side_sem.at[2]),
        pltpu.make_async_copy(back, back_buf, side_sem.at[3]),
    ]
    for block in order[:4]:
        loads[block].start()
    for copy in sides:
        copy.start()
    for block in order[4:]:
        loads[block].start()
    bottom = 3 * C

    def targets(block, side):
        row = side * first_blocks * BLOCK + block * BLOCK
        if row < bottom:
            return [(0, BLOCK, conv2.at[row : row + BLOCK])]
        parts, at = [], 0
        while at < BLOCK:
            which, begin = (row - bottom + at) // H, (row - bottom + at) % H
            count = min(BLOCK - at, H - begin)
            cols = slice(which * width, (which + 1) * width)
            parts.append((at, count, conv3.at[begin : begin + count, cols]))
            at += count
        return parts

    going = [[] for _ in range(slots)]
    for i, block in enumerate(order):
        slot = i % slots
        for copy in going[slot]:
            copy.wait()
        loads[block].wait()
        for side in range(2):

            def widen(r, c):
                at = pl.ds(pl.multiple_of(r * 64, 64), 64)
                value = held[block, side, at].astype(F32)
                if block >= first_blocks:
                    wide[slot, at, side * width : (side + 1) * width] = value
                else:
                    narrow[slot, side, at] = value
                return c

            lax.fori_loop(0, BLOCK // 64, widen, 0)
        if block >= first_blocks:
            row = (block - first_blocks) * BLOCK
            going[slot] = [
                pltpu.make_async_copy(
                    wide.at[slot], conv1.at[row : row + BLOCK], wide_sem.at[slot]
                )
            ]
        else:
            parts = [(side, *part) for side in range(2) for part in targets(block, side)]
            going[slot] = [
                pltpu.make_async_copy(
                    narrow.at[slot, side, at : at + count], to, narrow_sem.at[slot, j]
                )
                for j, (side, at, count, to) in enumerate(parts)
            ]
        for copy in going[slot]:
            copy.start()
        if i == 2:
            sides[3].wait()
            give = pltpu.make_async_copy(back_buf, back_out, side_sem.at[3])
            give.start()
        if i == 4:
            for copy in sides[:3]:
                copy.wait()
            for b in range(2 * B):
                turned = flips[b]

                def deliver(r, c):
                    at = pl.ds(pl.multiple_of(r * 64, 64), 64)
                    near_buf[b, at] = jnp.where(
                        turned == 1, far_buf[b, at].astype(F32), near_buf[b, at].astype(F32)
                    ).astype(BF16)
                    return c

                lax.fori_loop(0, L // 128, deliver, 0)
            hand = pltpu.make_async_copy(near_buf, result, side_sem.at[0])
            hand.start()
    for copies in going:
        for copy in copies:
            copy.wait()
    give.wait()
    hand.wait()


def on_device(
    nd,
    nq,
    inputs,
    shifts,
    flips,
    gain1,
    bias1,
    weight1,
    gain2,
    bias2,
    weight2,
    gain3,
    bias3,
    weight3,
    out_grad,
):
    sequences, L, C = inputs.shape
    H = weight3.shape[0]
    B, half = sequences // 2, L // 2
    rows = B * half
    dims = (C, H, L, B, nd, nq)
    anywhere = pl.BlockSpec(memory_space=pl.ANY)
    vmem = pl.BlockSpec(memory_space=pltpu.VMEM)
    smem = pl.BlockSpec(memory_space=pltpu.SMEM)
    peers = nd - 1 + nq - 1
    shape = jax.ShapeDtypeStruct
    dma = pltpu.SemaphoreType.DMA
    width = C // 2
    side = (3 * C * H + H * C) // width // 2
    first_blocks = side // BLOCK
    later_blocks = 5 * C // BLOCK
    depth = (nd.bit_length() - 1) + (nq.bit_length() - 1)

    def cube_scratch(blocks):
        return [
            dma((blocks,)),
            dma((blocks,)),
            dma((blocks, depth)),
            dma((blocks, halvings(depth))),
            dma((blocks,)),
        ]

    taps, grads, result, first, back, *vectors = pl.pallas_call(
        functools.partial(chain_kernel, dims),
        name="chain",
        out_shape=(
            shape((rows, 6 * C), BF16),
            shape((2, rows, C), BF16),
            shape((2, B, half, width), BF16),
            shape((2, first_blocks, BLOCK, width), BF16),
            shape((2 * B, L, width), BF16),
        )
        + (shape((C,), F32),) * 4
        + (shape((H,), F32),) * 2,
        in_specs=[
            anywhere,
            anywhere,
            smem,
            smem,
            vmem,
            vmem,
            anywhere,
            vmem,
            vmem,
            anywhere,
            vmem,
            vmem,
            anywhere,
        ],
        out_specs=[anywhere] * 5 + [vmem] * 6,
        scratch_shapes=[
            pltpu.VMEM((B, L + 4 * EDGE, C), BF16),
            pltpu.VMEM((B, 2, half + EDGE, C), BF16),
            pltpu.VMEM((half + 2 * EDGE, C), F32),
            pltpu.VMEM((rows, 6 * C), BF16),
            pltpu.VMEM((5 * C, C), BF16),
            pltpu.VMEM((3 * C, H), BF16),
            pltpu.VMEM((H, C), BF16),
            pltpu.VMEM((half, C // 3), F32),
            pltpu.VMEM((half, C // 3), F32),
            pltpu.VMEM((rows, C), F32),
            pltpu.VMEM((B, half + 2 * EDGE, C), BF16),
            pltpu.VMEM((4, 2, B, 2, EDGE, C), BF16),
            pltpu.VMEM((4, 2, B, 2, EDGE, C), BF16),
            pltpu.VMEM((rows, 3 * C), BF16),
            pltpu.VMEM((rows, H), F32),
            pltpu.VMEM((B, half, C), BF16),
            pltpu.VMEM((B, half, C), BF16),
            pltpu.VMEM((rows, H), F32),
            pltpu.VMEM((rows, H), BF16),
            pltpu.VMEM((B, half + 2 * EDGE, H), BF16),
            pltpu.VMEM((rows, 3 * H), BF16),
            pltpu.VMEM((rows, C), F32),
            pltpu.VMEM((2 * first_blocks, BLOCK, width), F32),
            pltpu.VMEM((2 * first_blocks, BLOCK, width), BF16),
            pltpu.VMEM((first_blocks, BLOCK, width), BF16),
            pltpu.VMEM((first_blocks, region(depth), width), BF16),
            pltpu.VMEM((2, first_blocks, BLOCK, width), BF16),
            pltpu.VMEM((2, rows, C), BF16),
            pltpu.VMEM((2, B, half, width), BF16),
            pltpu.VMEM((2, rows, C), F32),
            pltpu.VMEM((2, B, L, width), BF16),
            pltpu.VMEM((B, L, width), BF16),
            pltpu.VMEM((2, 8, C), F32),
            pltpu.VMEM((6 * B, nd, 2, C), F32),
            pltpu.VMEM((6 * B, nq, 2, C), F32),
            dma((6,)),
            dma((4 * B,)),
            dma((2 * B, peers)),
            dma((2 * B, peers)),
            dma((5, B, 2)),
            dma((5, B, 2)),
            dma((B, 4)),
            dma((B, 4)),
            dma((B + 1,)),
            dma((B + 1,)),
        ]
        + cube_scratch(first_blocks),
        compiler_params=pltpu.CompilerParams(
            collective_id=0, has_side_effects=True, vmem_limit_bytes=60 * 2**20
        ),
    )(
        inputs,
        out_grad,
        shifts,
        flips,
        gain1,
        bias1,
        weight1.reshape(5 * C, C),
        gain2,
        bias2,
        weight2.reshape(3 * C, H),
        gain3,
        bias3,
        weight3,
    )
    later, near, far = pl.pallas_call(
        functools.partial(sum_kernel, dims),
        name="weight_sum",
        out_shape=(
            shape((2, later_blocks, BLOCK, width), BF16),
            shape((B, half, width), BF16),
            shape((2 * B, half, width), BF16),
        ),
        in_specs=[anywhere] * 3,
        out_specs=[anywhere] * 3,
        scratch_shapes=[
            pltpu.VMEM((later_blocks, BLOCK, width), F32),
            pltpu.VMEM((later_blocks, BLOCK, width), BF16),
            pltpu.VMEM((later_blocks, BLOCK, width), BF16),
            pltpu.VMEM((later_blocks, region(depth), width), BF16),
            pltpu.VMEM((2, later_blocks, BLOCK, width), BF16),
            pltpu.VMEM((BLOCK, C), F32),
            pltpu.VMEM((rows, 6 * C), BF16),
            pltpu.VMEM((2, rows, C), BF16),
            dma((7,)),
            dma((1 + 2 * B,)),
            dma((1 + 2 * B,)),
        ]
        + cube_scratch(later_blocks),
        compiler_params=pltpu.CompilerParams(
            collective_id=1, has_side_effects=True, vmem_limit_bytes=60 * 2**20
        ),
    )(taps, grads, result)
    blocks = first_blocks + later_blocks
    slots = 6
    conv1, conv2, conv3, result, back, *vectors = pl.pallas_call(
        functools.partial(finish_kernel, dims),
        name="widen",
        out_shape=(
            shape((5 * C, C), F32),
            shape((3 * C, H), F32),
            shape((H, C), F32),
            shape((2 * B, half, width), BF16),
            shape((2 * B, L, width), BF16),
        )
        + (shape((C,), F32),) * 4
        + (shape((H,), F32),) * 2,
        in_specs=[anywhere] * 6 + [smem] + [vmem] * 6,
        out_specs=[anywhere] * 5 + [vmem] * 6,
        scratch_shapes=[
            pltpu.VMEM((blocks, 2, BLOCK, width), BF16),
            pltpu.VMEM((slots, BLOCK, C), F32),
            pltpu.VMEM((slots, 2, BLOCK, width), F32),
            pltpu.VMEM((2 * B, half, width), BF16),
            pltpu.VMEM((2 * B, half, width), BF16),
            pltpu.VMEM((2 * B, L, width), BF16),
            dma((blocks,)),
            dma((slots,)),
            dma((slots, 4)),
            dma((4,)),
        ],
        compiler_params=pltpu.CompilerParams(vmem_limit_bytes=60 * 2**20),
    )(first, later, result, near, far, back, flips, *vectors)
    return (
        result,
        back,
        conv1.reshape(5, C, C),
        vectors[0],
        vectors[1],
        conv2.reshape(3, C, H),
        vectors[2],
        vectors[3],
        conv3,
        vectors[4],
        vectors[5],
    )


def solution(mesh):
    whole = P()
    split = P("dp", "seq", None)
    return jax.shard_map(
        functools.partial(on_device, mesh.shape["dp"], mesh.shape["seq"]),
        mesh=mesh,
        in_specs=(split, P("dp"), P("dp")) + (whole,) * 9 + (split,),
        out_specs=(P("dp", "seq", "section"),) * 2 + (whole,) * 9,
        check_vma=False,
    )
```

time: 230 us -> 201 us (0.87); the launches traced: 227 us -> 201 us
  Pallas kernels: 215 us -> 200 us
  local copies, waits for them, and re-layouts: 10.4 us -> 0 us
    pallas_call x3, Pallas kernels: 215 us -> 200 us  [the longest x1 112 us: on_device(): pl.pallas_call(functools.partial(chain_kernel, dims), name='chain', out_s...]
    unnamed x30 -> x0, local copies, waits for them, and re-layouts: 10.4 us -> none
where the time goes in v4:
time: 201 us
  Pallas kernels  200 us (100%)
    pallas_call x1, Pallas kernels, on_device(): pl.pallas_call(functools.partial(chain_kernel, dims), name='chain', out_s...  112 us
    pallas_call x1, Pallas kernels, on_device(): pl.pallas_call(functools.partial(sum_kernel, dims), name='weight_sum', ou...  75.8 us
    pallas_call x1, Pallas kernels, on_device(): pl.pallas_call(functools.partial(finish_kernel, dims), name='widen', out_...  12.8 us

profile of v4, /device:TPU:9, one launch (start us, length us, event | category | flops | bytes accessed | tf_op | source)
XLA Modules:
  0.0 201.0 jit_solution(13636460681742768561)
XLA Ops:
  0.6 111.6 %chain.1 = (bf16[512,4608]{1,0:T(8,128)(2,1)}, bf16[2,512,768]{2,1,0:T(8,128)(2,1)}, bf16[2,2,256,384]{3,2,1,0:T(8,128)(2,1)}, bf16[2,6,256,384]{3,2,1,0:T(8,128...) custom-call(bf16[4,512,768]{2,1,0:T(8,128)(2,1)} %inputs.1, ...), custom_call_target="tpu_custom_call" | custom-call | tf_op jit(solution)/shard_map/chain/pallas_call | solution.py:1366
  112.3 75.8 %weight_sum.1 = (bf16[2,15,256,384]{3,2,1,0:T(8,128)(2,1)}, bf16[2,256,384]{2,1,0:T(8,128)(2,1)}, bf16[4,256,384]{2,1,0:T(8,128)(2,1)}) custom-call(bf16[512,4608]{1,0:T(8,128)(2,1)} %get-tuple-element.37.taps_in, bf16[2,512,768]{2,1,0:T(8,128)(2,1)} %get-tuple-element.38.grad_in, bf16[2,2,256,384]{3,2,1,0:T(8,128)(2,1)} %get-tuple-element.39.result_in.mine), custom_call_target="tpu_custom_call" | custom-call | tf_op jit(solution)/shard_map/weight_sum/pallas_call | solution.py:1460
  188.0 12.8 %widen.1 = (f32[3840,768]{1,0:T(8,128)}, f32[2304,384]{1,0:T(8,128)}, f32[384,768]{1,0:T(8,128)}, bf16[4,256,384]{2,1,0:T(8,128)(2,1)}, bf16[4,512,384]{2,1,0:T(...) custom-call(bf16[2,6,256,384]{3,2,1,0:T(8,128)(2,1)} %get-tuple-elem, ...), custom_call_target="tpu_custom_call" | custom-call | tf_op jit(solution)/shard_map/widen/pallas_call | solution.py:1490

commit v5 on v4

--- a/solution.py
+++ b/solution.py
@@ -71,7 +71,7 @@
         barrier = pltpu.get_barrier_semaphore()
         for device in devices:
             pl.semaphore_signal(barrier, inc=1, device_id=device, device_id_type=MESH)
-        pl.semaphore_wait(barrier, len(devices))
+        return lambda: pl.semaphore_wait(barrier, len(devices))
 
 
 def remote(src, dst, send_sem, recv_sem, device):
@@ -247,7 +247,7 @@
     cube = Cube(place, blocks, s * blocks, (block_grad, inbox, relayed, summed, summed_out) + cube_sems)
     for i in range(blocks):
         cube.sources[i] = block_send.at[(1 - s) * blocks + i]
-    place.greet(place.plane() + place.line() + [place.partner])
+    place.greet(place.plane() + place.line() + [place.partner])()
     flip = [flips[s * B + b] for b in range(B)]
     shift = [shifts[s * B + b] for b in range(B)]
     block_at = [flip[b] * (nq - 1 - q) + (1 - flip[b]) * q for b in range(B)]
@@ -988,15 +988,16 @@
 
 
 def cube_order(block, planar, depth):
-    order = [(block + i) % planar for i in range(planar)] + list(range(planar, depth))
-    if block % 8 == 7:
+    kind = KINDS[block % len(KINDS)]
+    order = [(kind + i) % planar for i in range(planar)] + list(range(planar, depth))
+    if kind < 0:
         order.remove(planar)
         order = [planar] + order
     return order
 
 
 def plan(planar, depth, blocks, pieces, events):
-    rate, cost = 80e3, 0.1
+    rate, cost = 70e3, 0.15
     free = [0.0] * (depth + 1)
     ready = {}
     now, order, done = 0.0, [], 0.0
@@ -1004,11 +1005,11 @@
 
     def send(axis, size):
         if axis == depth:
-            loads, speed, wait = [(depth, 1)], 6 * rate, 0.8
+            loads, speed, wait = [(depth, 1)], 6 * rate, 1.1
         elif axis > planar:
-            loads, speed, wait = [(planar, 1), (axis, 2)], rate, 3.4
+            loads, speed, wait = [(planar, 1), (axis, 2)], rate, 3.8
         else:
-            loads, speed, wait = [(axis, 1)], rate, 2.8
+            loads, speed, wait = [(axis, 1)], rate, 3.2
         begin = max([now] + [free[i] for i, _ in loads])
         for i, times in loads:
             free[i] = begin + times * size / speed
@@ -1089,7 +1090,7 @@
     ]
     for copy in [load_grads] + load_taps:
         copy.start()
-    place.greet(place.plane() + place.line() + [place.partner, cross])
+    meet = place.greet(place.plane() + place.line() + [place.partner, cross])
     for i in range(blocks):
         cube.sources[i] = sending.at[i]
     todo, pieces = {}, []
@@ -1116,7 +1117,6 @@
         for b in range(B)
         for i, side in enumerate((s, 1 - s))
     ]
-    across.start()
 
     def result_piece(i, after):
         @piece(("result", i), 0.05, (), [(depth - 1, 4 * half * width)], after)
@@ -1151,6 +1151,9 @@
                 return c
 
             lax.fori_loop(0, per_tap, tile, 0)
+            if k == 0:
+                meet()
+                across.start()
 
     early = len(away) // 2
     for k in range(5):
@@ -1170,7 +1173,8 @@
         copy.wait()
 
 
-WEIGHT_TIME = 5.0
+WEIGHT_TIME = 4.5
+KINDS = (0, 1, 0, 1, 0, 1, 0, -1, 0, 1, 0, 0, 0, 1, 0)
 LATE = 45.0
 
 

time: 201 us -> 195 us (0.970)
  Pallas kernels: 200 us -> 194 us
    pallas_call x1, Pallas kernels: 75.8 us -> 69.8 us  [on_device(): pl.pallas_call(functools.partial(sum_kernel, dims), name='weight_sum', ou...]
where the time goes in v5:
time: 195 us
  Pallas kernels  194 us (99%)
    pallas_call x1, Pallas kernels, on_device(): pl.pallas_call(functools.partial(chain_kernel, dims), name='chain', out_s...  112 us
    pallas_call x1, Pallas kernels, on_device(): pl.pallas_call(functools.partial(sum_kernel, dims), name='weight_sum', ou...  69.8 us
    pallas_call x1, Pallas kernels, on_device(): pl.pallas_call(functools.partial(finish_kernel, dims), name='widen', out_...  12.8 us

profile of v5, /device:TPU:9, one launch (start us, length us, event | category | flops | bytes accessed | tf_op | source)
XLA Modules:
  0.0 195.0 jit_solution(1189810929441198081)
XLA Ops:
  0.6 111.6 %chain.1 = (bf16[512,4608]{1,0:T(8,128)(2,1)}, bf16[2,512,768]{2,1,0:T(8,128)(2,1)}, bf16[2,2,256,384]{3,2,1,0:T(8,128)(2,1)}, bf16[2,6,256,384]{3,2,1,0:T(8,128...) custom-call(bf16[4,512,768]{2,1,0:T(8,128)(2,1)} %inputs.1, ...), custom_call_target="tpu_custom_call" | custom-call | tf_op jit(solution)/shard_map/chain/pallas_call | solution.py:1370
  112.3 69.8 %weight_sum.1 = (bf16[2,15,256,384]{3,2,1,0:T(8,128)(2,1)}, bf16[2,256,384]{2,1,0:T(8,128)(2,1)}, bf16[4,256,384]{2,1,0:T(8,128)(2,1)}) custom-call(bf16[512,4608]{1,0:T(8,128)(2,1)} %get-tuple-element.37.taps_in, bf16[2,512,768]{2,1,0:T(8,128)(2,1)} %get-tuple-element.38.grad_in, bf16[2,2,256,384]{3,2,1,0:T(8,128)(2,1)} %get-tuple-element.39.result_in.mine), custom_call_target="tpu_custom_call" | custom-call | tf_op jit(solution)/shard_map/weight_sum/pallas_call | solution.py:1464
  182.0 12.8 %widen.1 = (f32[3840,768]{1,0:T(8,128)}, f32[2304,384]{1,0:T(8,128)}, f32[384,768]{1,0:T(8,128)}, bf16[4,256,384]{2,1,0:T(8,128)(2,1)}, bf16[4,512,384]{2,1,0:T(...) custom-call(bf16[2,6,256,384]{3,2,1,0:T(8,128)(2,1)} %get-tuple-elem, ...), custom_call_target="tpu_custom_call" | custom-call | tf_op jit(solution)/shard_map/widen/pallas_call | solution.py:1494

commit v6 on v5

--- a/solution.py
+++ b/solution.py
@@ -425,6 +425,7 @@
         load[b].wait()
         step = exchange(0)
         step.start(moments(lambda r: window[b, pl.ds(EDGE + r, EDGE)].astype(F32), L, C))
+        post(1)
         yield
         for copy in rings[b]:
             copy.wait()
@@ -500,7 +501,7 @@
         )
         yield
         step.relay(join_moments(float(half)))
-        post(2)
+        post(1)
         yield
         norm2 = norm_of(step, half, gain2, bias2)
         for copy in ring:
@@ -1279,7 +1280,7 @@
                     narrow[slot, side, at] = value
                 return c
 
-            lax.fori_loop(0, BLOCK // 64, widen, 0)
+            lax.fori_loop(0, BLOCK // 64, widen, 0, unroll=True)
         if block >= first_blocks:
             row = (block - first_blocks) * BLOCK
             going[slot] = [

time: 195 us -> 197 us (1.010)
  Pallas kernels: 194 us -> 196 us
where the time goes in v6:
time: 197 us; the launch traced here: 196 us
  Pallas kernels  196 us (99%)
    pallas_call x1, Pallas kernels, on_device(): pl.pallas_call(functools.partial(chain_kernel, dims), name='chain', out_s...  113 us
    pallas_call x1, Pallas kernels, on_device(): pl.pallas_call(functools.partial(sum_kernel, dims), name='weight_sum', ou...  69.8 us
    pallas_call x1, Pallas kernels, on_device(): pl.pallas_call(functools.partial(finish_kernel, dims), name='widen', out_...  12.8 us

profile of v6, /device:TPU:9, one launch (start us, length us, event | category | flops | bytes accessed | tf_op | source)
XLA Modules:
  0.0 196.5 jit_solution(12000324371149010431)
XLA Ops:
  0.6 113.0 %chain.1 = (bf16[512,4608]{1,0:T(8,128)(2,1)}, bf16[2,512,768]{2,1,0:T(8,128)(2,1)}, bf16[2,2,256,384]{3,2,1,0:T(8,128)(2,1)}, bf16[2,6,256,384]{3,2,1,0:T(8,128...) custom-call(bf16[4,512,768]{2,1,0:T(8,128)(2,1)} %inputs.1, ...), custom_call_target="tpu_custom_call" | custom-call | tf_op jit(solution)/shard_map/chain/pallas_call | solution.py:1371
  113.7 69.8 %weight_sum.1 = (bf16[2,15,256,384]{3,2,1,0:T(8,128)(2,1)}, bf16[2,256,384]{2,1,0:T(8,128)(2,1)}, bf16[4,256,384]{2,1,0:T(8,128)(2,1)}) custom-call(bf16[512,4608]{1,0:T(8,128)(2,1)} %get-tuple-element.37.taps_in, bf16[2,512,768]{2,1,0:T(8,128)(2,1)} %get-tuple-element.38.grad_in, bf16[2,2,256,384]{3,2,1,0:T(8,128)(2,1)} %get-tuple-element.39.result_in.mine), custom_call_target="tpu_custom_call" | custom-call | tf_op jit(solution)/shard_map/weight_sum/pallas_call | solution.py:1465
  183.5 12.8 %widen.1 = (f32[3840,768]{1,0:T(8,128)}, f32[2304,384]{1,0:T(8,128)}, f32[384,768]{1,0:T(8,128)}, bf16[4,256,384]{2,1,0:T(8,128)(2,1)}, bf16[4,512,384]{2,1,0:T(...) custom-call(bf16[2,6,256,384]{3,2,1,0:T(8,128)(2,1)} %get-tuple-elem, ...), custom_call_target="tpu_custom_call" | custom-call | tf_op jit(solution)/shard_map/widen/pallas_call | solution.py:1495
